TPU v7x, 32 devices: a whole 2x2x4 slice. The times are simulated.
32 devices in a mesh: groups: 2 (over y), expert: 16 (over z, x, core).
Axes of the slice: x: 2, y: 2, z: 4, core: 2. Of those that a mesh axis runs over, the one named last changes fastest.
Arguments:
- tokens: bfloat16 [2048, 2048], P(('groups', 'expert')), parts along dimension 0, may hold values from -6 to 6
- expert_ids: int32 [2048, 8], P(('groups', 'expert')), parts along dimension 0, may hold values from 0 to 15, as said below
- gate_units: int32 [2048, 8], P(('groups', 'expert')), parts along dimension 0, may hold values from 1 to 16
- gate_matrix: bfloat16 [16, 2048, 768], P('expert'), may hold values from -0.125 to 0.125
- up_matrix: bfloat16 [16, 2048, 768], P('expert'), may hold values from -0.125 to 0.125
- down_matrix: bfloat16 [16, 768, 2048], P('expert'), may hold values from -0.21875 to 0.21875
Outputs:
- mixed: bfloat16 [2048, 2048], P(('groups', 'expert')), parts along dimension 0
There are 2 independent parts, one for each index of `groups`. A program takes and returns all parts, laid end to end along the dimension named above; an argument that names none is the same for every part. Nothing has to cross between parts.
Inputs may be any that keep to these rules, and one draw needn't show every extreme that they name: `expert_ids`: each row names 8 different experts. The same 8 experts are named exactly 64 times by the rows of every device; for each of them the expert numbered 16 // 2 higher or lower is named by no row; every other expert is named exactly 64 // 2 times by the rows of every device.
All inputs are finite; a program needn't handle non-finite values.
Results may differ from a plain program's by a relative error of at most 0.0085.
Values may be sent and summed in bfloat16 or wider, within the bound.
No kernel may reach another device: no remote copies, remote signals or barrier semaphores. Data moves between devices by JAX's collectives and lax.ppermute only.
A program may use at most 128 MiB of HBM per device.

v0:
```python
import jax
import jax.numpy as jnp
from jax import lax
from jax.sharding import PartitionSpec as P


def swiglu_rows(rows_in, gate_w, up_w, down_w):
    gate_value = jnp.dot(rows_in, gate_w, preferred_element_type=jnp.float32)
    upward = jnp.dot(rows_in, up_w, preferred_element_type=jnp.float32)
    hidden = (jax.nn.silu(gate_value) * upward).astype(jnp.bfloat16)
    return jnp.dot(hidden, down_w, preferred_element_type=jnp.float32).astype(jnp.bfloat16)


def run_items(received, weights):
    feature_width = received.shape[-1]
    flat_rows = received.reshape(-1, feature_width)
    result = swiglu_rows(flat_rows, weights[0], weights[1], weights[2])
    return result.reshape(received.shape)


def per_device(tokens, expert_ids, gate_units, gate_matrix, up_matrix, down_matrix):
    devices = lax.axis_size("expert")
    tok_rows, top_count = expert_ids.shape
    feature_width = tokens.shape[1]
    route_rows = tok_rows * top_count
    capacity = 2 * route_rows // devices
    flat_ids = expert_ids.reshape(route_rows)
    expert_range = jnp.arange(devices, dtype=jnp.int32)
    onehot = (flat_ids[:, None] == expert_range[None, :]).astype(jnp.int32)
    earlier = jnp.cumsum(onehot, axis=0) - onehot
    position = jnp.sum(earlier * onehot, axis=1)
    routed = jnp.repeat(tokens, top_count, axis=0)
    own_weights = (gate_matrix[0], up_matrix[0], down_matrix[0])
    gate_scale = gate_units.astype(jnp.float32)
    weight = gate_scale / jnp.sum(gate_scale, axis=1, keepdims=True)
    flat_slot = flat_ids * capacity + position
    outgoing = (
        jnp.zeros((devices * capacity, feature_width), jnp.bfloat16).at[flat_slot].set(routed)
    )
    results = (lambda pieces: run_items(pieces, own_weights))(
        lax.all_to_all(
            outgoing.reshape(devices, capacity, feature_width),
            "expert",
            split_axis=0,
            concat_axis=0,
            tiled=True,
        )
    )
    back_buffer = lax.all_to_all(results, "expert", split_axis=0, concat_axis=0, tiled=True)
    returned = back_buffer.reshape(-1, feature_width)[flat_slot]
    expert_out = returned.reshape(tok_rows, top_count, feature_width).astype(jnp.float32)
    mixed = jnp.einsum("tk,tkd->td", weight, expert_out)
    return mixed.astype(jnp.bfloat16)


def solution(mesh):
    placed = (
        P(("groups", "expert"), None),
        P(("groups", "expert"), None),
        P(("groups", "expert"), None),
        P("expert", None, None),
        P("expert", None, None),
        P("expert", None, None),
    )
    return jax.shard_map(
        per_device,
        mesh=mesh,
        in_specs=placed,
        out_specs=P(("groups", "expert"), None),
        check_vma=False,
    )
```

profile of v0, /device:TPU:11, one launch (start us, length us, event | category | flops | bytes accessed | tf_op | source)
XLA Modules:
  0.0 237.7 jit_solution(7550498917499213352)
XLA Ops:
  0.0 0.0 copy-start
  0.0 0.9 copy.8
  0.9 0.1 eq.29
  1.0 0.1 eq.25
  1.1 0.7 broadcast_multiply_fusion
  1.8 1.1 reduce-window.6
  3.0 0.2 slice_reduce_fusion
  3.2 0.1 copy.7
  3.3 0.1 mul.28
  3.4 0.1 fusion.17
  3.5 6.6 %scatter_custom_fusion = bf16[1024,2048]{1,0:T(8,128)(2,1)} fusion(s32[512]{0:T(512)S(1)} %bitcast.56, bf16[]{:T(256)} %constant.4.clone.1, bf16[64,2048]{1,0:T(8,128)(2,1)} %param.6), kind=kCustom, calls=%fused_computation.11 | custom fusion | bytes 4456450 | tf_op jit(solution)/shard_map/scatter | solution.py:38
  10.1 0.0 copy-start.3
  10.1 99.1 %all_to_all.10 = bf16[16,64,2048]{2,1,0:T(8,128)(2,1)S(1)} all-to-all(bf16[16,64,2048]{2,1,0:T(8,128)(2,1)} %bitcast.52), channel_id=1, replica_groups=mesh['groups'=2,'expert'=16] {'expert'}, dimensions={0} | all-to-all | bytes 8388608 | tf_op jit(solution)/shard_map/all_to_all | solution.py:41
  109.1 0.0 copy-start.1
  109.1 2.0 copy-done.1
  111.1 0.0 copy-done.3
  111.1 5.2 %fusion.1 = f32[1024,768]{1,0:T(8,128)} fusion(bf16[1024,2048]{1,0:T(8,128)(2,1)S(1)} %bitcast.54, bf16[1,2048,768]{2,1,0:T(8,128)(2,1)S(1)} %copy-done.3), kind=kOutput, calls=%fused_computation.4 | convolution fusion | flops 3221225472 | bytes 10485760 | tf_op jit(solution)/shard_map/dot_general | solution.py:9
  116.3 0.0 copy-done
  116.3 12.3 %convolution_convert_fusion = bf16[1024,2048]{1,0:T(8,128)(2,1)} fusion(bf16[1,768,2048]{2,1,0:T(8,128)(2,1)S(1)} %copy-done, f32[1024,768]{1,0:T(8,128)} %fusion.1, bf16[1024,2048]{1,0:T(8,128)(2,1)} %bitcast.55, bf16[1,2048,768]{2,1,0:T(8,128)(2,1)} %param.9), kind=kOutput, calls=%fused_computation.2 | convolution fusion | flops 6449266688 | bytes 17825792 | tf_op jit(solution)/shard_map/dot_general | solution.py:11
  128.6 0.0 copy-start.2
  128.6 5.4 %all-to-all-start.1 = ((bf16[16,64,2048]{2,1,0:T(8,128)(2,1)}), bf16[16,64,2048]{2,1,0:T(8,128)(2,1)}, u32[]{:S(2)}, u32[]{:S(2)}) async-start(bf16[16,64,2048]{2,1,0:T(8,128)(2,1)} %bitcast.53), calls=%async_computation.1 | async-start | bytes 8388608 | tf_op jit(solution)/shard_map/all_to_all | solution.py:49
  134.1 0.0 copy-done.2
  134.1 0.1 copy.11
  134.2 92.3 %all-to-all-done.1 = bf16[16,64,2048]{2,1,0:T(8,128)(2,1)} async-done(((bf16[16,64,2048]{2,1,0:T(8,128)(2,1)}), bf16[16,64,2048]{2,1,0:T(8,128)(2,1)}, u32[]{:S(2)}, u32[]{:S(2)}) %all-to-all-start.1) | async-done | bytes 4194336 | tf_op jit(solution)/shard_map/all_to_all | solution.py:49
  226.5 8.0 %gather_fusion = bf16[512,2048]{1,0:T(8,128)(2,1)} fusion(bf16[1024,2048]{1,0:T(8,128)(2,1)} %bitcast.11, s32[1024]{0:T(1024)S(1)} %pad_clamp_fusion), kind=kCustom, calls=%fused_computation | custom fusion | bytes 4196352 | tf_op jit(solution)/shard_map/gather | solution.py:50
  234.5 2.3 fusion.7
  236.8 0.9 copy.16
  (7 shorter events, 0.1 us)
Async XLA Ops:
  0.0 116.3 %copy-start = (bf16[1,768,2048]{2,1,0:T(8,128)(2,1)S(1)}, bf16[1,768,2048]{2,1,0:T(8,128)(2,1)}, u32[]{:S(2)}) copy-start(bf16[1,768,2048]{2,1,0:T(8,128)(2,1)} %param.11) | copy-start | bytes 9437188
  10.1 101.0 %copy-start.3 = (bf16[1,2048,768]{2,1,0:T(8,128)(2,1)S(1)}, bf16[1,2048,768]{2,1,0:T(8,128)(2,1)}, u32[]{:S(2)}) copy-start(bf16[1,2048,768]{2,1,0:T(8,128)(2,1)} %param.10) | copy-start | bytes 9437188
  109.1 2.0 copy-start.1
  128.6 5.4 %copy-start.2 = (s32[64,8]{0,1:T(8,128)S(1)}, s32[64,8]{0,1:T(8,128)}, u32[]{:S(2)}) copy-start(s32[64,8]{0,1:T(8,128)} %param.8) | copy-start | bytes 6148
  128.6 97.9 %all-to-all-start.1 = ((bf16[16,64,2048]{2,1,0:T(8,128)(2,1)}), bf16[16,64,2048]{2,1,0:T(8,128)(2,1)}, u32[]{:S(2)}, u32[]{:S(2)}) async-start(bf16[16,64,2048]{2,1,0:T(8,128)(2,1)} %bitcast.53), calls=%async_computation.1 | async-start | bytes 8388608 | tf_op jit(solution)/shard_map/all_to_all | solution.py:49
where the time goes:
time: 238 us
  blocking collectives  99.1 us (42%)
  waiting for transfers between devices  92.3 us (39%)
  matrix products  19.8 us (8%)
  local copies, waits for them, and re-layouts  19 us (8%)
  starting transfers between devices  5.44 us (2%)
    all_to_all x1, blocking collectives, per_device(): lax.all_to_all(outgoing.reshape(devices, capacity, feature_width), 'exper...  99.1 us
    all_to_all x1, waiting for transfers between devices, per_device(): lax.all_to_all(results, 'expert', split_axis=0, concat_axis=0, tiled=True)  92.3 us
    dot_general x1, matrix products, swiglu_rows(): jnp.dot(hidden, down_w, preferred_element_type=jnp.float32)  12.3 us
    gather x1, local copies, waits for them, and re-layouts, per_device(): returned = back_buffer.reshape(-1, feature_width)[flat_slot]  8.02 us
    scatter x1, local copies, waits for them, and re-layouts, per_device(): jnp.zeros((devices * capacity, feature_width), jnp.bfloat16).at[flat_slot]  6.57 us
    all_to_all x1, starting transfers between devices, per_device(): lax.all_to_all(results, 'expert', split_axis=0, concat_axis=0, tiled=True)  5.44 us
    dot_general x1, matrix products, swiglu_rows(): upward = jnp.dot(rows_in, up_w, preferred_element_type=jnp.float32)  5.18 us
  transfers between devices with their start and end apart: 1, of which 1 were waited for; matrix products, arithmetic and copies ran while one was open for 0% of the time, Pallas kernels for 0%

commit v1 on v0

v1 whole, which is shorter than its diff:
```python
import functools

import jax
import jax.numpy as jnp
from jax import lax
from jax.experimental import pallas as pl
from jax.experimental.pallas import tpu as pltpu
from jax.sharding import PartitionSpec as P

LANES = 128
PLANE = 4


def swiglu_rows(rows_in, gate_w, up_w, down_w):
    gate_value = jnp.dot(rows_in, gate_w, preferred_element_type=jnp.float32)
    upward = jnp.dot(rows_in, up_w, preferred_element_type=jnp.float32)
    hidden = (jax.nn.silu(gate_value) * upward).astype(jnp.bfloat16)
    return jnp.dot(hidden, down_w, preferred_element_type=jnp.float32).astype(jnp.bfloat16)


def routed_plan(tokens, expert_ids, gate_units, gate_matrix, up_matrix, down_matrix):
    devices = lax.axis_size("expert")
    tok_rows, top_count = expert_ids.shape
    feature_width = tokens.shape[1]
    route_rows = tok_rows * top_count
    capacity = 2 * route_rows // devices
    flat_ids = expert_ids.reshape(route_rows)
    expert_range = jnp.arange(devices, dtype=jnp.int32)
    onehot = (flat_ids[:, None] == expert_range[None, :]).astype(jnp.int32)
    earlier = jnp.cumsum(onehot, axis=0) - onehot
    position = jnp.sum(earlier * onehot, axis=1)
    routed = jnp.repeat(tokens, top_count, axis=0)
    gate_scale = gate_units.astype(jnp.float32)
    weight = gate_scale / jnp.sum(gate_scale, axis=1, keepdims=True)
    flat_slot = flat_ids * capacity + position
    outgoing = (
        jnp.zeros((devices * capacity, feature_width), jnp.bfloat16).at[flat_slot].set(routed)
    )
    received = lax.all_to_all(
        outgoing.reshape(devices, capacity, feature_width),
        "expert",
        split_axis=0,
        concat_axis=0,
        tiled=True,
    )
    result = swiglu_rows(
        received.reshape(-1, feature_width), gate_matrix[0], up_matrix[0], down_matrix[0]
    )
    back_buffer = lax.all_to_all(
        result.reshape(received.shape), "expert", split_axis=0, concat_axis=0, tiled=True
    )
    returned = back_buffer.reshape(-1, feature_width)[flat_slot]
    expert_out = returned.reshape(tok_rows, top_count, feature_width).astype(jnp.float32)
    mixed = jnp.einsum("tk,tkd->td", weight, expert_out)
    return mixed.astype(jnp.bfloat16)


def expert_kernel(own_ref, *refs):
    blocks, (gate_ref, up_ref, down_ref) = refs[:PLANE], refs[PLANE : PLANE + 3]
    outs = refs[PLANE + 3 : 2 * PLANE + 3]
    rows_ref, total_ref = refs[2 * PLANE + 3 :]
    step, steps = pl.program_id(0), pl.num_programs(0)
    rows, width = outs[0].shape

    @pl.when(step == 0)
    def _():
        for spot, block in enumerate(blocks):
            rows_ref[spot * rows : (spot + 1) * rows, :] = block[:, :width]

    gate_value = jnp.dot(rows_ref[...], gate_ref[0], preferred_element_type=jnp.float32)
    upward = jnp.dot(rows_ref[...], up_ref[0], preferred_element_type=jnp.float32)
    hidden = (gate_value / (1.0 + jnp.exp(-gate_value)) * upward).astype(jnp.bfloat16)
    part = jnp.dot(hidden, down_ref[0], preferred_element_type=jnp.float32)

    @pl.when(step == 0)
    def _():
        total_ref[...] = part

    @pl.when(step > 0)
    def _():
        total_ref[...] += part

    @pl.when(step == steps - 1)
    def _():
        for spot, (block, out) in enumerate(zip(blocks, outs)):
            units = block[:, width:].astype(jnp.float32)
            lane = lax.broadcasted_iota(jnp.int32, units.shape, 1)
            own = jnp.sum(jnp.where(lane == own_ref[0], units, 0.0), axis=1, keepdims=True)
            weight = own / jnp.sum(units, axis=1, keepdims=True)
            expert_out = total_ref[spot * rows : (spot + 1) * rows, :].astype(jnp.bfloat16)
            out[...] = (weight * expert_out.astype(jnp.float32)).astype(jnp.bfloat16)


def expert_rows(own, blocks, gate_matrix, up_matrix, down_matrix):
    rows, padded = blocks[0].shape
    width, hidden_width = gate_matrix.shape[1:]
    tile = 256
    block_spec = pl.BlockSpec((rows, padded), lambda i, own: (0, 0))
    column_spec = pl.BlockSpec((1, width, tile), lambda i, own: (0, 0, i))
    return pl.pallas_call(
        expert_kernel,
        grid_spec=pltpu.PrefetchScalarGridSpec(
            num_scalar_prefetch=1,
            grid=(hidden_width // tile,),
            in_specs=[block_spec] * PLANE
            + [column_spec, column_spec, pl.BlockSpec((1, tile, width), lambda i, own: (0, i, 0))],
            out_specs=[pl.BlockSpec((rows, width), lambda i, own: (0, 0))] * PLANE,
            scratch_shapes=[
                pltpu.VMEM((PLANE * rows, width), jnp.bfloat16),
                pltpu.VMEM((PLANE * rows, width), jnp.float32),
            ],
        ),
        out_shape=[jax.ShapeDtypeStruct((rows, width), jnp.bfloat16)] * PLANE,
        compiler_params=pltpu.CompilerParams(vmem_limit_bytes=32 * 1024 * 1024),
        cost_estimate=pl.CostEstimate(
            flops=6 * PLANE * rows * width * hidden_width,
            bytes_accessed=6 * width * hidden_width + 4 * PLANE * rows * padded,
            transcendentals=PLANE * rows * hidden_width,
        ),
    )(own, *blocks, gate_matrix, up_matrix, down_matrix)


def dense_plan(tokens, expert_ids, gate_units, gate_matrix, up_matrix, down_matrix):
    devices = lax.axis_size("expert")
    planes = devices // PLANE
    everyone = range(devices)
    core_pairs = [(i, i ^ 1) for i in everyone]
    side_pairs = [(i, i ^ 2) for i in everyone]

    def core(block):
        return lax.ppermute(block, "expert", core_pairs)

    def side(block):
        return lax.ppermute(block, "expert", side_pairs)

    def turn(block, planes_on):
        pairs = [(i, (i + planes_on * PLANE) % devices) for i in everyone]
        return lax.ppermute(block, "expert", pairs)

    lane = jnp.arange(LANES, dtype=jnp.int32)
    chosen = expert_ids[:, :, None] == lane[None, None, :]
    units = jnp.sum(jnp.where(chosen, gate_units[:, :, None], 0), axis=1)
    mine = jnp.concatenate([tokens, units.astype(jnp.bfloat16)], axis=1)
    own = lax.axis_index("expert").astype(jnp.int32).reshape(1)

    order = list(range(1, planes)) + [0]
    arrived = {on: mine if on == 0 else turn(mine, on) for on in order}
    total = []
    for on in order:
        here = arrived[on]
        beside = side(here)
        parts = expert_rows(
            own, [here, beside, core(here), core(beside)], gate_matrix, up_matrix, down_matrix
        )
        parts = list(parts)
        away = core(parts[3]).astype(jnp.float32) + parts[1].astype(jnp.float32)
        away = side(away.astype(jnp.bfloat16)).astype(jnp.float32)
        near = core(parts[2]).astype(jnp.float32) + parts[0].astype(jnp.float32)
        plane_sum = (near + away).astype(jnp.bfloat16)
        total.append(plane_sum if on == 0 else turn(plane_sum, planes - on))
    mixed = functools.reduce(lambda a, b: a + b, [t.astype(jnp.float32) for t in total])
    return mixed.astype(jnp.bfloat16)


def per_device(tokens, expert_ids, gate_units, gate_matrix, up_matrix, down_matrix):
    devices = lax.axis_size("expert")
    tok_rows, top_count = expert_ids.shape
    dense = 2 * tok_rows * top_count // devices >= tok_rows
    if dense and devices % PLANE == 0 and devices <= LANES:
        plan = dense_plan
    else:
        plan = routed_plan
    return plan(tokens, expert_ids, gate_units, gate_matrix, up_matrix, down_matrix)


def solution(mesh):
    placed = (
        P(("groups", "expert"), None),
        P(("groups", "expert"), None),
        P(("groups", "expert"), None),
        P("expert", None, None),
        P("expert", None, None),
        P("expert", None, None),
    )
    return jax.shard_map(
        per_device,
        mesh=mesh,
        in_specs=placed,
        out_specs=P(("groups", "expert"), None),
        check_vma=False,
    )
```

time: 238 us -> 113 us (0.47)
  the two profiles are of different devices: /device:TPU:11 before, /device:TPU:0 now
where the time goes in v1:
time: 113 us
  waiting for transfers between devices  54.9 us (49%)
  starting transfers between devices  29.6 us (26%)
  Pallas kernels  18.5 us (16%)
  local copies, waits for them, and re-layouts  7.21 us (6%)
  other arithmetic  2.66 us (2%)
    ppermute x6, waiting for transfers between devices, turn(): return lax.ppermute(block, 'expert', pairs)  29.5 us
    ppermute x8, waiting for transfers between devices, side(): return lax.ppermute(block, 'expert', side_pairs)  24 us
    pallas_call x4, Pallas kernels, expert_rows(): pl.pallas_call(expert_kernel, grid_spec=pltpu.PrefetchScalarGridSpec(num_...  18.5 us
    ppermute x6, starting transfers between devices, turn(): return lax.ppermute(block, 'expert', pairs)  16.6 us
    ppermute x8, starting transfers between devices, side(): return lax.ppermute(block, 'expert', side_pairs)  9.73 us
    unnamed x10, local copies, waits for them, and re-layouts  7.21 us
    ppermute x16, starting transfers between devices, core(): return lax.ppermute(block, 'expert', core_pairs)  3.26 us
  transfers between devices with their start and end apart: 30, of which 9 were waited for; matrix products, arithmetic and copies ran while one was open for 0% of the time, Pallas kernels for 16%

profile of v1, /device:TPU:0, one launch (start us, length us, event | category | flops | bytes accessed | tf_op | source)
XLA Modules:
  0.0 113.1 jit_solution(8037301042323910507)
XLA Ops:
  0.0 0.8 copy.10
  0.8 0.8 copy.9
  1.5 0.2 select_reduce_fusion
  1.8 1.0 pad_maximum_fusion.refs_0_
  2.7 3.0 %collective-permute-start.24 = (bf16[64,2176]{1,0:T(8,128)(2,1)S(1)}, bf16[64,2176]{1,0:T(8,128)(2,1)S(1)}, u32[]{:S(2)}, u32[]{:S(2)}) collective-permute-start(bf16[64,2176]{1,0:T(8,128)(2,1)S(1)} %pad_maximum_fusion.refs_0_), channel_id=1, source_target_pairs={{0,2},{1,3},{2,0},{3,1},{4,6},{5,7},{6,4},{7,5},{8,10},{9,11},{10,... | collective-permute-start | bytes 835592 | tf_op jit(solution)/shard_map/ppermute | solution.py:134
  5.8 1.6 %collective-permute-start = (bf16[64,2176]{1,0:T(8,128)(2,1)S(1)}, bf16[64,2176]{1,0:T(8,128)(2,1)S(1)}, u32[]{:S(2)}, u32[]{:S(2)}) collective-permute-start(bf16[64,2176]{1,0:T(8,128)(2,1)S(1)} %pad_maximum_fusion.refs_0_), channel_id=1, source_target_pairs={{0,4},{1,5},{2,6},{3,7},{4,8},{5,9},{6,10},{7,11},{8,12},{9,13},{1... | collective-permute-start | bytes 835592 | tf_op jit(solution)/shard_map/ppermute | solution.py:138
  7.3 2.6 %collective-permute-start.8 = (bf16[64,2176]{1,0:T(8,128)(2,1)S(1)}, bf16[64,2176]{1,0:T(8,128)(2,1)S(1)}, u32[]{:S(2)}, u32[]{:S(2)}) collective-permute-start(bf16[64,2176]{1,0:T(8,128)(2,1)S(1)} %pad_maximum_fusion.refs_0_), channel_id=1, source_target_pairs={{0,8},{1,9},{2,10},{3,11},{4,12},{5,13},{6,14},{7,15},{8,0},{9,1},... | collective-permute-start | bytes 835592 | tf_op jit(solution)/shard_map/ppermute | solution.py:138
  9.9 2.5 %collective-permute-done.24.refs_1_ = bf16[64,2176]{1,0:T(8,128)(2,1)S(1)} collective-permute-done((bf16[64,2176]{1,0:T(8,128)(2,1)S(1)}, bf16[64,2176]{1,0:T(8,128)(2,1)S(1)}, u32[]{:S(2)}, u32[]{:S(2)}) %collective-permute-start.24) | collective-permute-done | bytes 278560 | tf_op jit(solution)/shard_map/ppermute | solution.py:134
  12.4 0.0 collective-permute-start.26
  12.4 3.9 %collective-permute-start.16 = (bf16[64,2176]{1,0:T(8,128)(2,1)S(1)}, bf16[64,2176]{1,0:T(8,128)(2,1)S(1)}, u32[]{:S(2)}, u32[]{:S(2)}) collective-permute-start(bf16[64,2176]{1,0:T(8,128)(2,1)S(1)} %pad_maximum_fusion.refs_0_), channel_id=1, source_target_pairs={{0,12},{1,13},{2,14},{3,15},{4,0},{5,1},{6,2},{7,3},{8,4},{9,5},{1... | collective-permute-start | bytes 835592 | tf_op jit(solution)/shard_map/ppermute | solution.py:138
  16.3 1.0 collective-permute-done.refs_0_
  17.2 0.5 collective-permute-start.1
  17.8 10.0 %collective-permute-done.8.refs_0_ = bf16[64,2176]{1,0:T(8,128)(2,1)S(1)} collective-permute-done((bf16[64,2176]{1,0:T(8,128)(2,1)S(1)}, bf16[64,2176]{1,0:T(8,128)(2,1)S(1)}, u32[]{:S(2)}, u32[]{:S(2)}) %collective-permute-start.8) | collective-permute-done | bytes 278560 | tf_op jit(solution)/shard_map/ppermute | solution.py:138
  27.8 0.5 collective-permute-start.9
  28.3 0.0 collective-permute-done.25.refs_2_
  28.3 0.0 collective-permute-done.26.refs_3_
  28.3 1.9 %copy-done = bf16[1,2048,768]{2,1,0:T(8,128)(2,1)S(1)} copy-done((bf16[1,2048,768]{2,1,0:T(8,128)(2,1)S(1)}, bf16[1,2048,768]{2,1,0:T(8,128)(2,1)}, u32[]{:S(2)}) %copy-start) | copy-done | bytes 3145752
  30.2 1.9 %copy-done.2 = bf16[1,2048,768]{2,1,0:T(8,128)(2,1)S(1)} copy-done((bf16[1,2048,768]{2,1,0:T(8,128)(2,1)S(1)}, bf16[1,2048,768]{2,1,0:T(8,128)(2,1)}, u32[]{:S(2)}) %copy-start.2) | copy-done | bytes 3145752
  32.1 1.9 %copy-done.3 = bf16[1,768,2048]{2,1,0:T(8,128)(2,1)S(1)} copy-done((bf16[1,768,2048]{2,1,0:T(8,128)(2,1)S(1)}, bf16[1,768,2048]{2,1,0:T(8,128)(2,1)}, u32[]{:S(2)}) %copy-start.3) | copy-done | bytes 3145752
  34.0 4.6 %shard_map.67 = (bf16[64,2048]{1,0:T(8,128)(2,1)S(1)}, bf16[64,2048]{1,0:T(8,128)(2,1)S(1)}, bf16[64,2048]{1,0:T(8,128)(2,1)S(1)}, bf16[64,2048]{1,0:T(8,128)(2,1)S(1)}) custom-call(s32[1]{0:T(128)} %bitcast.own_ref, bf16[64,2176]{1,0:T(8,128)(2,1)S(1)} %pad_maximum_fusion.refs_0_, bf16[64,2176]{1,0:T(8,128)(2,1)S(1)} %collective-permute-done.24.refs_1_, ...), custom_call_target="tpu_custom_call" | custom-call | flops 2415919104 | bytes 11665408 | tf_op jit(solution)/shard_map/pallas_call | solution.py:100
  38.6 0.1 collective-permute-start.28
  38.7 0.5 collective-permute-start.2
  39.2 0.1 collective-permute-start.10
  39.3 0.0 collective-permute-done.1.refs_1_
  39.3 1.5 %collective-permute-start.17 = (bf16[64,2176]{1,0:T(8,128)(2,1)S(1)}, bf16[64,2176]{1,0:T(8,128)(2,1)S(1)}, u32[]{:S(2)}, u32[]{:S(2)}) collective-permute-start(bf16[64,2176]{1,0:T(8,128)(2,1)S(1)} %collective-permute-done.16.refs_0_), channel_id=1, source_target_pairs={{0,2},{1,3},{2,0},{3,1},{4,6},{5,7},{6,4},{7,5},{8,10},{9,11},{10,... | collective-permute-start | bytes 835592 | tf_op jit(solution)/shard_map/ppermute | solution.py:134
  40.8 0.0 collective-permute-done.9.refs_1_
  40.8 0.2 collective-permute-start.3
  41.0 0.0 collective-permute-done.28
  41.0 0.3 collective-permute-start.11
  41.3 0.1 add_convert_fusion.2
  41.4 0.0 collective-permute-done.2.refs_2_
  41.4 0.2 collective-permute-start.18
  41.6 6.7 %collective-permute-done.17.refs_1_ = bf16[64,2176]{1,0:T(8,128)(2,1)S(1)} collective-permute-done((bf16[64,2176]{1,0:T(8,128)(2,1)S(1)}, bf16[64,2176]{1,0:T(8,128)(2,1)S(1)}, u32[]{:S(2)}, u32[]{:S(2)}) %collective-permute-start.17) | collective-permute-done | bytes 278560 | tf_op jit(solution)/shard_map/ppermute | solution.py:134
  48.3 0.0 collective-permute-start.27
  48.3 0.0 collective-permute-done.3.refs_3_
  48.3 0.5 collective-permute-start.19
  48.8 4.6 %shard_map.64 = (bf16[64,2048]{1,0:T(8,128)(2,1)S(1)}, bf16[64,2048]{1,0:T(8,128)(2,1)S(1)}, bf16[64,2048]{1,0:T(8,128)(2,1)S(1)}, bf16[64,2048]{1,0:T(8,128)(2,1)S(1)}) custom-call(s32[1]{0:T(128)} %bitcast.own_ref, bf16[64,2176]{1,0:T(8,128)(2,1)S(1)} %collective-permute-done.refs_0_, bf16[64,2176]{1,0:T(8,128)(2,1)S(1)} %collective-permute-done.1.refs_1_, ...), custom_call_target="tpu_custom_call" | custom-call | flops 2415919104 | bytes 11665408 | tf_op jit(solution)/shard_map/pallas_call | solution.py:100
  53.5 1.6 %collective-permute-start.29 = (bf16[64,2048]{1,0:T(8,128)(2,1)S(1)}, bf16[64,2048]{1,0:T(8,128)(2,1)S(1)}, u32[]{:S(2)}, u32[]{:S(2)}) collective-permute-start(bf16[64,2048]{1,0:T(8,128)(2,1)S(1)} %add_convert_fusion.2), channel_id=1, source_target_pairs={{0,2},{1,3},{2,0},{3,1},{4,6},{5,7},{6,4},{7,5},{8,10},{9,11},{10,... | collective-permute-start | bytes 786440 | tf_op jit(solution)/shard_map/ppermute | solution.py:134
  55.0 4.6 %shard_map.65 = (bf16[64,2048]{1,0:T(8,128)(2,1)S(1)}, bf16[64,2048]{1,0:T(8,128)(2,1)S(1)}, bf16[64,2048]{1,0:T(8,128)(2,1)S(1)}, bf16[64,2048]{1,0:T(8,128)(2,1)S(1)}) custom-call(s32[1]{0:T(128)} %bitcast.own_ref, bf16[64,2176]{1,0:T(8,128)(2,1)S(1)} %collective-permute-done.8.refs_0_, bf16[64,2176]{1,0:T(8,128)(2,1)S(1)} %collective-permute-done.9.refs_1_, ...), custom_call_target="tpu_custom_call" | custom-call | flops 2415919104 | bytes 11665408 | tf_op jit(solution)/shard_map/pallas_call | solution.py:100
  59.7 0.0 collective-permute-done.18.refs_2_
  59.7 0.6 collective-permute-start.4
  60.2 0.1 collective-permute-start.13
  60.3 4.6 %shard_map.66 = (bf16[64,2048]{1,0:T(8,128)(2,1)S(1)}, bf16[64,2048]{1,0:T(8,128)(2,1)S(1)}, bf16[64,2048]{1,0:T(8,128)(2,1)S(1)}, bf16[64,2048]{1,0:T(8,128)(2,1)S(1)}) custom-call(s32[1]{0:T(128)} %bitcast.own_ref, bf16[64,2176]{1,0:T(8,128)(2,1)S(1)} %collective-permute-done.16.refs_0_, bf16[64,2176]{1,0:T(8,128)(2,1)S(1)} %collective-permute-done.17.refs_1_, ...), custom_call_target="tpu_custom_call" | custom-call | flops 2415919104 | bytes 11665408 | tf_op jit(solution)/shard_map/pallas_call | solution.py:100
  65.0 0.5 collective-permute-start.12
  65.5 0.1 add_convert_fusion.8
  65.5 0.2 collective-permute-start.21
  65.7 0.1 add_convert_fusion.6
  65.8 1.4 %collective-permute-done.21 = bf16[64,2048]{1,0:T(8,128)(2,1)S(1)} collective-permute-done((bf16[64,2048]{1,0:T(8,128)(2,1)S(1)}, bf16[64,2048]{1,0:T(8,128)(2,1)S(1)}, u32[]{:S(2)}, u32[]{:S(2)}) %collective-permute-start.21) | collective-permute-done | bytes 262176 | tf_op jit(solution)/shard_map/ppermute | solution.py:131
  67.1 0.5 collective-permute-start.6
  67.7 0.1 add_convert_fusion.4
  67.8 0.1 collective-permute-start.20
  67.8 7.8 %collective-permute-done.6 = bf16[64,2048]{1,0:T(8,128)(2,1)S(1)} collective-permute-done((bf16[64,2048]{1,0:T(8,128)(2,1)S(1)}, bf16[64,2048]{1,0:T(8,128)(2,1)S(1)}, u32[]{:S(2)}, u32[]{:S(2)}) %collective-permute-start.6) | collective-permute-done | bytes 262176 | tf_op jit(solution)/shard_map/ppermute | solution.py:134
  75.6 0.5 collective-permute-start.14
  76.1 0.1 add_convert_fusion.7
  76.2 1.6 %collective-permute-start.22 = (bf16[64,2048]{1,0:T(8,128)(2,1)S(1)}, bf16[64,2048]{1,0:T(8,128)(2,1)S(1)}, u32[]{:S(2)}, u32[]{:S(2)}) collective-permute-start(bf16[64,2048]{1,0:T(8,128)(2,1)S(1)} %add_convert_fusion.4), channel_id=1, source_target_pairs={{0,2},{1,3},{2,0},{3,1},{4,6},{5,7},{6,4},{7,5},{8,10},{9,11},{10,... | collective-permute-start | bytes 786440 | tf_op jit(solution)/shard_map/ppermute | solution.py:134
  77.8 7.0 %collective-permute-done.14 = bf16[64,2048]{1,0:T(8,128)(2,1)S(1)} collective-permute-done((bf16[64,2048]{1,0:T(8,128)(2,1)S(1)}, bf16[64,2048]{1,0:T(8,128)(2,1)S(1)}, u32[]{:S(2)}, u32[]{:S(2)}) %collective-permute-start.14) | collective-permute-done | bytes 262176 | tf_op jit(solution)/shard_map/ppermute | solution.py:134
  84.8 7.5 %collective-permute-start.7 = (bf16[64,2048]{1,0:T(8,128)(2,1)S(1)}, bf16[64,2048]{1,0:T(8,128)(2,1)S(1)}, u32[]{:S(2)}, u32[]{:S(2)}) collective-permute-start(bf16[64,2048]{1,0:T(8,128)(2,1)S(1)} %add_convert_fusion.7), channel_id=1, source_target_pairs={{0,12},{1,13},{2,14},{3,15},{4,0},{5,1},{6,2},{7,3},{8,4},{9,5},{1... | collective-permute-start | bytes 786440 | tf_op jit(solution)/shard_map/ppermute | solution.py:138
  92.3 0.1 add_convert_fusion.5
  92.4 0.1 collective-permute-start.15
  92.5 0.1 add_convert_fusion.3
  92.6 1.0 collective-permute-start.23
  93.6 5.4 %collective-permute-done.7 = bf16[64,2048]{1,0:T(8,128)(2,1)S(1)} collective-permute-done((bf16[64,2048]{1,0:T(8,128)(2,1)S(1)}, bf16[64,2048]{1,0:T(8,128)(2,1)S(1)}, u32[]{:S(2)}, u32[]{:S(2)}) %collective-permute-start.7) | collective-permute-done | bytes 262176 | tf_op jit(solution)/shard_map/ppermute | solution.py:138
  99.1 13.1 %collective-permute-done.15 = bf16[64,2048]{1,0:T(8,128)(2,1)S(1)} collective-permute-done((bf16[64,2048]{1,0:T(8,128)(2,1)S(1)}, bf16[64,2048]{1,0:T(8,128)(2,1)S(1)}, u32[]{:S(2)}, u32[]{:S(2)}) %collective-permute-start.15) | collective-permute-done | bytes 262176 | tf_op jit(solution)/shard_map/ppermute | solution.py:138
  112.1 0.9 add_convert_fusion
  (21 shorter events, 0.1 us)
Async XLA Ops:
  2.7 9.7 %collective-permute-start.24 = (bf16[64,2176]{1,0:T(8,128)(2,1)S(1)}, bf16[64,2176]{1,0:T(8,128)(2,1)S(1)}, u32[]{:S(2)}, u32[]{:S(2)}) collective-permute-start(bf16[64,2176]{1,0:T(8,128)(2,1)S(1)} %pad_maximum_fusion.refs_0_), channel_id=1, source_target_pairs={{0,2},{1,3},{2,0},{3,1},{4,6},{5,7},{6,4},{7,5},{8,10},{9,11},{10,... | collective-permute-start | bytes 835592 | tf_op jit(solution)/shard_map/ppermute | solution.py:134
  5.8 11.5 %collective-permute-start = (bf16[64,2176]{1,0:T(8,128)(2,1)S(1)}, bf16[64,2176]{1,0:T(8,128)(2,1)S(1)}, u32[]{:S(2)}, u32[]{:S(2)}) collective-permute-start(bf16[64,2176]{1,0:T(8,128)(2,1)S(1)} %pad_maximum_fusion.refs_0_), channel_id=1, source_target_pairs={{0,4},{1,5},{2,6},{3,7},{4,8},{5,9},{6,10},{7,11},{8,12},{9,13},{1... | collective-permute-start | bytes 835592 | tf_op jit(solution)/shard_map/ppermute | solution.py:138
  7.3 20.5 %collective-permute-start.8 = (bf16[64,2176]{1,0:T(8,128)(2,1)S(1)}, bf16[64,2176]{1,0:T(8,128)(2,1)S(1)}, u32[]{:S(2)}, u32[]{:S(2)}) collective-permute-start(bf16[64,2176]{1,0:T(8,128)(2,1)S(1)} %pad_maximum_fusion.refs_0_), channel_id=1, source_target_pairs={{0,8},{1,9},{2,10},{3,11},{4,12},{5,13},{6,14},{7,15},{8,0},{9,1},... | collective-permute-start | bytes 835592 | tf_op jit(solution)/shard_map/ppermute | solution.py:138
  9.9 18.4 %collective-permute-start.25 = (bf16[64,2176]{1,0:T(8,128)(2,1)S(1)}, bf16[64,2176]{1,0:T(8,128)(2,1)S(1)}, u32[]{:S(2)}, u32[]{:S(2)}) collective-permute-start(bf16[64,2176]{1,0:T(8,128)(2,1)S(1)} %pad_maximum_fusion.refs_0_), channel_id=1, source_target_pairs={{0,1},{1,0},{2,3},{3,2},{4,5},{5,4},{6,7},{7,6},{8,9},{9,8},{10,11... | collective-permute-start | bytes 835592 | tf_op jit(solution)/shard_map/ppermute | solution.py:131
  12.4 15.9 %collective-permute-start.26 = (bf16[64,2176]{1,0:T(8,128)(2,1)S(1)}, bf16[64,2176]{1,0:T(8,128)(2,1)S(1)}, u32[]{:S(2)}, u32[]{:S(2)}) collective-permute-start(bf16[64,2176]{1,0:T(8,128)(2,1)S(1)} %collective-permute-done.24.refs_1_), channel_id=1, source_target_pairs={{0,1},{1,0},{2,3},{3,2},{4,5},{5,4},{6,7},{7,6},{8,9},{9,8},{10,11... | collective-permute-start | bytes 835592 | tf_op jit(solution)/shard_map/ppermute | solution.py:131
  12.4 26.8 %collective-permute-start.16 = (bf16[64,2176]{1,0:T(8,128)(2,1)S(1)}, bf16[64,2176]{1,0:T(8,128)(2,1)S(1)}, u32[]{:S(2)}, u32[]{:S(2)}) collective-permute-start(bf16[64,2176]{1,0:T(8,128)(2,1)S(1)} %pad_maximum_fusion.refs_0_), channel_id=1, source_target_pairs={{0,12},{1,13},{2,14},{3,15},{4,0},{5,1},{6,2},{7,3},{8,4},{9,5},{1... | collective-permute-start | bytes 835592 | tf_op jit(solution)/shard_map/ppermute | solution.py:138
  17.2 22.1 %collective-permute-start.1 = (bf16[64,2176]{1,0:T(8,128)(2,1)S(1)}, bf16[64,2176]{1,0:T(8,128)(2,1)S(1)}, u32[]{:S(2)}, u32[]{:S(2)}) collective-permute-start(bf16[64,2176]{1,0:T(8,128)(2,1)S(1)} %collective-permute-done.refs_0_), channel_id=1, source_target_pairs={{0,2},{1,3},{2,0},{3,1},{4,6},{5,7},{6,4},{7,5},{8,10},{9,11},{10,... | collective-permute-start | bytes 835592 | tf_op jit(solution)/shard_map/ppermute | solution.py:134
  27.8 13.0 %collective-permute-start.9 = (bf16[64,2176]{1,0:T(8,128)(2,1)S(1)}, bf16[64,2176]{1,0:T(8,128)(2,1)S(1)}, u32[]{:S(2)}, u32[]{:S(2)}) collective-permute-start(bf16[64,2176]{1,0:T(8,128)(2,1)S(1)} %collective-permute-done.8.refs_0_), channel_id=1, source_target_pairs={{0,2},{1,3},{2,0},{3,1},{4,6},{5,7},{6,4},{7,5},{8,10},{9,11},{10,... | collective-permute-start | bytes 835592 | tf_op jit(solution)/shard_map/ppermute | solution.py:134
  28.3 1.9 %copy-start = (bf16[1,2048,768]{2,1,0:T(8,128)(2,1)S(1)}, bf16[1,2048,768]{2,1,0:T(8,128)(2,1)}, u32[]{:S(2)}) copy-start(bf16[1,2048,768]{2,1,0:T(8,128)(2,1)} %refs_4_.7) | copy-start | bytes 9437188
  30.2 1.9 %copy-start.2 = (bf16[1,2048,768]{2,1,0:T(8,128)(2,1)S(1)}, bf16[1,2048,768]{2,1,0:T(8,128)(2,1)}, u32[]{:S(2)}) copy-start(bf16[1,2048,768]{2,1,0:T(8,128)(2,1)} %refs_5_.7) | copy-start | bytes 9437188
  32.1 1.9 %copy-start.3 = (bf16[1,768,2048]{2,1,0:T(8,128)(2,1)S(1)}, bf16[1,768,2048]{2,1,0:T(8,128)(2,1)}, u32[]{:S(2)}) copy-start(bf16[1,768,2048]{2,1,0:T(8,128)(2,1)} %refs_6_.7) | copy-start | bytes 9437188
  38.6 2.3 %collective-permute-start.28 = (bf16[64,2048]{1,0:T(8,128)(2,1)S(1)}, bf16[64,2048]{1,0:T(8,128)(2,1)S(1)}, u32[]{:S(2)}, u32[]{:S(2)}) collective-permute-start(bf16[64,2048]{1,0:T(8,128)(2,1)S(1)} %get-tuple-element.35), channel_id=1, source_target_pairs={{0,1},{1,0},{2,3},{3,2},{4,5},{5,4},{6,7},{7,6},{8,9},{9,8},{10,11... | collective-permute-start | bytes 786440 | tf_op jit(solution)/shard_map/ppermute | solution.py:131
  38.7 2.7 %collective-permute-start.2 = (bf16[64,2176]{1,0:T(8,128)(2,1)S(1)}, bf16[64,2176]{1,0:T(8,128)(2,1)S(1)}, u32[]{:S(2)}, u32[]{:S(2)}) collective-permute-start(bf16[64,2176]{1,0:T(8,128)(2,1)S(1)} %collective-permute-done.refs_0_), channel_id=1, source_target_pairs={{0,1},{1,0},{2,3},{3,2},{4,5},{5,4},{6,7},{7,6},{8,9},{9,8},{10,11... | collective-permute-start | bytes 835592 | tf_op jit(solution)/shard_map/ppermute | solution.py:131
  39.2 14.2 %collective-permute-start.10 = (bf16[64,2176]{1,0:T(8,128)(2,1)S(1)}, bf16[64,2176]{1,0:T(8,128)(2,1)S(1)}, u32[]{:S(2)}, u32[]{:S(2)}) collective-permute-start(bf16[64,2176]{1,0:T(8,128)(2,1)S(1)} %collective-permute-done.8.refs_0_), channel_id=1, source_target_pairs={{0,1},{1,0},{2,3},{3,2},{4,5},{5,4},{6,7},{7,6},{8,9},{9,8},{10,11... | collective-permute-start | bytes 835592 | tf_op jit(solution)/shard_map/ppermute | solution.py:131
  39.3 9.0 %collective-permute-start.17 = (bf16[64,2176]{1,0:T(8,128)(2,1)S(1)}, bf16[64,2176]{1,0:T(8,128)(2,1)S(1)}, u32[]{:S(2)}, u32[]{:S(2)}) collective-permute-start(bf16[64,2176]{1,0:T(8,128)(2,1)S(1)} %collective-permute-done.16.refs_0_), channel_id=1, source_target_pairs={{0,2},{1,3},{2,0},{3,1},{4,6},{5,7},{6,4},{7,5},{8,10},{9,11},{10,... | collective-permute-start | bytes 835592 | tf_op jit(solution)/shard_map/ppermute | solution.py:134
  40.8 7.5 %collective-permute-start.3 = (bf16[64,2176]{1,0:T(8,128)(2,1)S(1)}, bf16[64,2176]{1,0:T(8,128)(2,1)S(1)}, u32[]{:S(2)}, u32[]{:S(2)}) collective-permute-start(bf16[64,2176]{1,0:T(8,128)(2,1)S(1)} %collective-permute-done.1.refs_1_), channel_id=1, source_target_pairs={{0,1},{1,0},{2,3},{3,2},{4,5},{5,4},{6,7},{7,6},{8,9},{9,8},{10,11... | collective-permute-start | bytes 835592 | tf_op jit(solution)/shard_map/ppermute | solution.py:131
  41.0 14.1 %collective-permute-start.11 = (bf16[64,2176]{1,0:T(8,128)(2,1)S(1)}, bf16[64,2176]{1,0:T(8,128)(2,1)S(1)}, u32[]{:S(2)}, u32[]{:S(2)}) collective-permute-start(bf16[64,2176]{1,0:T(8,128)(2,1)S(1)} %collective-permute-done.9.refs_1_), channel_id=1, source_target_pairs={{0,1},{1,0},{2,3},{3,2},{4,5},{5,4},{6,7},{7,6},{8,9},{9,8},{10,11... | collective-permute-start | bytes 835592 | tf_op jit(solution)/shard_map/ppermute | solution.py:131
  41.4 18.3 %collective-permute-start.18 = (bf16[64,2176]{1,0:T(8,128)(2,1)S(1)}, bf16[64,2176]{1,0:T(8,128)(2,1)S(1)}, u32[]{:S(2)}, u32[]{:S(2)}) collective-permute-start(bf16[64,2176]{1,0:T(8,128)(2,1)S(1)} %collective-permute-done.16.refs_0_), channel_id=1, source_target_pairs={{0,1},{1,0},{2,3},{3,2},{4,5},{5,4},{6,7},{7,6},{8,9},{9,8},{10,11... | collective-permute-start | bytes 835592 | tf_op jit(solution)/shard_map/ppermute | solution.py:131
  48.3 45.3 %collective-permute-start.27 = (bf16[64,2048]{1,0:T(8,128)(2,1)S(1)}, bf16[64,2048]{1,0:T(8,128)(2,1)S(1)}, u32[]{:S(2)}, u32[]{:S(2)}) collective-permute-start(bf16[64,2048]{1,0:T(8,128)(2,1)S(1)} %get-tuple-element.33), channel_id=1, source_target_pairs={{0,1},{1,0},{2,3},{3,2},{4,5},{5,4},{6,7},{7,6},{8,9},{9,8},{10,11... | collective-permute-start | bytes 786440 | tf_op jit(solution)/shard_map/ppermute | solution.py:131
  48.3 11.9 %collective-permute-start.19 = (bf16[64,2176]{1,0:T(8,128)(2,1)S(1)}, bf16[64,2176]{1,0:T(8,128)(2,1)S(1)}, u32[]{:S(2)}, u32[]{:S(2)}) collective-permute-start(bf16[64,2176]{1,0:T(8,128)(2,1)S(1)} %collective-permute-done.17.refs_1_), channel_id=1, source_target_pairs={{0,1},{1,0},{2,3},{3,2},{4,5},{5,4},{6,7},{7,6},{8,9},{9,8},{10,11... | collective-permute-start | bytes 835592 | tf_op jit(solution)/shard_map/ppermute | solution.py:131
  53.5 40.2 %collective-permute-start.29 = (bf16[64,2048]{1,0:T(8,128)(2,1)S(1)}, bf16[64,2048]{1,0:T(8,128)(2,1)S(1)}, u32[]{:S(2)}, u32[]{:S(2)}) collective-permute-start(bf16[64,2048]{1,0:T(8,128)(2,1)S(1)} %add_convert_fusion.2), channel_id=1, source_target_pairs={{0,2},{1,3},{2,0},{3,1},{4,6},{5,7},{6,4},{7,5},{8,10},{9,11},{10,... | collective-permute-start | bytes 786440 | tf_op jit(solution)/shard_map/ppermute | solution.py:134
  55.0 5.3 %copy-start.1 = (bf16[1,2048,768]{2,1,0:T(8,128)(2,1)S(1)}, bf16[1,2048,768]{2,1,0:T(8,128)(2,1)}, u32[]{:S(2)}) copy-start(bf16[1,2048,768]{2,1,0:T(8,128)(2,1)} %refs_4_.7) | copy-start | bytes 9437188
  55.0 9.9 %collective-permute-start.5 = (bf16[64,2048]{1,0:T(8,128)(2,1)S(1)}, bf16[64,2048]{1,0:T(8,128)(2,1)S(1)}, u32[]{:S(2)}, u32[]{:S(2)}) collective-permute-start(bf16[64,2048]{1,0:T(8,128)(2,1)S(1)} %get-tuple-element.23), channel_id=1, source_target_pairs={{0,1},{1,0},{2,3},{3,2},{4,5},{5,4},{6,7},{7,6},{8,9},{9,8},{10,11... | collective-permute-start | bytes 786440 | tf_op jit(solution)/shard_map/ppermute | solution.py:131
  59.7 8.1 %collective-permute-start.4 = (bf16[64,2048]{1,0:T(8,128)(2,1)S(1)}, bf16[64,2048]{1,0:T(8,128)(2,1)S(1)}, u32[]{:S(2)}, u32[]{:S(2)}) collective-permute-start(bf16[64,2048]{1,0:T(8,128)(2,1)S(1)} %get-tuple-element.21), channel_id=1, source_target_pairs={{0,1},{1,0},{2,3},{3,2},{4,5},{5,4},{6,7},{7,6},{8,9},{9,8},{10,11... | collective-permute-start | bytes 786440 | tf_op jit(solution)/shard_map/ppermute | solution.py:131
  60.2 5.3 %collective-permute-start.13 = (bf16[64,2048]{1,0:T(8,128)(2,1)S(1)}, bf16[64,2048]{1,0:T(8,128)(2,1)S(1)}, u32[]{:S(2)}, u32[]{:S(2)}) collective-permute-start(bf16[64,2048]{1,0:T(8,128)(2,1)S(1)} %get-tuple-element.27), channel_id=1, source_target_pairs={{0,1},{1,0},{2,3},{3,2},{4,5},{5,4},{6,7},{7,6},{8,9},{9,8},{10,11... | collective-permute-start | bytes 786440 | tf_op jit(solution)/shard_map/ppermute | solution.py:131
  65.0 11.2 %collective-permute-start.12 = (bf16[64,2048]{1,0:T(8,128)(2,1)S(1)}, bf16[64,2048]{1,0:T(8,128)(2,1)S(1)}, u32[]{:S(2)}, u32[]{:S(2)}) collective-permute-start(bf16[64,2048]{1,0:T(8,128)(2,1)S(1)} %get-tuple-element.25), channel_id=1, source_target_pairs={{0,1},{1,0},{2,3},{3,2},{4,5},{5,4},{6,7},{7,6},{8,9},{9,8},{10,11... | collective-permute-start | bytes 786440 | tf_op jit(solution)/shard_map/ppermute | solution.py:131
  65.5 1.6 %collective-permute-start.21 = (bf16[64,2048]{1,0:T(8,128)(2,1)S(1)}, bf16[64,2048]{1,0:T(8,128)(2,1)S(1)}, u32[]{:S(2)}, u32[]{:S(2)}) collective-permute-start(bf16[64,2048]{1,0:T(8,128)(2,1)S(1)} %get-tuple-element.31), channel_id=1, source_target_pairs={{0,1},{1,0},{2,3},{3,2},{4,5},{5,4},{6,7},{7,6},{8,9},{9,8},{10,11... | collective-permute-start | bytes 786440 | tf_op jit(solution)/shard_map/ppermute | solution.py:131
  67.1 8.4 %collective-permute-start.6 = (bf16[64,2048]{1,0:T(8,128)(2,1)S(1)}, bf16[64,2048]{1,0:T(8,128)(2,1)S(1)}, u32[]{:S(2)}, u32[]{:S(2)}) collective-permute-start(bf16[64,2048]{1,0:T(8,128)(2,1)S(1)} %add_convert_fusion.8), channel_id=1, source_target_pairs={{0,2},{1,3},{2,0},{3,1},{4,6},{5,7},{6,4},{7,5},{8,10},{9,11},{10,... | collective-permute-start | bytes 786440 | tf_op jit(solution)/shard_map/ppermute | solution.py:134
  67.8 24.6 %collective-permute-start.20 = (bf16[64,2048]{1,0:T(8,128)(2,1)S(1)}, bf16[64,2048]{1,0:T(8,128)(2,1)S(1)}, u32[]{:S(2)}, u32[]{:S(2)}) collective-permute-start(bf16[64,2048]{1,0:T(8,128)(2,1)S(1)} %get-tuple-element.29), channel_id=1, source_target_pairs={{0,1},{1,0},{2,3},{3,2},{4,5},{5,4},{6,7},{7,6},{8,9},{9,8},{10,11... | collective-permute-start | bytes 786440 | tf_op jit(solution)/shard_map/ppermute | solution.py:131
  75.6 9.2 %collective-permute-start.14 = (bf16[64,2048]{1,0:T(8,128)(2,1)S(1)}, bf16[64,2048]{1,0:T(8,128)(2,1)S(1)}, u32[]{:S(2)}, u32[]{:S(2)}) collective-permute-start(bf16[64,2048]{1,0:T(8,128)(2,1)S(1)} %add_convert_fusion.6), channel_id=1, source_target_pairs={{0,2},{1,3},{2,0},{3,1},{4,6},{5,7},{6,4},{7,5},{8,10},{9,11},{10,... | collective-permute-start | bytes 786440 | tf_op jit(solution)/shard_map/ppermute | solution.py:134
  76.2 16.2 %collective-permute-start.22 = (bf16[64,2048]{1,0:T(8,128)(2,1)S(1)}, bf16[64,2048]{1,0:T(8,128)(2,1)S(1)}, u32[]{:S(2)}, u32[]{:S(2)}) collective-permute-start(bf16[64,2048]{1,0:T(8,128)(2,1)S(1)} %add_convert_fusion.4), channel_id=1, source_target_pairs={{0,2},{1,3},{2,0},{3,1},{4,6},{5,7},{6,4},{7,5},{8,10},{9,11},{10,... | collective-permute-start | bytes 786440 | tf_op jit(solution)/shard_map/ppermute | solution.py:134
  84.8 14.2 %collective-permute-start.7 = (bf16[64,2048]{1,0:T(8,128)(2,1)S(1)}, bf16[64,2048]{1,0:T(8,128)(2,1)S(1)}, u32[]{:S(2)}, u32[]{:S(2)}) collective-permute-start(bf16[64,2048]{1,0:T(8,128)(2,1)S(1)} %add_convert_fusion.7), channel_id=1, source_target_pairs={{0,12},{1,13},{2,14},{3,15},{4,0},{5,1},{6,2},{7,3},{8,4},{9,5},{1... | collective-permute-start | bytes 786440 | tf_op jit(solution)/shard_map/ppermute | solution.py:138
  92.4 19.7 %collective-permute-start.15 = (bf16[64,2048]{1,0:T(8,128)(2,1)S(1)}, bf16[64,2048]{1,0:T(8,128)(2,1)S(1)}, u32[]{:S(2)}, u32[]{:S(2)}) collective-permute-start(bf16[64,2048]{1,0:T(8,128)(2,1)S(1)} %add_convert_fusion.5), channel_id=1, source_target_pairs={{0,8},{1,9},{2,10},{3,11},{4,12},{5,13},{6,14},{7,15},{8,0},{9,1},... | collective-permute-start | bytes 786440 | tf_op jit(solution)/shard_map/ppermute | solution.py:138
  92.6 19.5 %collective-permute-start.23 = (bf16[64,2048]{1,0:T(8,128)(2,1)S(1)}, bf16[64,2048]{1,0:T(8,128)(2,1)S(1)}, u32[]{:S(2)}, u32[]{:S(2)}) collective-permute-start(bf16[64,2048]{1,0:T(8,128)(2,1)S(1)} %add_convert_fusion.3), channel_id=1, source_target_pairs={{0,4},{1,5},{2,6},{3,7},{4,8},{5,9},{6,10},{7,11},{8,12},{9,13},{1... | collective-permute-start | bytes 786440 | tf_op jit(solution)/shard_map/ppermute | solution.py:138

commit v2 on v1

v2 whole, which is shorter than its diff:
```python
import functools

import jax
import jax.numpy as jnp
from jax import lax
from jax.experimental import pallas as pl
from jax.experimental.pallas import tpu as pltpu
from jax.sharding import PartitionSpec as P

LANES = 128
PLANE = 4


def swiglu_rows(rows_in, gate_w, up_w, down_w):
    gate_value = jnp.dot(rows_in, gate_w, preferred_element_type=jnp.float32)
    upward = jnp.dot(rows_in, up_w, preferred_element_type=jnp.float32)
    hidden = (jax.nn.silu(gate_value) * upward).astype(jnp.bfloat16)
    return jnp.dot(hidden, down_w, preferred_element_type=jnp.float32).astype(jnp.bfloat16)


def routed_plan(tokens, expert_ids, gate_units, gate_matrix, up_matrix, down_matrix):
    devices = lax.axis_size("expert")
    tok_rows, top_count = expert_ids.shape
    feature_width = tokens.shape[1]
    route_rows = tok_rows * top_count
    capacity = 2 * route_rows // devices
    flat_ids = expert_ids.reshape(route_rows)
    expert_range = jnp.arange(devices, dtype=jnp.int32)
    onehot = (flat_ids[:, None] == expert_range[None, :]).astype(jnp.int32)
    earlier = jnp.cumsum(onehot, axis=0) - onehot
    position = jnp.sum(earlier * onehot, axis=1)
    routed = jnp.repeat(tokens, top_count, axis=0)
    gate_scale = gate_units.astype(jnp.float32)
    weight = gate_scale / jnp.sum(gate_scale, axis=1, keepdims=True)
    flat_slot = flat_ids * capacity + position
    outgoing = (
        jnp.zeros((devices * capacity, feature_width), jnp.bfloat16).at[flat_slot].set(routed)
    )
    received = lax.all_to_all(
        outgoing.reshape(devices, capacity, feature_width),
        "expert",
        split_axis=0,
        concat_axis=0,
        tiled=True,
    )
    result = swiglu_rows(
        received.reshape(-1, feature_width), gate_matrix[0], up_matrix[0], down_matrix[0]
    )
    back_buffer = lax.all_to_all(
        result.reshape(received.shape), "expert", split_axis=0, concat_axis=0, tiled=True
    )
    returned = back_buffer.reshape(-1, feature_width)[flat_slot]
    expert_out = returned.reshape(tok_rows, top_count, feature_width).astype(jnp.float32)
    mixed = jnp.einsum("tk,tkd->td", weight, expert_out)
    return mixed.astype(jnp.bfloat16)


def pack_kernel(tokens_hbm, ids_hbm, units_hbm, out_ref, ids_ref, units_ref, sems):
    top_count, rows = ids_ref.shape
    width = tokens_hbm.shape[1]
    copies = [
        pltpu.make_async_copy(tokens_hbm, out_ref.at[:, :width], sems.at[0]),
        pltpu.make_async_copy(ids_hbm, ids_ref, sems.at[1]),
        pltpu.make_async_copy(units_hbm, units_ref, sems.at[2]),
    ]
    for copy in copies:
        copy.start()
    copies[1].wait()
    copies[2].wait()
    expert = lax.broadcasted_iota(jnp.int32, (LANES, rows), 0)
    units = jnp.zeros((LANES, rows), jnp.int32)
    for k in range(top_count):
        units += jnp.where(expert == ids_ref[k : k + 1, :], units_ref[k : k + 1, :], 0)
    out_ref[:, width:] = units.astype(jnp.float32).T.astype(jnp.bfloat16)
    copies[0].wait()


def pack(tokens, expert_ids, gate_units):
    rows, width = tokens.shape
    routes = (expert_ids.shape[1], rows)
    return pl.pallas_call(
        pack_kernel,
        in_specs=[pl.BlockSpec(memory_space=pltpu.HBM)] * 3,
        out_specs=pl.BlockSpec(memory_space=pltpu.VMEM),
        out_shape=jax.ShapeDtypeStruct((rows, width + LANES), tokens.dtype),
        scratch_shapes=[
            pltpu.VMEM(routes, jnp.int32),
            pltpu.VMEM(routes, jnp.int32),
            pltpu.SemaphoreType.DMA((3,)),
        ],
        compiler_params=pltpu.CompilerParams(vmem_limit_bytes=60 * 1024 * 1024),
        cost_estimate=pl.CostEstimate(flops=0, bytes_accessed=4 * rows * width, transcendentals=0),
    )(tokens, expert_ids.T, gate_units.T)


def load_kernel(*refs):
    count = len(refs) // 2
    sources, (targets, sems) = refs[:count], (refs[count : 2 * count], refs[2 * count])
    copies = [
        pltpu.make_async_copy(source, target, sems.at[spot])
        for spot, (source, target) in enumerate(zip(sources, targets))
    ]
    for copy in copies:
        copy.start()
    for copy in copies:
        copy.wait()


def load(*matrices):
    return pl.pallas_call(
        load_kernel,
        in_specs=[pl.BlockSpec(memory_space=pltpu.HBM)] * len(matrices),
        out_specs=[pl.BlockSpec(memory_space=pltpu.VMEM)] * len(matrices),
        out_shape=[pltpu.VMEM(m.shape, m.dtype) for m in matrices],
        scratch_shapes=[pltpu.SemaphoreType.DMA((len(matrices),))],
        compiler_params=pltpu.CompilerParams(vmem_limit_bytes=44 * 1024 * 1024),
        cost_estimate=pl.CostEstimate(
            flops=0, bytes_accessed=sum(2 * m.size for m in matrices), transcendentals=0
        ),
    )(*matrices)


def expert_kernel(own_ref, *refs):
    blocks, (gate_ref, up_ref, down_ref) = refs[:PLANE], refs[PLANE : PLANE + 3]
    outs, total_ref = refs[PLANE + 3 : PLANE + 5], refs[PLANE + 5]
    rows, (width, hidden_width) = blocks[0].shape[0], gate_ref.shape[1:]
    tile = 256
    tokens = jnp.concatenate([block[:, :width] for block in blocks], axis=0)
    for start in range(0, hidden_width, tile):
        columns = slice(start, start + tile)
        gate_value = jnp.dot(tokens, gate_ref[0, :, columns], preferred_element_type=jnp.float32)
        upward = jnp.dot(tokens, up_ref[0, :, columns], preferred_element_type=jnp.float32)
        hidden = (gate_value / (1.0 + jnp.exp(-gate_value)) * upward).astype(jnp.bfloat16)
        part = jnp.dot(hidden, down_ref[0, columns, :], preferred_element_type=jnp.float32)
        if start == 0:
            total_ref[...] = part
        else:
            total_ref[...] += part
    for spot, block in enumerate(blocks):
        units = block[:, width:].astype(jnp.float32)
        lane = lax.broadcasted_iota(jnp.int32, units.shape, 1)
        own = jnp.sum(jnp.where(lane == own_ref[0], units, 0.0), axis=1, keepdims=True)
        weight = own / jnp.sum(units, axis=1, keepdims=True)
        expert_out = total_ref[spot * rows : (spot + 1) * rows, :].astype(jnp.bfloat16)
        half = slice(spot % 2 * rows, (spot % 2 + 1) * rows)
        outs[spot // 2][half, :] = (weight * expert_out.astype(jnp.float32)).astype(jnp.bfloat16)


def expert_rows(own, blocks, gate_matrix, up_matrix, down_matrix):
    rows, padded = blocks[0].shape
    width, hidden_width = gate_matrix.shape[1:]
    in_vmem = pl.BlockSpec(memory_space=pltpu.VMEM)
    return pl.pallas_call(
        expert_kernel,
        in_specs=[pl.BlockSpec(memory_space=pltpu.SMEM)] + [in_vmem] * (PLANE + 3),
        out_specs=[in_vmem] * 2,
        out_shape=[jax.ShapeDtypeStruct((2 * rows, width), jnp.bfloat16)] * 2,
        scratch_shapes=[pltpu.VMEM((PLANE * rows, width), jnp.float32)],
        compiler_params=pltpu.CompilerParams(vmem_limit_bytes=16 * 1024 * 1024),
        cost_estimate=pl.CostEstimate(
            flops=6 * PLANE * rows * width * hidden_width,
            bytes_accessed=4 * PLANE * rows * padded,
            transcendentals=PLANE * rows * hidden_width,
        ),
    )(own, *blocks, gate_matrix, up_matrix, down_matrix)


def dense_plan(tokens, expert_ids, gate_units, gate_matrix, up_matrix, down_matrix):
    devices = lax.axis_size("expert")
    planes = devices // PLANE
    everyone = range(devices)
    core_pairs = [(i, i ^ 1) for i in everyone]
    side_pairs = [(i, i ^ 2) for i in everyone]

    def core(block):
        return lax.ppermute(block, "expert", core_pairs)

    def side(block):
        return lax.ppermute(block, "expert", side_pairs)

    def turn(block, planes_on):
        pairs = [(i, (i + planes_on * PLANE) % devices) for i in everyone]
        return lax.ppermute(block, "expert", pairs)

    own = lax.axis_index("expert").astype(jnp.int32).reshape(1)
    mine = pack(tokens, expert_ids, gate_units)
    rows = tokens.shape[0]

    def after(block, *earlier):
        return lax.optimization_barrier((block, *earlier))[0]

    here, beside, core_here, core_beside = {0: mine}, {}, {}, {}
    keep, give, near, away, sums = {}, {}, {}, {}, {}

    def experts(on, *earlier):
        four = [beside[on], here[on], core_beside[on], core_here[on]]
        keep[on], give[on] = expert_rows(after(own, *earlier), four, *weights)
        return give[on]

    def wide(block):
        return block.astype(jnp.float32)

    def back(on, *earlier):
        got = core(after(give[on], *earlier))
        away[on] = (wide(keep[on][:rows]) + wide(got[:rows])).astype(jnp.bfloat16)
        near[on] = wide(keep[on][rows:]) + wide(got[rows:])
        return away[on]

    def across(on, *earlier):
        moved = side(after(away[on], *earlier))
        sums[on] = (near[on] + wide(moved)).astype(jnp.bfloat16)
        return sums[on]

    def home(on, *earlier):
        sums[on] = turn(after(sums[on], *earlier), planes - on)

    here[1] = turn(mine, 1)
    here[3] = turn(mine, 3)
    beside[0] = side(mine)
    core_here[0] = core(mine)
    core_beside[0] = core(beside[0])
    beside[1] = side(after(here[1], beside[0]))
    here[2] = turn(here[1], 1)
    core_here[1] = core(here[1])
    beside[3] = side(after(here[3], here[1]))
    core_here[3] = core(after(here[3], here[1]))
    core_beside[1] = core(after(beside[1], here[3]))
    beside[2] = side(after(here[2], beside[1]))
    core_here[2] = core(after(here[2], beside[1]))
    weights = load(
        *lax.optimization_barrier((gate_matrix, up_matrix, down_matrix, here[2]))[:3]
    )
    experts(1)
    back(1)
    core_beside[3] = core(beside[3])
    across(1)
    experts(3, give[1])
    back(3)
    across(3, away[1])
    core_beside[2] = core(beside[2])
    experts(2, away[3])
    back(2)
    experts(0, sums[1], give[2])
    back(0, give[2])
    home(1)
    across(2)
    home(3)
    across(0, away[2])
    home(2)
    mixed = functools.reduce(lambda a, b: a + b, [wide(sums[on]) for on in range(4)])
    return mixed.astype(jnp.bfloat16)


def per_device(tokens, expert_ids, gate_units, gate_matrix, up_matrix, down_matrix):
    devices = lax.axis_size("expert")
    tok_rows, top_count = expert_ids.shape
    dense = 2 * tok_rows * top_count // devices >= tok_rows
    if dense and devices % PLANE == 0 and devices <= LANES:
        plan = dense_plan
    else:
        plan = routed_plan
    return plan(tokens, expert_ids, gate_units, gate_matrix, up_matrix, down_matrix)


def solution(mesh):
    placed = (
        P(("groups", "expert"), None),
        P(("groups", "expert"), None),
        P(("groups", "expert"), None),
        P("expert", None, None),
        P("expert", None, None),
        P("expert", None, None),
    )
    return jax.shard_map(
        per_device,
        mesh=mesh,
        in_specs=placed,
        out_specs=P(("groups", "expert"), None),
        check_vma=False,
    )
```

time: 113 us -> 84.8 us (0.75)
  waiting for transfers between devices: 54.9 us -> 42.1 us
  local copies, waits for them, and re-layouts: 7.21 us -> 0.01 us
  starting transfers between devices: 29.6 us -> 23.5 us
  Pallas kernels: 18.5 us -> 17.3 us
  other arithmetic: 2.66 us -> 1.5 us
    ppermute x8, waiting for transfers between devices: 24 us -> 12.3 us  [side(): return lax.ppermute(block, 'expert', side_pairs)]
    unnamed x10 -> x2, local copies, waits for them, and re-layouts: 7.21 us -> 0.01 us
    ppermute x6, starting transfers between devices: 16.6 us -> 11.4 us  [turn(): return lax.ppermute(block, 'expert', pairs)]
    ppermute x16 -> x12, waiting for transfers between devices: 1.42 us -> 0.15 us  [core(): return lax.ppermute(block, 'expert', core_pairs)]
    pallas_call x4 -> x6, Pallas kernels: 18.5 us -> 17.3 us  [the longest x4 11.8 us: expert_rows(): pl.pallas_call(expert_kernel, in_specs=[pl.BlockSpec(memory_space=pltpu.S...]
    ppermute x16 -> x12, starting transfers between devices: 3.26 us -> 2.43 us  [core(): return lax.ppermute(block, 'expert', core_pairs)]
  transfers between devices with their start and end apart: 30 -> 26, of which waited for: 9 -> 10; matrix products, arithmetic and copies ran while one was open for 0% -> 1% of each run, Pallas kernels for 16% -> 18%
where the time goes in v2:
time: 84.8 us; the launch traced here: 84.6 us
  waiting for transfers between devices  42.1 us (50%)
  starting transfers between devices  23.5 us (28%)
  Pallas kernels  17.3 us (20%)
  other arithmetic  1.5 us (2%)
    ppermute x6, waiting for transfers between devices, turn(): return lax.ppermute(block, 'expert', pairs)  29.7 us
    ppermute x8, waiting for transfers between devices, side(): return lax.ppermute(block, 'expert', side_pairs)  12.3 us
    pallas_call x4, Pallas kernels, expert_rows(): pl.pallas_call(expert_kernel, in_specs=[pl.BlockSpec(memory_space=pltpu.S...  11.8 us
    ppermute x6, starting transfers between devices, turn(): return lax.ppermute(block, 'expert', pairs)  11.4 us
    ppermute x8, starting transfers between devices, side(): return lax.ppermute(block, 'expert', side_pairs)  9.65 us
    pallas_call x1, Pallas kernels, load(): pl.pallas_call(load_kernel, in_specs=[pl.BlockSpec(memory_space=pltpu.HBM...  3.78 us
    ppermute x12, starting transfers between devices, core(): return lax.ppermute(block, 'expert', core_pairs)  2.43 us
  transfers between devices with their start and end apart: 26, of which 10 were waited for; matrix products, arithmetic and copies ran while one was open for 1% of the time, Pallas kernels for 18%

profile of v2, /device:TPU:0, one launch (start us, length us, event | category | flops | bytes accessed | tf_op | source)
XLA Modules:
  0.0 84.6 jit_solution(4317418077144662299)
XLA Ops:
  0.0 1.7 %shard_map.64.refs_1_ = bf16[64,2176]{1,0:T(8,128)(2,1)} custom-call(bf16[64,2048]{1,0:T(8,128)(2,1)} %tokens_hbm.1, s32[8,64]{1,0:T(8,128)} %bitcast.3, s32[8,64]{1,0:T(8,128)} %bitcast.4), custom_call_target="tpu_custom_call" | custom-call | bytes 524288 | tf_op jit(solution)/shard_map/pallas_call | solution.py:81
  1.7 3.1 %collective-permute-start = (bf16[64,2176]{1,0:T(8,128)(2,1)}, bf16[64,2176]{1,0:T(8,128)(2,1)S(1)}, u32[]{:S(2)}, u32[]{:S(2)}) collective-permute-start(bf16[64,2176]{1,0:T(8,128)(2,1)} %shard_map.64.refs_1_), channel_id=1, source_target_pairs={{0,4},{1,5},{2,6},{3,7},{4,8},{5,9},{6,10},{7,11},{8,12},{9,13},{1... | collective-permute-start | bytes 835592 | tf_op jit(solution)/shard_map/ppermute | solution.py:183
  4.8 1.5 %collective-permute-start.1 = (bf16[64,2176]{1,0:T(8,128)(2,1)}, bf16[64,2176]{1,0:T(8,128)(2,1)S(1)}, u32[]{:S(2)}, u32[]{:S(2)}) collective-permute-start(bf16[64,2176]{1,0:T(8,128)(2,1)} %shard_map.64.refs_1_), channel_id=1, source_target_pairs={{0,2},{1,3},{2,0},{3,1},{4,6},{5,7},{6,4},{7,5},{8,10},{9,11},{10,... | collective-permute-start | bytes 835592 | tf_op jit(solution)/shard_map/ppermute | solution.py:179
  6.3 2.2 %collective-permute-start.3 = (bf16[64,2176]{1,0:T(8,128)(2,1)}, bf16[64,2176]{1,0:T(8,128)(2,1)S(1)}, u32[]{:S(2)}, u32[]{:S(2)}) collective-permute-start(bf16[64,2176]{1,0:T(8,128)(2,1)} %shard_map.64.refs_1_), channel_id=1, source_target_pairs={{0,12},{1,13},{2,14},{3,15},{4,0},{5,1},{6,2},{7,3},{8,4},{9,5},{1... | collective-permute-start | bytes 835592 | tf_op jit(solution)/shard_map/ppermute | solution.py:183
  8.5 6.0 %collective-permute-done.refs_1_ = bf16[64,2176]{1,0:T(8,128)(2,1)S(1)} collective-permute-done((bf16[64,2176]{1,0:T(8,128)(2,1)}, bf16[64,2176]{1,0:T(8,128)(2,1)S(1)}, u32[]{:S(2)}, u32[]{:S(2)}) %collective-permute-start) | collective-permute-done | bytes 278560 | tf_op jit(solution)/shard_map/ppermute | solution.py:183
  14.5 0.0 collective-permute-done.1.refs_0_
  14.5 1.7 %collective-permute-start.2 = (bf16[64,2176]{1,0:T(8,128)(2,1)S(1)}, bf16[64,2176]{1,0:T(8,128)(2,1)S(1)}, u32[]{:S(2)}, u32[]{:S(2)}) collective-permute-start(bf16[64,2176]{1,0:T(8,128)(2,1)S(1)} %collective-permute-done.refs_1_), channel_id=1, source_target_pairs={{0,2},{1,3},{2,0},{3,1},{4,6},{5,7},{6,4},{7,5},{8,10},{9,11},{10,... | collective-permute-start | bytes 835592 | tf_op jit(solution)/shard_map/ppermute | solution.py:179
  16.3 0.0 collective-permute-start.6
  16.3 4.1 %collective-permute-done.3.refs_1_ = bf16[64,2176]{1,0:T(8,128)(2,1)S(1)} collective-permute-done((bf16[64,2176]{1,0:T(8,128)(2,1)}, bf16[64,2176]{1,0:T(8,128)(2,1)S(1)}, u32[]{:S(2)}, u32[]{:S(2)}) %collective-permute-start.3) | collective-permute-done | bytes 278560 | tf_op jit(solution)/shard_map/ppermute | solution.py:183
  20.4 1.1 %collective-permute-start.9 = (bf16[64,2176]{1,0:T(8,128)(2,1)S(1)}, bf16[64,2176]{1,0:T(8,128)(2,1)S(1)}, u32[]{:S(2)}, u32[]{:S(2)}) collective-permute-start(bf16[64,2176]{1,0:T(8,128)(2,1)S(1)} %collective-permute-done.3.refs_1_), channel_id=1, source_target_pairs={{0,2},{1,3},{2,0},{3,1},{4,6},{5,7},{6,4},{7,5},{8,10},{9,11},{10,... | collective-permute-start | bytes 835592 | tf_op jit(solution)/shard_map/ppermute | solution.py:179
  21.5 0.0 collective-permute-start.5
  21.5 0.0 collective-permute-done.2.refs_0_
  21.5 0.5 collective-permute-start.4
  22.0 0.0 collective-permute-start.11
  22.1 4.4 %collective-permute-done.6.refs_1_ = bf16[64,2176]{1,0:T(8,128)(2,1)S(1)} collective-permute-done((bf16[64,2176]{1,0:T(8,128)(2,1)S(1)}, bf16[64,2176]{1,0:T(8,128)(2,1)S(1)}, u32[]{:S(2)}, u32[]{:S(2)}) %collective-permute-start.6) | collective-permute-done | bytes 278560 | tf_op jit(solution)/shard_map/ppermute | solution.py:183
  26.4 3.8 %shard_map.65 = (bf16[1,2048,768]{2,1,0:T(8,128)(2,1)S(1)}, bf16[1,2048,768]{2,1,0:T(8,128)(2,1)S(1)}, bf16[1,768,2048]{2,1,0:T(8,128)(2,1)S(1)}) custom-call(bf16[1,2048,768]{2,1,0:T(8,128)(2,1)} %refs_0_, bf16[1,2048,768]{2,1,0:T(8,128)(2,1)} %refs_1_, bf16[1,768,2048]{2,1,0:T(8,128)(2,1)} %refs_2_), custom_call_target="tpu_custom_call" | custom-call | bytes 9437184 | tf_op jit(solution)/shard_map/pallas_call | solution.py:110
  30.2 0.0 collective-permute-done.9.refs_0_
  30.2 0.1 collective-permute-start.10
  30.3 0.0 collective-permute-done.5.refs_3_
  30.3 0.0 collective-permute-done.4.refs_2_
  30.3 3.0 %shard_map.66 = (bf16[128,2048]{1,0:T(8,128)(2,1)S(1)}, bf16[128,2048]{1,0:T(8,128)(2,1)S(1)}) custom-call(s32[1]{0:T(128)} %bitcast.own_ref, bf16[64,2176]{1,0:T(8,128)(2,1)S(1)} %collective-permute-done.2.refs_0_, bf16[64,2176]{1,0:T(8,128)(2,1)S(1)} %collective-permute-done.refs_1_, bf16[64,2176]{1,0:T(8,128)(2,1)S(1)} %collective-permute-done.4.refs_2_, ...), custom_call_target="tpu_custom_call" | custom-call | flops 2415919104 | bytes 2228224 | tf_op jit(solution)/shard_map/pallas_call | solution.py:153
  33.3 0.5 collective-permute-start.7
  33.8 0.7 collective-permute-start.13
  34.5 0.0 collective-permute-done.11.refs_3_
  34.6 0.0 collective-permute-done.10.refs_2_
  34.6 3.0 %shard_map.67 = (bf16[128,2048]{1,0:T(8,128)(2,1)S(1)}, bf16[128,2048]{1,0:T(8,128)(2,1)S(1)}) custom-call(s32[1]{0:T(128)} %bitcast.own_ref, bf16[64,2176]{1,0:T(8,128)(2,1)S(1)} %collective-permute-done.9.refs_0_, bf16[64,2176]{1,0:T(8,128)(2,1)S(1)} %collective-permute-done.3.refs_1_, bf16[64,2176]{1,0:T(8,128)(2,1)S(1)} %collective-permute-done.10.refs_2_, ...), custom_call_target="tpu_custom_call" | custom-call | flops 2415919104 | bytes 2228224 | tf_op jit(solution)/shard_map/pallas_call | solution.py:153
  37.5 0.1 collective-permute-start.12
  37.6 0.5 collective-permute-start.17
  38.1 0.1 collective-permute-start.16
  38.2 4.3 %collective-permute-done.13.refs_0_ = bf16[64,2176]{1,0:T(8,128)(2,1)S(1)} collective-permute-done((bf16[64,2176]{1,0:T(8,128)(2,1)S(1)}, bf16[64,2176]{1,0:T(8,128)(2,1)S(1)}, u32[]{:S(2)}, u32[]{:S(2)}) %collective-permute-start.13) | collective-permute-done | bytes 278560 | tf_op jit(solution)/shard_map/ppermute | solution.py:179
  42.5 0.0 collective-permute-start.15
  42.5 0.0 collective-permute-done.7
  42.5 0.5 collective-permute-start.14
  43.0 0.1 add_convert_fusion.8
  43.1 0.0 collective-permute-done.12
  43.1 0.8 collective-permute-start.8
  43.8 0.1 add_convert_fusion.6
  43.9 0.1 collective-permute-done.15.refs_3_
  44.0 1.3 %collective-permute-start.24 = (bf16[64,2048]{1,0:T(8,128)(2,1)S(1)}, bf16[64,2048]{1,0:T(8,128)(2,1)S(1)}, u32[]{:S(2)}, u32[]{:S(2)}) collective-permute-start(bf16[64,2048]{1,0:T(8,128)(2,1)S(1)} %add_convert_fusion.6), channel_id=1, source_target_pairs={{0,2},{1,3},{2,0},{3,1},{4,6},{5,7},{6,4},{7,5},{8,10},{9,11},{10,... | collective-permute-start | bytes 786440 | tf_op jit(solution)/shard_map/ppermute | solution.py:179
  45.3 0.0 collective-permute-done.14.refs_2_
  45.3 3.0 %shard_map.68 = (bf16[128,2048]{1,0:T(8,128)(2,1)S(1)}, bf16[128,2048]{1,0:T(8,128)(2,1)S(1)}) custom-call(s32[1]{0:T(128)} %bitcast.own_ref, bf16[64,2176]{1,0:T(8,128)(2,1)S(1)} %collective-permute-done.13.refs_0_, bf16[64,2176]{1,0:T(8,128)(2,1)S(1)} %collective-permute-done.6.refs_1_, bf16[64,2176]{1,0:T(8,128)(2,1)S(1)} %collective-permute-done.14.refs_2_, ...), custom_call_target="tpu_custom_call" | custom-call | flops 2415919104 | bytes 2228224 | tf_op jit(solution)/shard_map/pallas_call | solution.py:153
  48.3 0.1 collective-permute-start.19
  48.4 4.0 %collective-permute-done.8 = bf16[64,2048]{1,0:T(8,128)(2,1)S(1)} collective-permute-done((bf16[64,2048]{1,0:T(8,128)(2,1)S(1)}, bf16[64,2048]{1,0:T(8,128)(2,1)S(1)}, u32[]{:S(2)}, u32[]{:S(2)}) %collective-permute-start.8) | collective-permute-done | bytes 262176 | tf_op jit(solution)/shard_map/ppermute | solution.py:179
  52.3 0.1 add_convert_fusion.7
  52.4 0.0 collective-permute-done.17.refs_3_
  52.4 0.0 collective-permute-done.16.refs_2_
  52.4 3.0 %shard_map.69 = (bf16[128,2048]{1,0:T(8,128)(2,1)S(1)}, bf16[128,2048]{1,0:T(8,128)(2,1)S(1)}) custom-call(s32[1]{0:T(128)} %bitcast.own_ref, bf16[64,2176]{1,0:T(8,128)(2,1)S(1)} %collective-permute-done.1.refs_0_, bf16[64,2176]{1,0:T(8,128)(2,1)S(1)} %copy-done, bf16[64,2176]{1,0:T(8,128)(2,1)S(1)} %collective-permute-done.16.refs_2_, ...), custom_call_target="tpu_custom_call" | custom-call | flops 2415919104 | bytes 2228224 | tf_op jit(solution)/shard_map/pallas_call | solution.py:153
  55.4 0.1 collective-permute-start.18
  55.5 0.0 collective-permute-done.19
  55.5 0.1 add_convert_fusion.4
  55.6 0.8 collective-permute-start.22
  56.3 0.6 collective-permute-done.24
  57.0 0.1 add_convert_fusion.1
  57.1 0.1 collective-permute-start.25
  57.1 3.8 %collective-permute-start.21 = (bf16[64,2048]{1,0:T(8,128)(2,1)S(1)}, bf16[64,2048]{1,0:T(8,128)(2,1)S(1)}, u32[]{:S(2)}, u32[]{:S(2)}) collective-permute-start(bf16[64,2048]{1,0:T(8,128)(2,1)S(1)} %add_convert_fusion.7), channel_id=1, source_target_pairs={{0,12},{1,13},{2,14},{3,15},{4,0},{5,1},{6,2},{7,3},{8,4},{9,5},{1... | collective-permute-start | bytes 786440 | tf_op jit(solution)/shard_map/ppermute | solution.py:183
  61.0 3.4 %collective-permute-done.22 = bf16[64,2048]{1,0:T(8,128)(2,1)S(1)} collective-permute-done((bf16[64,2048]{1,0:T(8,128)(2,1)S(1)}, bf16[64,2048]{1,0:T(8,128)(2,1)S(1)}, u32[]{:S(2)}, u32[]{:S(2)}) %collective-permute-start.22) | collective-permute-done | bytes 262176 | tf_op jit(solution)/shard_map/ppermute | solution.py:179
  64.3 0.1 add_convert_fusion.2
  64.4 2.2 %collective-permute-start.23 = (bf16[64,2048]{1,0:T(8,128)(2,1)S(1)}, bf16[64,2048]{1,0:T(8,128)(2,1)S(1)}, u32[]{:S(2)}, u32[]{:S(2)}) collective-permute-start(bf16[64,2048]{1,0:T(8,128)(2,1)S(1)} %add_convert_fusion.2), channel_id=1, source_target_pairs={{0,8},{1,9},{2,10},{3,11},{4,12},{5,13},{6,14},{7,15},{8,0},{9,1},... | collective-permute-start | bytes 786440 | tf_op jit(solution)/shard_map/ppermute | solution.py:183
  66.7 0.1 add_convert_fusion.5
  66.7 1.8 %collective-permute-start.20 = (bf16[64,2048]{1,0:T(8,128)(2,1)S(1)}, bf16[64,2048]{1,0:T(8,128)(2,1)S(1)}, u32[]{:S(2)}, u32[]{:S(2)}) collective-permute-start(bf16[64,2048]{1,0:T(8,128)(2,1)S(1)} %add_convert_fusion.5), channel_id=1, source_target_pairs={{0,2},{1,3},{2,0},{3,1},{4,6},{5,7},{6,4},{7,5},{8,10},{9,11},{10,... | collective-permute-start | bytes 786440 | tf_op jit(solution)/shard_map/ppermute | solution.py:179
  68.5 3.7 %collective-permute-done.21 = bf16[64,2048]{1,0:T(8,128)(2,1)S(1)} collective-permute-done((bf16[64,2048]{1,0:T(8,128)(2,1)S(1)}, bf16[64,2048]{1,0:T(8,128)(2,1)S(1)}, u32[]{:S(2)}, u32[]{:S(2)}) %collective-permute-start.21) | collective-permute-done | bytes 262176 | tf_op jit(solution)/shard_map/ppermute | solution.py:183
  72.3 11.4 %collective-permute-done.23 = bf16[64,2048]{1,0:T(8,128)(2,1)S(1)} collective-permute-done((bf16[64,2048]{1,0:T(8,128)(2,1)S(1)}, bf16[64,2048]{1,0:T(8,128)(2,1)S(1)}, u32[]{:S(2)}, u32[]{:S(2)}) %collective-permute-start.23) | collective-permute-done | bytes 262176 | tf_op jit(solution)/shard_map/ppermute | solution.py:183
  83.7 0.0 collective-permute-done.20
  83.7 0.9 %add_convert_fusion = bf16[64,2048]{1,0:T(8,128)(2,1)} fusion(bf16[64,2048]{1,0:T(8,128)(2,1)S(1)} %collective-permute-done.25, bf16[64,2048]{1,0:T(8,128)(2,1)S(1)} %collective-permute-done.23, bf16[64,2048]{1,0:T(8,128)(2,1)S(1)} %collective-permute-done.21, bf16[64,2048]{1,0:T(8,128)(2,1)S(1)} %collective-permute-done.20, ...), kind=kLoop, calls=%fused_computation | loop fusion | flops 1835008 | bytes 1835008 | tf_op jit(solution)/shard_map/convert_element_type | solution.py:251
  (4 shorter events, 0.0 us)
Async XLA Ops:
  1.7 12.8 %collective-permute-start = (bf16[64,2176]{1,0:T(8,128)(2,1)}, bf16[64,2176]{1,0:T(8,128)(2,1)S(1)}, u32[]{:S(2)}, u32[]{:S(2)}) collective-permute-start(bf16[64,2176]{1,0:T(8,128)(2,1)} %shard_map.64.refs_1_), channel_id=1, source_target_pairs={{0,4},{1,5},{2,6},{3,7},{4,8},{5,9},{6,10},{7,11},{8,12},{9,13},{1... | collective-permute-start | bytes 835592 | tf_op jit(solution)/shard_map/ppermute | solution.py:183
  4.8 9.8 %collective-permute-start.1 = (bf16[64,2176]{1,0:T(8,128)(2,1)}, bf16[64,2176]{1,0:T(8,128)(2,1)S(1)}, u32[]{:S(2)}, u32[]{:S(2)}) collective-permute-start(bf16[64,2176]{1,0:T(8,128)(2,1)} %shard_map.64.refs_1_), channel_id=1, source_target_pairs={{0,2},{1,3},{2,0},{3,1},{4,6},{5,7},{6,4},{7,5},{8,10},{9,11},{10,... | collective-permute-start | bytes 835592 | tf_op jit(solution)/shard_map/ppermute | solution.py:179
  6.3 14.2 %collective-permute-start.3 = (bf16[64,2176]{1,0:T(8,128)(2,1)}, bf16[64,2176]{1,0:T(8,128)(2,1)S(1)}, u32[]{:S(2)}, u32[]{:S(2)}) collective-permute-start(bf16[64,2176]{1,0:T(8,128)(2,1)} %shard_map.64.refs_1_), channel_id=1, source_target_pairs={{0,12},{1,13},{2,14},{3,15},{4,0},{5,1},{6,2},{7,3},{8,4},{9,5},{1... | collective-permute-start | bytes 835592 | tf_op jit(solution)/shard_map/ppermute | solution.py:183
  14.5 7.0 %collective-permute-start.2 = (bf16[64,2176]{1,0:T(8,128)(2,1)S(1)}, bf16[64,2176]{1,0:T(8,128)(2,1)S(1)}, u32[]{:S(2)}, u32[]{:S(2)}) collective-permute-start(bf16[64,2176]{1,0:T(8,128)(2,1)S(1)} %collective-permute-done.refs_1_), channel_id=1, source_target_pairs={{0,2},{1,3},{2,0},{3,1},{4,6},{5,7},{6,4},{7,5},{8,10},{9,11},{10,... | collective-permute-start | bytes 835592 | tf_op jit(solution)/shard_map/ppermute | solution.py:179
  16.3 10.1 %collective-permute-start.6 = (bf16[64,2176]{1,0:T(8,128)(2,1)S(1)}, bf16[64,2176]{1,0:T(8,128)(2,1)S(1)}, u32[]{:S(2)}, u32[]{:S(2)}) collective-permute-start(bf16[64,2176]{1,0:T(8,128)(2,1)S(1)} %collective-permute-done.refs_1_), channel_id=1, source_target_pairs={{0,4},{1,5},{2,6},{3,7},{4,8},{5,9},{6,10},{7,11},{8,12},{9,13},{1... | collective-permute-start | bytes 835592 | tf_op jit(solution)/shard_map/ppermute | solution.py:183
  20.4 9.8 %collective-permute-start.9 = (bf16[64,2176]{1,0:T(8,128)(2,1)S(1)}, bf16[64,2176]{1,0:T(8,128)(2,1)S(1)}, u32[]{:S(2)}, u32[]{:S(2)}) collective-permute-start(bf16[64,2176]{1,0:T(8,128)(2,1)S(1)} %collective-permute-done.3.refs_1_), channel_id=1, source_target_pairs={{0,2},{1,3},{2,0},{3,1},{4,6},{5,7},{6,4},{7,5},{8,10},{9,11},{10,... | collective-permute-start | bytes 835592 | tf_op jit(solution)/shard_map/ppermute | solution.py:179
  21.5 8.8 %collective-permute-start.5 = (bf16[64,2176]{1,0:T(8,128)(2,1)S(1)}, bf16[64,2176]{1,0:T(8,128)(2,1)S(1)}, u32[]{:S(2)}, u32[]{:S(2)}) collective-permute-start(bf16[64,2176]{1,0:T(8,128)(2,1)S(1)} %collective-permute-done.refs_1_), channel_id=1, source_target_pairs={{0,1},{1,0},{2,3},{3,2},{4,5},{5,4},{6,7},{7,6},{8,9},{9,8},{10,11... | collective-permute-start | bytes 835592 | tf_op jit(solution)/shard_map/ppermute | solution.py:176
  21.5 8.8 %collective-permute-start.4 = (bf16[64,2176]{1,0:T(8,128)(2,1)S(1)}, bf16[64,2176]{1,0:T(8,128)(2,1)S(1)}, u32[]{:S(2)}, u32[]{:S(2)}) collective-permute-start(bf16[64,2176]{1,0:T(8,128)(2,1)S(1)} %collective-permute-done.2.refs_0_), channel_id=1, source_target_pairs={{0,1},{1,0},{2,3},{3,2},{4,5},{5,4},{6,7},{7,6},{8,9},{9,8},{10,11... | collective-permute-start | bytes 835592 | tf_op jit(solution)/shard_map/ppermute | solution.py:176
  22.0 12.5 %collective-permute-start.11 = (bf16[64,2176]{1,0:T(8,128)(2,1)S(1)}, bf16[64,2176]{1,0:T(8,128)(2,1)S(1)}, u32[]{:S(2)}, u32[]{:S(2)}) collective-permute-start(bf16[64,2176]{1,0:T(8,128)(2,1)S(1)} %collective-permute-done.3.refs_1_), channel_id=1, source_target_pairs={{0,1},{1,0},{2,3},{3,2},{4,5},{5,4},{6,7},{7,6},{8,9},{9,8},{10,11... | collective-permute-start | bytes 835592 | tf_op jit(solution)/shard_map/ppermute | solution.py:176
  30.2 4.3 %collective-permute-start.10 = (bf16[64,2176]{1,0:T(8,128)(2,1)S(1)}, bf16[64,2176]{1,0:T(8,128)(2,1)S(1)}, u32[]{:S(2)}, u32[]{:S(2)}) collective-permute-start(bf16[64,2176]{1,0:T(8,128)(2,1)S(1)} %collective-permute-done.9.refs_0_), channel_id=1, source_target_pairs={{0,1},{1,0},{2,3},{3,2},{4,5},{5,4},{6,7},{7,6},{8,9},{9,8},{10,11... | collective-permute-start | bytes 835592 | tf_op jit(solution)/shard_map/ppermute | solution.py:176
  33.3 4.3 %copy-start = (bf16[64,2176]{1,0:T(8,128)(2,1)S(1)}, bf16[64,2176]{1,0:T(8,128)(2,1)}, u32[]{:S(2)}) copy-start(bf16[64,2176]{1,0:T(8,128)(2,1)} %shard_map.64.refs_1_) | copy-start | bytes 835588
  33.3 9.2 %collective-permute-start.7 = (bf16[128,2048]{1,0:T(8,128)(2,1)S(1)}, bf16[128,2048]{1,0:T(8,128)(2,1)S(1)}, u32[]{:S(2)}, u32[]{:S(2)}) collective-permute-start(bf16[128,2048]{1,0:T(8,128)(2,1)S(1)} %get-tuple-element.38), channel_id=1, source_target_pairs={{0,1},{1,0},{2,3},{3,2},{4,5},{5,4},{6,7},{7,6},{8,9},{9,8},{10,11... | collective-permute-start | bytes 1572872 | tf_op jit(solution)/shard_map/ppermute | solution.py:176
  33.8 8.6 %collective-permute-start.13 = (bf16[64,2176]{1,0:T(8,128)(2,1)S(1)}, bf16[64,2176]{1,0:T(8,128)(2,1)S(1)}, u32[]{:S(2)}, u32[]{:S(2)}) collective-permute-start(bf16[64,2176]{1,0:T(8,128)(2,1)S(1)} %collective-permute-done.6.refs_1_), channel_id=1, source_target_pairs={{0,2},{1,3},{2,0},{3,1},{4,6},{5,7},{6,4},{7,5},{8,10},{9,11},{10,... | collective-permute-start | bytes 835592 | tf_op jit(solution)/shard_map/ppermute | solution.py:179
  37.5 5.6 %collective-permute-start.12 = (bf16[128,2048]{1,0:T(8,128)(2,1)S(1)}, bf16[128,2048]{1,0:T(8,128)(2,1)S(1)}, u32[]{:S(2)}, u32[]{:S(2)}) collective-permute-start(bf16[128,2048]{1,0:T(8,128)(2,1)S(1)} %get-tuple-element.42), channel_id=1, source_target_pairs={{0,1},{1,0},{2,3},{3,2},{4,5},{5,4},{6,7},{7,6},{8,9},{9,8},{10,11... | collective-permute-start | bytes 1572872 | tf_op jit(solution)/shard_map/ppermute | solution.py:176
  37.6 14.8 %collective-permute-start.17 = (bf16[64,2176]{1,0:T(8,128)(2,1)S(1)}, bf16[64,2176]{1,0:T(8,128)(2,1)S(1)}, u32[]{:S(2)}, u32[]{:S(2)}) collective-permute-start(bf16[64,2176]{1,0:T(8,128)(2,1)S(1)} %copy-done), channel_id=1, source_target_pairs={{0,1},{1,0},{2,3},{3,2},{4,5},{5,4},{6,7},{7,6},{8,9},{9,8},{10,11... | collective-permute-start | bytes 835592 | tf_op jit(solution)/shard_map/ppermute | solution.py:176
  38.1 14.3 %collective-permute-start.16 = (bf16[64,2176]{1,0:T(8,128)(2,1)S(1)}, bf16[64,2176]{1,0:T(8,128)(2,1)S(1)}, u32[]{:S(2)}, u32[]{:S(2)}) collective-permute-start(bf16[64,2176]{1,0:T(8,128)(2,1)S(1)} %collective-permute-done.1.refs_0_), channel_id=1, source_target_pairs={{0,1},{1,0},{2,3},{3,2},{4,5},{5,4},{6,7},{7,6},{8,9},{9,8},{10,11... | collective-permute-start | bytes 835592 | tf_op jit(solution)/shard_map/ppermute | solution.py:176
  42.5 1.6 %collective-permute-start.15 = (bf16[64,2176]{1,0:T(8,128)(2,1)S(1)}, bf16[64,2176]{1,0:T(8,128)(2,1)S(1)}, u32[]{:S(2)}, u32[]{:S(2)}) collective-permute-start(bf16[64,2176]{1,0:T(8,128)(2,1)S(1)} %collective-permute-done.6.refs_1_), channel_id=1, source_target_pairs={{0,1},{1,0},{2,3},{3,2},{4,5},{5,4},{6,7},{7,6},{8,9},{9,8},{10,11... | collective-permute-start | bytes 835592 | tf_op jit(solution)/shard_map/ppermute | solution.py:176
  42.5 2.8 %collective-permute-start.14 = (bf16[64,2176]{1,0:T(8,128)(2,1)S(1)}, bf16[64,2176]{1,0:T(8,128)(2,1)S(1)}, u32[]{:S(2)}, u32[]{:S(2)}) collective-permute-start(bf16[64,2176]{1,0:T(8,128)(2,1)S(1)} %collective-permute-done.13.refs_0_), channel_id=1, source_target_pairs={{0,1},{1,0},{2,3},{3,2},{4,5},{5,4},{6,7},{7,6},{8,9},{9,8},{10,11... | collective-permute-start | bytes 835592 | tf_op jit(solution)/shard_map/ppermute | solution.py:176
  43.1 9.2 %collective-permute-start.8 = (bf16[64,2048]{1,0:T(8,128)(2,1)S(1)}, bf16[64,2048]{1,0:T(8,128)(2,1)S(1)}, u32[]{:S(2)}, u32[]{:S(2)}) collective-permute-start(bf16[64,2048]{1,0:T(8,128)(2,1)S(1)} %add_convert_fusion.8), channel_id=1, source_target_pairs={{0,2},{1,3},{2,0},{3,1},{4,6},{5,7},{6,4},{7,5},{8,10},{9,11},{10,... | collective-permute-start | bytes 786440 | tf_op jit(solution)/shard_map/ppermute | solution.py:179
  44.0 12.9 %collective-permute-start.24 = (bf16[64,2048]{1,0:T(8,128)(2,1)S(1)}, bf16[64,2048]{1,0:T(8,128)(2,1)S(1)}, u32[]{:S(2)}, u32[]{:S(2)}) collective-permute-start(bf16[64,2048]{1,0:T(8,128)(2,1)S(1)} %add_convert_fusion.6), channel_id=1, source_target_pairs={{0,2},{1,3},{2,0},{3,1},{4,6},{5,7},{6,4},{7,5},{8,10},{9,11},{10,... | collective-permute-start | bytes 786440 | tf_op jit(solution)/shard_map/ppermute | solution.py:179
  48.3 7.2 %collective-permute-start.19 = (bf16[128,2048]{1,0:T(8,128)(2,1)S(1)}, bf16[128,2048]{1,0:T(8,128)(2,1)S(1)}, u32[]{:S(2)}, u32[]{:S(2)}) collective-permute-start(bf16[128,2048]{1,0:T(8,128)(2,1)S(1)} %get-tuple-element.45), channel_id=1, source_target_pairs={{0,1},{1,0},{2,3},{3,2},{4,5},{5,4},{6,7},{7,6},{8,9},{9,8},{10,11... | collective-permute-start | bytes 1572872 | tf_op jit(solution)/shard_map/ppermute | solution.py:176
  55.4 11.3 %collective-permute-start.18 = (bf16[128,2048]{1,0:T(8,128)(2,1)S(1)}, bf16[128,2048]{1,0:T(8,128)(2,1)S(1)}, u32[]{:S(2)}, u32[]{:S(2)}) collective-permute-start(bf16[128,2048]{1,0:T(8,128)(2,1)S(1)} %get-tuple-element.49), channel_id=1, source_target_pairs={{0,1},{1,0},{2,3},{3,2},{4,5},{5,4},{6,7},{7,6},{8,9},{9,8},{10,11... | collective-permute-start | bytes 1572872 | tf_op jit(solution)/shard_map/ppermute | solution.py:176
  55.6 8.8 %collective-permute-start.22 = (bf16[64,2048]{1,0:T(8,128)(2,1)S(1)}, bf16[64,2048]{1,0:T(8,128)(2,1)S(1)}, u32[]{:S(2)}, u32[]{:S(2)}) collective-permute-start(bf16[64,2048]{1,0:T(8,128)(2,1)S(1)} %add_convert_fusion.4), channel_id=1, source_target_pairs={{0,2},{1,3},{2,0},{3,1},{4,6},{5,7},{6,4},{7,5},{8,10},{9,11},{10,... | collective-permute-start | bytes 786440 | tf_op jit(solution)/shard_map/ppermute | solution.py:179
  57.1 11.4 %collective-permute-start.25 = (bf16[64,2048]{1,0:T(8,128)(2,1)S(1)}, bf16[64,2048]{1,0:T(8,128)(2,1)S(1)}, u32[]{:S(2)}, u32[]{:S(2)}) collective-permute-start(bf16[64,2048]{1,0:T(8,128)(2,1)S(1)} %add_convert_fusion.1), channel_id=1, source_target_pairs={{0,4},{1,5},{2,6},{3,7},{4,8},{5,9},{6,10},{7,11},{8,12},{9,13},{1... | collective-permute-start | bytes 786440 | tf_op jit(solution)/shard_map/ppermute | solution.py:183
  57.1 15.1 %collective-permute-start.21 = (bf16[64,2048]{1,0:T(8,128)(2,1)S(1)}, bf16[64,2048]{1,0:T(8,128)(2,1)S(1)}, u32[]{:S(2)}, u32[]{:S(2)}) collective-permute-start(bf16[64,2048]{1,0:T(8,128)(2,1)S(1)} %add_convert_fusion.7), channel_id=1, source_target_pairs={{0,12},{1,13},{2,14},{3,15},{4,0},{5,1},{6,2},{7,3},{8,4},{9,5},{1... | collective-permute-start | bytes 786440 | tf_op jit(solution)/shard_map/ppermute | solution.py:183
  64.4 19.2 %collective-permute-start.23 = (bf16[64,2048]{1,0:T(8,128)(2,1)S(1)}, bf16[64,2048]{1,0:T(8,128)(2,1)S(1)}, u32[]{:S(2)}, u32[]{:S(2)}) collective-permute-start(bf16[64,2048]{1,0:T(8,128)(2,1)S(1)} %add_convert_fusion.2), channel_id=1, source_target_pairs={{0,8},{1,9},{2,10},{3,11},{4,12},{5,13},{6,14},{7,15},{8,0},{9,1},... | collective-permute-start | bytes 786440 | tf_op jit(solution)/shard_map/ppermute | solution.py:183
  66.7 16.9 %collective-permute-start.20 = (bf16[64,2048]{1,0:T(8,128)(2,1)S(1)}, bf16[64,2048]{1,0:T(8,128)(2,1)S(1)}, u32[]{:S(2)}, u32[]{:S(2)}) collective-permute-start(bf16[64,2048]{1,0:T(8,128)(2,1)S(1)} %add_convert_fusion.5), channel_id=1, source_target_pairs={{0,2},{1,3},{2,0},{3,1},{4,6},{5,7},{6,4},{7,5},{8,10},{9,11},{10,... | collective-permute-start | bytes 786440 | tf_op jit(solution)/shard_map/ppermute | solution.py:179

commit v3 on v2

--- a/solution.py
+++ b/solution.py
@@ -9,6 +9,13 @@
 
 LANES = 128
 PLANE = 4
+PLANES = 4
+ORDER = (
+    ("x", 0, 0), ("z", 1, 1), ("z", 3, 1), ("x", 1, 1), ("z", 2, 1),
+    ("w", 0, 1), ("k", 1, 0), ("x", 3, 1), ("k", 3, 1), ("k", 0, 1),
+    ("x", 2, 1), ("c", 1, 0), ("k", 2, 1), ("c", 2, 0), ("c", 3, 1),
+    ("s", 1, 2), ("s", 2, 0), ("c", 0, 1), ("s", 3, 0), ("s", 0, 0),
+)
 
 
 def swiglu_rows(rows_in, gate_w, up_w, down_w):
@@ -114,9 +121,7 @@
         out_shape=[pltpu.VMEM(m.shape, m.dtype) for m in matrices],
         scratch_shapes=[pltpu.SemaphoreType.DMA((len(matrices),))],
         compiler_params=pltpu.CompilerParams(vmem_limit_bytes=44 * 1024 * 1024),
-        cost_estimate=pl.CostEstimate(
-            flops=0, bytes_accessed=sum(2 * m.size for m in matrices), transcendentals=0
-        ),
+        cost_estimate=pl.CostEstimate(flops=0, bytes_accessed=0, transcendentals=0),
     )(*matrices)
 
 
@@ -157,17 +162,13 @@
         out_shape=[jax.ShapeDtypeStruct((2 * rows, width), jnp.bfloat16)] * 2,
         scratch_shapes=[pltpu.VMEM((PLANE * rows, width), jnp.float32)],
         compiler_params=pltpu.CompilerParams(vmem_limit_bytes=16 * 1024 * 1024),
-        cost_estimate=pl.CostEstimate(
-            flops=6 * PLANE * rows * width * hidden_width,
-            bytes_accessed=4 * PLANE * rows * padded,
-            transcendentals=PLANE * rows * hidden_width,
-        ),
+        cost_estimate=pl.CostEstimate(flops=0, bytes_accessed=0, transcendentals=0),
     )(own, *blocks, gate_matrix, up_matrix, down_matrix)
 
 
-def dense_plan(tokens, expert_ids, gate_units, gate_matrix, up_matrix, down_matrix):
+def dense_plan(tokens, expert_ids, gate_units, *matrices):
     devices = lax.axis_size("expert")
-    planes = devices // PLANE
+    planes = PLANES
     everyone = range(devices)
     core_pairs = [(i, i ^ 1) for i in everyone]
     side_pairs = [(i, i ^ 2) for i in everyone]
@@ -186,68 +187,45 @@
     mine = pack(tokens, expert_ids, gate_units)
     rows = tokens.shape[0]
 
-    def after(block, *earlier):
-        return lax.optimization_barrier((block, *earlier))[0]
-
-    here, beside, core_here, core_beside = {0: mine}, {}, {}, {}
-    keep, give, near, away, sums = {}, {}, {}, {}, {}
-
-    def experts(on, *earlier):
-        four = [beside[on], here[on], core_beside[on], core_here[on]]
-        keep[on], give[on] = expert_rows(after(own, *earlier), four, *weights)
-        return give[on]
+    here, beside, core_here, core_beside, weights = {0: mine}, {}, {}, {}, []
+    keep, give, moved, near, away, sums, homes = {}, {}, {}, {}, {}, {}, []
+    done = []
 
     def wide(block):
         return block.astype(jnp.float32)
 
-    def back(on, *earlier):
-        got = core(after(give[on], *earlier))
-        away[on] = (wide(keep[on][:rows]) + wide(got[:rows])).astype(jnp.bfloat16)
-        near[on] = wide(keep[on][rows:]) + wide(got[rows:])
-        return away[on]
-
-    def across(on, *earlier):
-        moved = side(after(away[on], *earlier))
-        sums[on] = (near[on] + wide(moved)).astype(jnp.bfloat16)
-        return sums[on]
-
-    def home(on, *earlier):
-        sums[on] = turn(after(sums[on], *earlier), planes - on)
-
-    here[1] = turn(mine, 1)
-    here[3] = turn(mine, 3)
-    beside[0] = side(mine)
-    core_here[0] = core(mine)
-    core_beside[0] = core(beside[0])
-    beside[1] = side(after(here[1], beside[0]))
-    here[2] = turn(here[1], 1)
-    core_here[1] = core(here[1])
-    beside[3] = side(after(here[3], here[1]))
-    core_here[3] = core(after(here[3], here[1]))
-    core_beside[1] = core(after(beside[1], here[3]))
-    beside[2] = side(after(here[2], beside[1]))
-    core_here[2] = core(after(here[2], beside[1]))
-    weights = load(
-        *lax.optimization_barrier((gate_matrix, up_matrix, down_matrix, here[2]))[:3]
-    )
-    experts(1)
-    back(1)
-    core_beside[3] = core(beside[3])
-    across(1)
-    experts(3, give[1])
-    back(3)
-    across(3, away[1])
-    core_beside[2] = core(beside[2])
-    experts(2, away[3])
-    back(2)
-    experts(0, sums[1], give[2])
-    back(0, give[2])
-    home(1)
-    across(2)
-    home(3)
-    across(0, away[2])
-    home(2)
-    mixed = functools.reduce(lambda a, b: a + b, [wide(sums[on]) for on in range(4)])
+    def after(block):
+        earlier = done[max(0, len(done) - back) :]
+        return lax.optimization_barrier((block, *earlier))[0]
+
+    for what, on, back in ORDER:
+        if what == "z":
+            here[on] = turn(here[1], 1) if on == 2 else turn(mine, on)
+            beside[on] = side(after(here[on]))
+            core_here[on] = core(after(here[on]))
+            done.append(here[on])
+        elif what == "x":
+            if on == 0:
+                beside[0], core_here[0] = side(mine), core(mine)
+            core_beside[on] = core(after(beside[on]))
+            done.append(beside[on])
+        elif what == "k":
+            blocks = [beside[on], here[on], core_beside[on], core_here[on]]
+            keep[on], give[on] = expert_rows(after(own), blocks, *weights)
+            done.append(give[on])
+        elif what == "w":
+            weights = load(*(after(matrix) for matrix in matrices))
+        elif what == "c":
+            got = core(give[on])
+            near[on] = wide(keep[on][rows:]) + wide(got[rows:])
+            away[on] = (wide(keep[on][:rows]) + wide(got[:rows])).astype(jnp.bfloat16)
+            moved[on] = side(after(away[on]))
+            done.append(away[on])
+        else:
+            sums[on] = (near[on] + wide(moved[on])).astype(jnp.bfloat16)
+            homes.append(turn(after(sums[on]), planes - on) if on else sums[on])
+            done.append(sums[on])
+    mixed = functools.reduce(lambda a, b: a + b, [wide(home) for home in homes])
     return mixed.astype(jnp.bfloat16)
 
 
@@ -255,7 +233,7 @@
     devices = lax.axis_size("expert")
     tok_rows, top_count = expert_ids.shape
     dense = 2 * tok_rows * top_count // devices >= tok_rows
-    if dense and devices % PLANE == 0 and devices <= LANES:
+    if dense and devices == PLANE * PLANES:
         plan = dense_plan
     else:
         plan = routed_plan

time: 84.8 us -> 81 us (0.955)
  starting transfers between devices: 23.5 us -> 21.4 us
  waiting for transfers between devices: 42.1 us -> 40.4 us
    ppermute x6, waiting for transfers between devices: 29.7 us -> 22.1 us  [turn(): return lax.ppermute(block, 'expert', pairs)]
    ppermute x8, waiting for transfers between devices: 12.3 us -> 17.6 us  [side(): return lax.ppermute(block, 'expert', side_pairs)]
    ppermute x8, starting transfers between devices: 9.65 us -> 8.07 us  [side(): return lax.ppermute(block, 'expert', side_pairs)]
  transfers between devices with their start and end apart: 26 -> 26, of which waited for: 10 -> 12; matrix products, arithmetic and copies ran while one was open for 1% -> 1% of each run, Pallas kernels for 18% -> 19%
where the time goes in v3:
time: 81 us; the launch traced here: 80.8 us
  waiting for transfers between devices  40.4 us (50%)
  starting transfers between devices  21.4 us (26%)
  Pallas kernels  17.3 us (21%)
  other arithmetic  1.49 us (2%)
    ppermute x6, waiting for transfers between devices, turn(): return lax.ppermute(block, 'expert', pairs)  22.1 us
    ppermute x8, waiting for transfers between devices, side(): return lax.ppermute(block, 'expert', side_pairs)  17.6 us
    pallas_call x4, Pallas kernels, expert_rows(): pl.pallas_call(expert_kernel, in_specs=[pl.BlockSpec(memory_space=pltpu.S...  11.8 us
    ppermute x6, starting transfers between devices, turn(): return lax.ppermute(block, 'expert', pairs)  11.2 us
    ppermute x8, starting transfers between devices, side(): return lax.ppermute(block, 'expert', side_pairs)  8.07 us
    pallas_call x1, Pallas kernels, load(): pl.pallas_call(load_kernel, in_specs=[pl.BlockSpec(memory_space=pltpu.HBM...  3.78 us
    ppermute x12, starting transfers between devices, core(): return lax.ppermute(block, 'expert', core_pairs)  2.15 us
    pallas_call x1, Pallas kernels, pack(): pl.pallas_call(pack_kernel, in_specs=[pl.BlockSpec(memory_space=pltpu.HBM...  1.68 us
  transfers between devices with their start and end apart: 26, of which 12 were waited for; matrix products, arithmetic and copies ran while one was open for 1% of the time, Pallas kernels for 19%

profile of v3, /device:TPU:0, one launch (start us, length us, event | category | flops | bytes accessed | tf_op | source)
XLA Modules:
  0.0 80.8 jit_solution(1675477901626549677)
XLA Ops:
  0.0 1.7 %shard_map.64.refs_1_ = bf16[64,2176]{1,0:T(8,128)(2,1)} custom-call(bf16[64,2048]{1,0:T(8,128)(2,1)} %tokens_hbm.1, s32[8,64]{1,0:T(8,128)} %bitcast.3, s32[8,64]{1,0:T(8,128)} %bitcast.4), custom_call_target="tpu_custom_call" | custom-call | bytes 524288 | tf_op jit(solution)/shard_map/pallas_call | solution.py:88
  1.7 3.1 %collective-permute-start = (bf16[64,2176]{1,0:T(8,128)(2,1)}, bf16[64,2176]{1,0:T(8,128)(2,1)S(1)}, u32[]{:S(2)}, u32[]{:S(2)}) collective-permute-start(bf16[64,2176]{1,0:T(8,128)(2,1)} %shard_map.64.refs_1_), channel_id=1, source_target_pairs={{0,4},{1,5},{2,6},{3,7},{4,8},{5,9},{6,10},{7,11},{8,12},{9,13},{1... | collective-permute-start | bytes 835592 | tf_op jit(solution)/shard_map/ppermute | solution.py:184
  4.8 1.5 %collective-permute-start.1 = (bf16[64,2176]{1,0:T(8,128)(2,1)}, bf16[64,2176]{1,0:T(8,128)(2,1)S(1)}, u32[]{:S(2)}, u32[]{:S(2)}) collective-permute-start(bf16[64,2176]{1,0:T(8,128)(2,1)} %shard_map.64.refs_1_), channel_id=1, source_target_pairs={{0,2},{1,3},{2,0},{3,1},{4,6},{5,7},{6,4},{7,5},{8,10},{9,11},{10,... | collective-permute-start | bytes 835592 | tf_op jit(solution)/shard_map/ppermute | solution.py:180
  6.3 2.2 %collective-permute-start.3 = (bf16[64,2176]{1,0:T(8,128)(2,1)}, bf16[64,2176]{1,0:T(8,128)(2,1)S(1)}, u32[]{:S(2)}, u32[]{:S(2)}) collective-permute-start(bf16[64,2176]{1,0:T(8,128)(2,1)} %shard_map.64.refs_1_), channel_id=1, source_target_pairs={{0,12},{1,13},{2,14},{3,15},{4,0},{5,1},{6,2},{7,3},{8,4},{9,5},{1... | collective-permute-start | bytes 835592 | tf_op jit(solution)/shard_map/ppermute | solution.py:184
  8.5 6.0 %collective-permute-done.refs_1_ = bf16[64,2176]{1,0:T(8,128)(2,1)S(1)} collective-permute-done((bf16[64,2176]{1,0:T(8,128)(2,1)}, bf16[64,2176]{1,0:T(8,128)(2,1)S(1)}, u32[]{:S(2)}, u32[]{:S(2)}) %collective-permute-start) | collective-permute-done | bytes 278560 | tf_op jit(solution)/shard_map/ppermute | solution.py:184
  14.5 0.0 collective-permute-done.1.refs_0_
  14.5 1.7 %collective-permute-start.2 = (bf16[64,2176]{1,0:T(8,128)(2,1)S(1)}, bf16[64,2176]{1,0:T(8,128)(2,1)S(1)}, u32[]{:S(2)}, u32[]{:S(2)}) collective-permute-start(bf16[64,2176]{1,0:T(8,128)(2,1)S(1)} %collective-permute-done.refs_1_), channel_id=1, source_target_pairs={{0,2},{1,3},{2,0},{3,1},{4,6},{5,7},{6,4},{7,5},{8,10},{9,11},{10,... | collective-permute-start | bytes 835592 | tf_op jit(solution)/shard_map/ppermute | solution.py:180
  16.3 0.0 collective-permute-start.6
  16.3 0.0 collective-permute-start.5
  16.3 4.1 %collective-permute-done.3.refs_1_ = bf16[64,2176]{1,0:T(8,128)(2,1)S(1)} collective-permute-done((bf16[64,2176]{1,0:T(8,128)(2,1)}, bf16[64,2176]{1,0:T(8,128)(2,1)S(1)}, u32[]{:S(2)}, u32[]{:S(2)}) %collective-permute-start.3) | collective-permute-done | bytes 278560 | tf_op jit(solution)/shard_map/ppermute | solution.py:184
  20.4 1.1 %collective-permute-done.2.refs_0_ = bf16[64,2176]{1,0:T(8,128)(2,1)S(1)} collective-permute-done((bf16[64,2176]{1,0:T(8,128)(2,1)S(1)}, bf16[64,2176]{1,0:T(8,128)(2,1)S(1)}, u32[]{:S(2)}, u32[]{:S(2)}) %collective-permute-start.2) | collective-permute-done | bytes 278560 | tf_op jit(solution)/shard_map/ppermute | solution.py:180
  21.5 0.0 collective-permute-start.4
  21.6 1.3 %collective-permute-start.10 = (bf16[64,2176]{1,0:T(8,128)(2,1)S(1)}, bf16[64,2176]{1,0:T(8,128)(2,1)S(1)}, u32[]{:S(2)}, u32[]{:S(2)}) collective-permute-start(bf16[64,2176]{1,0:T(8,128)(2,1)S(1)} %collective-permute-done.3.refs_1_), channel_id=1, source_target_pairs={{0,2},{1,3},{2,0},{3,1},{4,6},{5,7},{6,4},{7,5},{8,10},{9,11},{10,... | collective-permute-start | bytes 835592 | tf_op jit(solution)/shard_map/ppermute | solution.py:180
  22.8 0.2 collective-permute-start.12
  23.1 3.4 %collective-permute-done.6.refs_1_ = bf16[64,2176]{1,0:T(8,128)(2,1)S(1)} collective-permute-done((bf16[64,2176]{1,0:T(8,128)(2,1)S(1)}, bf16[64,2176]{1,0:T(8,128)(2,1)S(1)}, u32[]{:S(2)}, u32[]{:S(2)}) %collective-permute-start.6) | collective-permute-done | bytes 278560 | tf_op jit(solution)/shard_map/ppermute | solution.py:184
  26.4 3.8 %shard_map.65 = (bf16[1,2048,768]{2,1,0:T(8,128)(2,1)S(1)}, bf16[1,2048,768]{2,1,0:T(8,128)(2,1)S(1)}, bf16[1,768,2048]{2,1,0:T(8,128)(2,1)S(1)}) custom-call(bf16[1,2048,768]{2,1,0:T(8,128)(2,1)} %refs_0_, bf16[1,2048,768]{2,1,0:T(8,128)(2,1)} %refs_1_, bf16[1,768,2048]{2,1,0:T(8,128)(2,1)} %refs_2_), custom_call_target="tpu_custom_call" | custom-call | tf_op jit(solution)/shard_map/pallas_call | solution.py:117
  30.2 0.0 collective-permute-done.5.refs_3_
  30.2 0.0 collective-permute-done.4.refs_2_
  30.2 3.0 %shard_map.66 = (bf16[128,2048]{1,0:T(8,128)(2,1)S(1)}, bf16[128,2048]{1,0:T(8,128)(2,1)S(1)}) custom-call(s32[1]{0:T(128)} %bitcast.own_ref, bf16[64,2176]{1,0:T(8,128)(2,1)S(1)} %collective-permute-done.2.refs_0_, bf16[64,2176]{1,0:T(8,128)(2,1)S(1)} %collective-permute-done.refs_1_, bf16[64,2176]{1,0:T(8,128)(2,1)S(1)} %collective-permute-done.4.refs_2_, ...), custom_call_target="tpu_custom_call" | custom-call | tf_op jit(solution)/shard_map/pallas_call | solution.py:158
  33.2 0.1 collective-permute-start.7
  33.3 0.0 collective-permute-done.10.refs_0_
  33.3 0.5 collective-permute-start.11
  33.8 0.1 collective-permute-start.14
  33.9 0.4 collective-permute-start.13
  34.3 0.0 collective-permute-done.12.refs_3_
  34.3 0.7 collective-permute-start.9
  35.0 0.6 collective-permute-done.11.refs_2_
  35.6 0.1 collective-permute-start.16
  35.7 2.9 %shard_map.67 = (bf16[128,2048]{1,0:T(8,128)(2,1)S(1)}, bf16[128,2048]{1,0:T(8,128)(2,1)S(1)}) custom-call(s32[1]{0:T(128)} %bitcast.own_ref, bf16[64,2176]{1,0:T(8,128)(2,1)S(1)} %collective-permute-done.10.refs_0_, bf16[64,2176]{1,0:T(8,128)(2,1)S(1)} %collective-permute-done.3.refs_1_, bf16[64,2176]{1,0:T(8,128)(2,1)S(1)} %collective-permute-done.11.refs_2_, ...), custom_call_target="tpu_custom_call" | custom-call | tf_op jit(solution)/shard_map/pallas_call | solution.py:158
  38.7 0.0 collective-permute-done.14.refs_3_
  38.7 0.0 collective-permute-done.13.refs_2_
  38.7 3.0 %shard_map.68 = (bf16[128,2048]{1,0:T(8,128)(2,1)S(1)}, bf16[128,2048]{1,0:T(8,128)(2,1)S(1)}) custom-call(s32[1]{0:T(128)} %bitcast.own_ref, bf16[64,2176]{1,0:T(8,128)(2,1)S(1)} %collective-permute-done.1.refs_0_, bf16[64,2176]{1,0:T(8,128)(2,1)S(1)} %copy-done, bf16[64,2176]{1,0:T(8,128)(2,1)S(1)} %collective-permute-done.13.refs_2_, ...), custom_call_target="tpu_custom_call" | custom-call | tf_op jit(solution)/shard_map/pallas_call | solution.py:158
  41.7 1.3 %collective-permute-done.9.refs_0_ = bf16[64,2176]{1,0:T(8,128)(2,1)S(1)} collective-permute-done((bf16[64,2176]{1,0:T(8,128)(2,1)S(1)}, bf16[64,2176]{1,0:T(8,128)(2,1)S(1)}, u32[]{:S(2)}, u32[]{:S(2)}) %collective-permute-start.9) | collective-permute-done | bytes 278560 | tf_op jit(solution)/shard_map/ppermute | solution.py:180
  42.9 0.0 collective-permute-start.15
  43.0 0.0 collective-permute-done.7
  43.0 0.1 add_convert_fusion.8
  43.0 0.8 collective-permute-start.8
  43.8 0.2 collective-permute-start.24
  44.0 0.3 collective-permute-start.18
  44.3 0.0 collective-permute-done.16.refs_3_
  44.3 0.2 collective-permute-done.15.refs_2_
  44.5 3.0 %shard_map.69 = (bf16[128,2048]{1,0:T(8,128)(2,1)S(1)}, bf16[128,2048]{1,0:T(8,128)(2,1)S(1)}) custom-call(s32[1]{0:T(128)} %bitcast.own_ref, bf16[64,2176]{1,0:T(8,128)(2,1)S(1)} %collective-permute-done.9.refs_0_, bf16[64,2176]{1,0:T(8,128)(2,1)S(1)} %collective-permute-done.6.refs_1_, bf16[64,2176]{1,0:T(8,128)(2,1)S(1)} %collective-permute-done.15.refs_2_, ...), custom_call_target="tpu_custom_call" | custom-call | tf_op jit(solution)/shard_map/pallas_call | solution.py:158
  47.5 0.2 collective-permute-start.17
  47.7 4.1 %collective-permute-done.8 = bf16[64,2048]{1,0:T(8,128)(2,1)S(1)} collective-permute-done((bf16[64,2048]{1,0:T(8,128)(2,1)S(1)}, bf16[64,2048]{1,0:T(8,128)(2,1)S(1)}, u32[]{:S(2)}, u32[]{:S(2)}) %collective-permute-start.8) | collective-permute-done | bytes 262176 | tf_op jit(solution)/shard_map/ppermute | solution.py:180
  51.8 0.1 add_convert_fusion.7
  51.9 0.0 collective-permute-done.24
  51.9 0.1 add_convert_fusion.2
  52.0 0.0 collective-permute-done.17
  52.0 0.1 add_convert_fusion.6
  52.1 0.8 collective-permute-start.20
  52.9 0.0 collective-permute-done.18
  52.9 0.1 add_convert_fusion.5
  52.9 3.5 %collective-permute-start.19 = (bf16[64,2048]{1,0:T(8,128)(2,1)S(1)}, bf16[64,2048]{1,0:T(8,128)(2,1)S(1)}, u32[]{:S(2)}, u32[]{:S(2)}) collective-permute-start(bf16[64,2048]{1,0:T(8,128)(2,1)S(1)} %add_convert_fusion.7), channel_id=1, source_target_pairs={{0,12},{1,13},{2,14},{3,15},{4,0},{5,1},{6,2},{7,3},{8,4},{9,5},{1... | collective-permute-start | bytes 786440 | tf_op jit(solution)/shard_map/ppermute | solution.py:184
  56.4 0.5 collective-permute-start.22
  57.0 4.4 %collective-permute-done.20 = bf16[64,2048]{1,0:T(8,128)(2,1)S(1)} collective-permute-done((bf16[64,2048]{1,0:T(8,128)(2,1)S(1)}, bf16[64,2048]{1,0:T(8,128)(2,1)S(1)}, u32[]{:S(2)}, u32[]{:S(2)}) %collective-permute-start.20) | collective-permute-done | bytes 262176 | tf_op jit(solution)/shard_map/ppermute | solution.py:180
  61.4 0.1 add_convert_fusion.4
  61.5 0.8 collective-permute-start.25
  62.2 2.3 %collective-permute-start.21 = (bf16[64,2048]{1,0:T(8,128)(2,1)S(1)}, bf16[64,2048]{1,0:T(8,128)(2,1)S(1)}, u32[]{:S(2)}, u32[]{:S(2)}) collective-permute-start(bf16[64,2048]{1,0:T(8,128)(2,1)S(1)} %add_convert_fusion.4), channel_id=1, source_target_pairs={{0,8},{1,9},{2,10},{3,11},{4,12},{5,13},{6,14},{7,15},{8,0},{9,1},... | collective-permute-start | bytes 786440 | tf_op jit(solution)/shard_map/ppermute | solution.py:184
  64.5 2.4 %collective-permute-done.22 = bf16[64,2048]{1,0:T(8,128)(2,1)S(1)} collective-permute-done((bf16[64,2048]{1,0:T(8,128)(2,1)S(1)}, bf16[64,2048]{1,0:T(8,128)(2,1)S(1)}, u32[]{:S(2)}, u32[]{:S(2)}) %collective-permute-start.22) | collective-permute-done | bytes 262176 | tf_op jit(solution)/shard_map/ppermute | solution.py:180
  67.0 0.1 add_convert_fusion.3
  67.1 0.1 collective-permute-start.23
  67.2 4.2 %collective-permute-done.25 = bf16[64,2048]{1,0:T(8,128)(2,1)S(1)} collective-permute-done((bf16[64,2048]{1,0:T(8,128)(2,1)S(1)}, bf16[64,2048]{1,0:T(8,128)(2,1)S(1)}, u32[]{:S(2)}, u32[]{:S(2)}) %collective-permute-start.25) | collective-permute-done | bytes 262176 | tf_op jit(solution)/shard_map/ppermute | solution.py:180
  71.3 8.5 %collective-permute-done.21 = bf16[64,2048]{1,0:T(8,128)(2,1)S(1)} collective-permute-done((bf16[64,2048]{1,0:T(8,128)(2,1)S(1)}, bf16[64,2048]{1,0:T(8,128)(2,1)S(1)}, u32[]{:S(2)}, u32[]{:S(2)}) %collective-permute-start.21) | collective-permute-done | bytes 262176 | tf_op jit(solution)/shard_map/ppermute | solution.py:184
  79.9 0.9 %add_convert_fusion = bf16[64,2048]{1,0:T(8,128)(2,1)} fusion(bf16[64,2048]{1,0:T(8,128)(2,1)S(1)} %collective-permute-done.23, bf16[64,2048]{1,0:T(8,128)(2,1)S(1)} %collective-permute-done.21, bf16[64,2048]{1,0:T(8,128)(2,1)S(1)} %collective-permute-done.19, bf16[64,2048]{1,0:T(8,128)(2,1)S(1)} %collective-permute-done.25, ...), kind=kLoop, calls=%fused_computation | loop fusion | flops 1835008 | bytes 1835008 | tf_op jit(solution)/shard_map/convert_element_type | solution.py:229
  (4 shorter events, 0.0 us)
Async XLA Ops:
  1.7 12.8 %collective-permute-start = (bf16[64,2176]{1,0:T(8,128)(2,1)}, bf16[64,2176]{1,0:T(8,128)(2,1)S(1)}, u32[]{:S(2)}, u32[]{:S(2)}) collective-permute-start(bf16[64,2176]{1,0:T(8,128)(2,1)} %shard_map.64.refs_1_), channel_id=1, source_target_pairs={{0,4},{1,5},{2,6},{3,7},{4,8},{5,9},{6,10},{7,11},{8,12},{9,13},{1... | collective-permute-start | bytes 835592 | tf_op jit(solution)/shard_map/ppermute | solution.py:184
  4.8 9.8 %collective-permute-start.1 = (bf16[64,2176]{1,0:T(8,128)(2,1)}, bf16[64,2176]{1,0:T(8,128)(2,1)S(1)}, u32[]{:S(2)}, u32[]{:S(2)}) collective-permute-start(bf16[64,2176]{1,0:T(8,128)(2,1)} %shard_map.64.refs_1_), channel_id=1, source_target_pairs={{0,2},{1,3},{2,0},{3,1},{4,6},{5,7},{6,4},{7,5},{8,10},{9,11},{10,... | collective-permute-start | bytes 835592 | tf_op jit(solution)/shard_map/ppermute | solution.py:180
  6.3 14.2 %collective-permute-start.3 = (bf16[64,2176]{1,0:T(8,128)(2,1)}, bf16[64,2176]{1,0:T(8,128)(2,1)S(1)}, u32[]{:S(2)}, u32[]{:S(2)}) collective-permute-start(bf16[64,2176]{1,0:T(8,128)(2,1)} %shard_map.64.refs_1_), channel_id=1, source_target_pairs={{0,12},{1,13},{2,14},{3,15},{4,0},{5,1},{6,2},{7,3},{8,4},{9,5},{1... | collective-permute-start | bytes 835592 | tf_op jit(solution)/shard_map/ppermute | solution.py:184
  14.5 7.0 %collective-permute-start.2 = (bf16[64,2176]{1,0:T(8,128)(2,1)S(1)}, bf16[64,2176]{1,0:T(8,128)(2,1)S(1)}, u32[]{:S(2)}, u32[]{:S(2)}) collective-permute-start(bf16[64,2176]{1,0:T(8,128)(2,1)S(1)} %collective-permute-done.refs_1_), channel_id=1, source_target_pairs={{0,2},{1,3},{2,0},{3,1},{4,6},{5,7},{6,4},{7,5},{8,10},{9,11},{10,... | collective-permute-start | bytes 835592 | tf_op jit(solution)/shard_map/ppermute | solution.py:180
  16.3 10.1 %collective-permute-start.6 = (bf16[64,2176]{1,0:T(8,128)(2,1)S(1)}, bf16[64,2176]{1,0:T(8,128)(2,1)S(1)}, u32[]{:S(2)}, u32[]{:S(2)}) collective-permute-start(bf16[64,2176]{1,0:T(8,128)(2,1)S(1)} %collective-permute-done.refs_1_), channel_id=1, source_target_pairs={{0,4},{1,5},{2,6},{3,7},{4,8},{5,9},{6,10},{7,11},{8,12},{9,13},{1... | collective-permute-start | bytes 835592 | tf_op jit(solution)/shard_map/ppermute | solution.py:184
  16.3 13.9 %collective-permute-start.5 = (bf16[64,2176]{1,0:T(8,128)(2,1)S(1)}, bf16[64,2176]{1,0:T(8,128)(2,1)S(1)}, u32[]{:S(2)}, u32[]{:S(2)}) collective-permute-start(bf16[64,2176]{1,0:T(8,128)(2,1)S(1)} %collective-permute-done.refs_1_), channel_id=1, source_target_pairs={{0,1},{1,0},{2,3},{3,2},{4,5},{5,4},{6,7},{7,6},{8,9},{9,8},{10,11... | collective-permute-start | bytes 835592 | tf_op jit(solution)/shard_map/ppermute | solution.py:177
  21.5 8.7 %collective-permute-start.4 = (bf16[64,2176]{1,0:T(8,128)(2,1)S(1)}, bf16[64,2176]{1,0:T(8,128)(2,1)S(1)}, u32[]{:S(2)}, u32[]{:S(2)}) collective-permute-start(bf16[64,2176]{1,0:T(8,128)(2,1)S(1)} %collective-permute-done.2.refs_0_), channel_id=1, source_target_pairs={{0,1},{1,0},{2,3},{3,2},{4,5},{5,4},{6,7},{7,6},{8,9},{9,8},{10,11... | collective-permute-start | bytes 835592 | tf_op jit(solution)/shard_map/ppermute | solution.py:177
  21.6 11.7 %collective-permute-start.10 = (bf16[64,2176]{1,0:T(8,128)(2,1)S(1)}, bf16[64,2176]{1,0:T(8,128)(2,1)S(1)}, u32[]{:S(2)}, u32[]{:S(2)}) collective-permute-start(bf16[64,2176]{1,0:T(8,128)(2,1)S(1)} %collective-permute-done.3.refs_1_), channel_id=1, source_target_pairs={{0,2},{1,3},{2,0},{3,1},{4,6},{5,7},{6,4},{7,5},{8,10},{9,11},{10,... | collective-permute-start | bytes 835592 | tf_op jit(solution)/shard_map/ppermute | solution.py:180
  22.8 11.5 %collective-permute-start.12 = (bf16[64,2176]{1,0:T(8,128)(2,1)S(1)}, bf16[64,2176]{1,0:T(8,128)(2,1)S(1)}, u32[]{:S(2)}, u32[]{:S(2)}) collective-permute-start(bf16[64,2176]{1,0:T(8,128)(2,1)S(1)} %collective-permute-done.3.refs_1_), channel_id=1, source_target_pairs={{0,1},{1,0},{2,3},{3,2},{4,5},{5,4},{6,7},{7,6},{8,9},{9,8},{10,11... | collective-permute-start | bytes 835592 | tf_op jit(solution)/shard_map/ppermute | solution.py:177
  30.2 3.6 %copy-start = (bf16[64,2176]{1,0:T(8,128)(2,1)S(1)}, bf16[64,2176]{1,0:T(8,128)(2,1)}, u32[]{:S(2)}) copy-start(bf16[64,2176]{1,0:T(8,128)(2,1)} %shard_map.64.refs_1_) | copy-start | bytes 835588
  33.2 9.8 %collective-permute-start.7 = (bf16[128,2048]{1,0:T(8,128)(2,1)S(1)}, bf16[128,2048]{1,0:T(8,128)(2,1)S(1)}, u32[]{:S(2)}, u32[]{:S(2)}) collective-permute-start(bf16[128,2048]{1,0:T(8,128)(2,1)S(1)} %get-tuple-element.40), channel_id=1, source_target_pairs={{0,1},{1,0},{2,3},{3,2},{4,5},{5,4},{6,7},{7,6},{8,9},{9,8},{10,11... | collective-permute-start | bytes 1572872 | tf_op jit(solution)/shard_map/ppermute | solution.py:177
  33.3 2.3 %collective-permute-start.11 = (bf16[64,2176]{1,0:T(8,128)(2,1)S(1)}, bf16[64,2176]{1,0:T(8,128)(2,1)S(1)}, u32[]{:S(2)}, u32[]{:S(2)}) collective-permute-start(bf16[64,2176]{1,0:T(8,128)(2,1)S(1)} %collective-permute-done.10.refs_0_), channel_id=1, source_target_pairs={{0,1},{1,0},{2,3},{3,2},{4,5},{5,4},{6,7},{7,6},{8,9},{9,8},{10,11... | collective-permute-start | bytes 835592 | tf_op jit(solution)/shard_map/ppermute | solution.py:177
  33.8 4.9 %collective-permute-start.14 = (bf16[64,2176]{1,0:T(8,128)(2,1)S(1)}, bf16[64,2176]{1,0:T(8,128)(2,1)S(1)}, u32[]{:S(2)}, u32[]{:S(2)}) collective-permute-start(bf16[64,2176]{1,0:T(8,128)(2,1)S(1)} %copy-done), channel_id=1, source_target_pairs={{0,1},{1,0},{2,3},{3,2},{4,5},{5,4},{6,7},{7,6},{8,9},{9,8},{10,11... | collective-permute-start | bytes 835592 | tf_op jit(solution)/shard_map/ppermute | solution.py:177
  33.9 4.8 %collective-permute-start.13 = (bf16[64,2176]{1,0:T(8,128)(2,1)S(1)}, bf16[64,2176]{1,0:T(8,128)(2,1)S(1)}, u32[]{:S(2)}, u32[]{:S(2)}) collective-permute-start(bf16[64,2176]{1,0:T(8,128)(2,1)S(1)} %collective-permute-done.1.refs_0_), channel_id=1, source_target_pairs={{0,1},{1,0},{2,3},{3,2},{4,5},{5,4},{6,7},{7,6},{8,9},{9,8},{10,11... | collective-permute-start | bytes 835592 | tf_op jit(solution)/shard_map/ppermute | solution.py:177
  34.3 8.6 %collective-permute-start.9 = (bf16[64,2176]{1,0:T(8,128)(2,1)S(1)}, bf16[64,2176]{1,0:T(8,128)(2,1)S(1)}, u32[]{:S(2)}, u32[]{:S(2)}) collective-permute-start(bf16[64,2176]{1,0:T(8,128)(2,1)S(1)} %collective-permute-done.6.refs_1_), channel_id=1, source_target_pairs={{0,2},{1,3},{2,0},{3,1},{4,6},{5,7},{6,4},{7,5},{8,10},{9,11},{10,... | collective-permute-start | bytes 835592 | tf_op jit(solution)/shard_map/ppermute | solution.py:180
  35.6 8.7 %collective-permute-start.16 = (bf16[64,2176]{1,0:T(8,128)(2,1)S(1)}, bf16[64,2176]{1,0:T(8,128)(2,1)S(1)}, u32[]{:S(2)}, u32[]{:S(2)}) collective-permute-start(bf16[64,2176]{1,0:T(8,128)(2,1)S(1)} %collective-permute-done.6.refs_1_), channel_id=1, source_target_pairs={{0,1},{1,0},{2,3},{3,2},{4,5},{5,4},{6,7},{7,6},{8,9},{9,8},{10,11... | collective-permute-start | bytes 835592 | tf_op jit(solution)/shard_map/ppermute | solution.py:177
  42.9 1.6 %collective-permute-start.15 = (bf16[64,2176]{1,0:T(8,128)(2,1)S(1)}, bf16[64,2176]{1,0:T(8,128)(2,1)S(1)}, u32[]{:S(2)}, u32[]{:S(2)}) collective-permute-start(bf16[64,2176]{1,0:T(8,128)(2,1)S(1)} %collective-permute-done.9.refs_0_), channel_id=1, source_target_pairs={{0,1},{1,0},{2,3},{3,2},{4,5},{5,4},{6,7},{7,6},{8,9},{9,8},{10,11... | collective-permute-start | bytes 835592 | tf_op jit(solution)/shard_map/ppermute | solution.py:177
  43.0 8.8 %collective-permute-start.8 = (bf16[64,2048]{1,0:T(8,128)(2,1)S(1)}, bf16[64,2048]{1,0:T(8,128)(2,1)S(1)}, u32[]{:S(2)}, u32[]{:S(2)}) collective-permute-start(bf16[64,2048]{1,0:T(8,128)(2,1)S(1)} %add_convert_fusion.8), channel_id=1, source_target_pairs={{0,2},{1,3},{2,0},{3,1},{4,6},{5,7},{6,4},{7,5},{8,10},{9,11},{10,... | collective-permute-start | bytes 786440 | tf_op jit(solution)/shard_map/ppermute | solution.py:180
  43.8 8.1 %collective-permute-start.24 = (bf16[128,2048]{1,0:T(8,128)(2,1)S(1)}, bf16[128,2048]{1,0:T(8,128)(2,1)S(1)}, u32[]{:S(2)}, u32[]{:S(2)}) collective-permute-start(bf16[128,2048]{1,0:T(8,128)(2,1)S(1)} %get-tuple-element.48), channel_id=1, source_target_pairs={{0,1},{1,0},{2,3},{3,2},{4,5},{5,4},{6,7},{7,6},{8,9},{9,8},{10,11... | collective-permute-start | bytes 1572872 | tf_op jit(solution)/shard_map/ppermute | solution.py:177
  44.0 8.8 %collective-permute-start.18 = (bf16[128,2048]{1,0:T(8,128)(2,1)S(1)}, bf16[128,2048]{1,0:T(8,128)(2,1)S(1)}, u32[]{:S(2)}, u32[]{:S(2)}) collective-permute-start(bf16[128,2048]{1,0:T(8,128)(2,1)S(1)} %get-tuple-element.46), channel_id=1, source_target_pairs={{0,1},{1,0},{2,3},{3,2},{4,5},{5,4},{6,7},{7,6},{8,9},{9,8},{10,11... | collective-permute-start | bytes 1572872 | tf_op jit(solution)/shard_map/ppermute | solution.py:177
  47.5 4.5 %collective-permute-start.17 = (bf16[128,2048]{1,0:T(8,128)(2,1)S(1)}, bf16[128,2048]{1,0:T(8,128)(2,1)S(1)}, u32[]{:S(2)}, u32[]{:S(2)}) collective-permute-start(bf16[128,2048]{1,0:T(8,128)(2,1)S(1)} %get-tuple-element.51), channel_id=1, source_target_pairs={{0,1},{1,0},{2,3},{3,2},{4,5},{5,4},{6,7},{7,6},{8,9},{9,8},{10,11... | collective-permute-start | bytes 1572872 | tf_op jit(solution)/shard_map/ppermute | solution.py:177
  52.1 9.3 %collective-permute-start.20 = (bf16[64,2048]{1,0:T(8,128)(2,1)S(1)}, bf16[64,2048]{1,0:T(8,128)(2,1)S(1)}, u32[]{:S(2)}, u32[]{:S(2)}) collective-permute-start(bf16[64,2048]{1,0:T(8,128)(2,1)S(1)} %add_convert_fusion.6), channel_id=1, source_target_pairs={{0,2},{1,3},{2,0},{3,1},{4,6},{5,7},{6,4},{7,5},{8,10},{9,11},{10,... | collective-permute-start | bytes 786440 | tf_op jit(solution)/shard_map/ppermute | solution.py:180
  52.9 14.2 %collective-permute-start.19 = (bf16[64,2048]{1,0:T(8,128)(2,1)S(1)}, bf16[64,2048]{1,0:T(8,128)(2,1)S(1)}, u32[]{:S(2)}, u32[]{:S(2)}) collective-permute-start(bf16[64,2048]{1,0:T(8,128)(2,1)S(1)} %add_convert_fusion.7), channel_id=1, source_target_pairs={{0,12},{1,13},{2,14},{3,15},{4,0},{5,1},{6,2},{7,3},{8,4},{9,5},{1... | collective-permute-start | bytes 786440 | tf_op jit(solution)/shard_map/ppermute | solution.py:184
  56.4 10.5 %collective-permute-start.22 = (bf16[64,2048]{1,0:T(8,128)(2,1)S(1)}, bf16[64,2048]{1,0:T(8,128)(2,1)S(1)}, u32[]{:S(2)}, u32[]{:S(2)}) collective-permute-start(bf16[64,2048]{1,0:T(8,128)(2,1)S(1)} %add_convert_fusion.5), channel_id=1, source_target_pairs={{0,2},{1,3},{2,0},{3,1},{4,6},{5,7},{6,4},{7,5},{8,10},{9,11},{10,... | collective-permute-start | bytes 786440 | tf_op jit(solution)/shard_map/ppermute | solution.py:180
  61.5 9.9 %collective-permute-start.25 = (bf16[64,2048]{1,0:T(8,128)(2,1)S(1)}, bf16[64,2048]{1,0:T(8,128)(2,1)S(1)}, u32[]{:S(2)}, u32[]{:S(2)}) collective-permute-start(bf16[64,2048]{1,0:T(8,128)(2,1)S(1)} %add_convert_fusion.2), channel_id=1, source_target_pairs={{0,2},{1,3},{2,0},{3,1},{4,6},{5,7},{6,4},{7,5},{8,10},{9,11},{10,... | collective-permute-start | bytes 786440 | tf_op jit(solution)/shard_map/ppermute | solution.py:180
  62.2 17.6 %collective-permute-start.21 = (bf16[64,2048]{1,0:T(8,128)(2,1)S(1)}, bf16[64,2048]{1,0:T(8,128)(2,1)S(1)}, u32[]{:S(2)}, u32[]{:S(2)}) collective-permute-start(bf16[64,2048]{1,0:T(8,128)(2,1)S(1)} %add_convert_fusion.4), channel_id=1, source_target_pairs={{0,8},{1,9},{2,10},{3,11},{4,12},{5,13},{6,14},{7,15},{8,0},{9,1},... | collective-permute-start | bytes 786440 | tf_op jit(solution)/shard_map/ppermute | solution.py:184
  67.1 12.8 %collective-permute-start.23 = (bf16[64,2048]{1,0:T(8,128)(2,1)S(1)}, bf16[64,2048]{1,0:T(8,128)(2,1)S(1)}, u32[]{:S(2)}, u32[]{:S(2)}) collective-permute-start(bf16[64,2048]{1,0:T(8,128)(2,1)S(1)} %add_convert_fusion.3), channel_id=1, source_target_pairs={{0,4},{1,5},{2,6},{3,7},{4,8},{5,9},{6,10},{7,11},{8,12},{9,13},{1... | collective-permute-start | bytes 786440 | tf_op jit(solution)/shard_map/ppermute | solution.py:184

commit v4 on v3

--- a/solution.py
+++ b/solution.py
@@ -12,7 +12,7 @@
 PLANES = 4
 ORDER = (
     ("x", 0, 0), ("z", 1, 1), ("z", 3, 1), ("x", 1, 1), ("z", 2, 1),
-    ("w", 0, 1), ("k", 1, 0), ("x", 3, 1), ("k", 3, 1), ("k", 0, 1),
+    ("w", 0, 1), ("k", 1, 0), ("x", 3, 1), ("k", 0, 1), ("k", 3, 1),
     ("x", 2, 1), ("c", 1, 0), ("k", 2, 1), ("c", 2, 0), ("c", 3, 1),
     ("s", 1, 2), ("s", 2, 0), ("c", 0, 1), ("s", 3, 0), ("s", 0, 0),
 )

time: 81 us -> 80.9 us (level)
    ppermute x6, starting transfers between devices: 11.2 us -> 10.2 us  [turn(): return lax.ppermute(block, 'expert', pairs)]
where the time goes in v4:
time: 80.9 us; the launch traced here: 80.7 us
  waiting for transfers between devices  40.7 us (50%)
  starting transfers between devices  21.1 us (26%)
  Pallas kernels  17.3 us (21%)
  other arithmetic  1.49 us (2%)
    ppermute x6, waiting for transfers between devices, turn(): return lax.ppermute(block, 'expert', pairs)  22.1 us
    ppermute x8, waiting for transfers between devices, side(): return lax.ppermute(block, 'expert', side_pairs)  17.3 us
    pallas_call x4, Pallas kernels, expert_rows(): pl.pallas_call(expert_kernel, in_specs=[pl.BlockSpec(memory_space=pltpu.S...  11.8 us
    ppermute x6, starting transfers between devices, turn(): return lax.ppermute(block, 'expert', pairs)  10.2 us
    ppermute x8, starting transfers between devices, side(): return lax.ppermute(block, 'expert', side_pairs)  8.37 us
    pallas_call x1, Pallas kernels, load(): pl.pallas_call(load_kernel, in_specs=[pl.BlockSpec(memory_space=pltpu.HBM...  3.78 us
    ppermute x12, starting transfers between devices, core(): return lax.ppermute(block, 'expert', core_pairs)  2.53 us
    pallas_call x1, Pallas kernels, pack(): pl.pallas_call(pack_kernel, in_specs=[pl.BlockSpec(memory_space=pltpu.HBM...  1.68 us
  transfers between devices with their start and end apart: 26, of which 12 were waited for; matrix products, arithmetic and copies ran while one was open for 1% of the time, Pallas kernels for 19%

profile of v4, /device:TPU:0, one launch (start us, length us, event | category | flops | bytes accessed | tf_op | source)
XLA Modules:
  0.0 80.7 jit_solution(6810127628115012516)
XLA Ops:
  0.0 1.7 %shard_map.64.refs_1_ = bf16[64,2176]{1,0:T(8,128)(2,1)} custom-call(bf16[64,2048]{1,0:T(8,128)(2,1)} %tokens_hbm.1, s32[8,64]{1,0:T(8,128)} %bitcast.3, s32[8,64]{1,0:T(8,128)} %bitcast.4), custom_call_target="tpu_custom_call" | custom-call | bytes 524288 | tf_op jit(solution)/shard_map/pallas_call | solution.py:88
  1.7 3.1 %collective-permute-start = (bf16[64,2176]{1,0:T(8,128)(2,1)}, bf16[64,2176]{1,0:T(8,128)(2,1)S(1)}, u32[]{:S(2)}, u32[]{:S(2)}) collective-permute-start(bf16[64,2176]{1,0:T(8,128)(2,1)} %shard_map.64.refs_1_), channel_id=1, source_target_pairs={{0,4},{1,5},{2,6},{3,7},{4,8},{5,9},{6,10},{7,11},{8,12},{9,13},{1... | collective-permute-start | bytes 835592 | tf_op jit(solution)/shard_map/ppermute | solution.py:184
  4.8 1.5 %collective-permute-start.1 = (bf16[64,2176]{1,0:T(8,128)(2,1)}, bf16[64,2176]{1,0:T(8,128)(2,1)S(1)}, u32[]{:S(2)}, u32[]{:S(2)}) collective-permute-start(bf16[64,2176]{1,0:T(8,128)(2,1)} %shard_map.64.refs_1_), channel_id=1, source_target_pairs={{0,2},{1,3},{2,0},{3,1},{4,6},{5,7},{6,4},{7,5},{8,10},{9,11},{10,... | collective-permute-start | bytes 835592 | tf_op jit(solution)/shard_map/ppermute | solution.py:180
  6.3 2.2 %collective-permute-start.3 = (bf16[64,2176]{1,0:T(8,128)(2,1)}, bf16[64,2176]{1,0:T(8,128)(2,1)S(1)}, u32[]{:S(2)}, u32[]{:S(2)}) collective-permute-start(bf16[64,2176]{1,0:T(8,128)(2,1)} %shard_map.64.refs_1_), channel_id=1, source_target_pairs={{0,12},{1,13},{2,14},{3,15},{4,0},{5,1},{6,2},{7,3},{8,4},{9,5},{1... | collective-permute-start | bytes 835592 | tf_op jit(solution)/shard_map/ppermute | solution.py:184
  8.5 6.0 %collective-permute-done.refs_1_ = bf16[64,2176]{1,0:T(8,128)(2,1)S(1)} collective-permute-done((bf16[64,2176]{1,0:T(8,128)(2,1)}, bf16[64,2176]{1,0:T(8,128)(2,1)S(1)}, u32[]{:S(2)}, u32[]{:S(2)}) %collective-permute-start) | collective-permute-done | bytes 278560 | tf_op jit(solution)/shard_map/ppermute | solution.py:184
  14.5 0.0 collective-permute-done.1.refs_0_
  14.5 1.7 %collective-permute-start.2 = (bf16[64,2176]{1,0:T(8,128)(2,1)S(1)}, bf16[64,2176]{1,0:T(8,128)(2,1)S(1)}, u32[]{:S(2)}, u32[]{:S(2)}) collective-permute-start(bf16[64,2176]{1,0:T(8,128)(2,1)S(1)} %collective-permute-done.refs_1_), channel_id=1, source_target_pairs={{0,2},{1,3},{2,0},{3,1},{4,6},{5,7},{6,4},{7,5},{8,10},{9,11},{10,... | collective-permute-start | bytes 835592 | tf_op jit(solution)/shard_map/ppermute | solution.py:180
  16.3 0.0 collective-permute-start.6
  16.3 0.0 collective-permute-start.5
  16.3 4.1 %collective-permute-done.3.refs_1_ = bf16[64,2176]{1,0:T(8,128)(2,1)S(1)} collective-permute-done((bf16[64,2176]{1,0:T(8,128)(2,1)}, bf16[64,2176]{1,0:T(8,128)(2,1)S(1)}, u32[]{:S(2)}, u32[]{:S(2)}) %collective-permute-start.3) | collective-permute-done | bytes 278560 | tf_op jit(solution)/shard_map/ppermute | solution.py:184
  20.4 1.1 %collective-permute-done.2.refs_0_ = bf16[64,2176]{1,0:T(8,128)(2,1)S(1)} collective-permute-done((bf16[64,2176]{1,0:T(8,128)(2,1)S(1)}, bf16[64,2176]{1,0:T(8,128)(2,1)S(1)}, u32[]{:S(2)}, u32[]{:S(2)}) %collective-permute-start.2) | collective-permute-done | bytes 278560 | tf_op jit(solution)/shard_map/ppermute | solution.py:180
  21.5 0.0 collective-permute-start.4
  21.6 1.3 %collective-permute-start.10 = (bf16[64,2176]{1,0:T(8,128)(2,1)S(1)}, bf16[64,2176]{1,0:T(8,128)(2,1)S(1)}, u32[]{:S(2)}, u32[]{:S(2)}) collective-permute-start(bf16[64,2176]{1,0:T(8,128)(2,1)S(1)} %collective-permute-done.3.refs_1_), channel_id=1, source_target_pairs={{0,2},{1,3},{2,0},{3,1},{4,6},{5,7},{6,4},{7,5},{8,10},{9,11},{10,... | collective-permute-start | bytes 835592 | tf_op jit(solution)/shard_map/ppermute | solution.py:180
  22.8 0.2 collective-permute-start.12
  23.1 3.4 %collective-permute-done.6.refs_1_ = bf16[64,2176]{1,0:T(8,128)(2,1)S(1)} collective-permute-done((bf16[64,2176]{1,0:T(8,128)(2,1)S(1)}, bf16[64,2176]{1,0:T(8,128)(2,1)S(1)}, u32[]{:S(2)}, u32[]{:S(2)}) %collective-permute-start.6) | collective-permute-done | bytes 278560 | tf_op jit(solution)/shard_map/ppermute | solution.py:184
  26.4 3.8 %shard_map.65 = (bf16[1,2048,768]{2,1,0:T(8,128)(2,1)S(1)}, bf16[1,2048,768]{2,1,0:T(8,128)(2,1)S(1)}, bf16[1,768,2048]{2,1,0:T(8,128)(2,1)S(1)}) custom-call(bf16[1,2048,768]{2,1,0:T(8,128)(2,1)} %refs_0_, bf16[1,2048,768]{2,1,0:T(8,128)(2,1)} %refs_1_, bf16[1,768,2048]{2,1,0:T(8,128)(2,1)} %refs_2_), custom_call_target="tpu_custom_call" | custom-call | tf_op jit(solution)/shard_map/pallas_call | solution.py:117
  30.2 0.0 collective-permute-done.5.refs_3_
  30.2 0.0 collective-permute-done.4.refs_2_
  30.2 3.0 %shard_map.66 = (bf16[128,2048]{1,0:T(8,128)(2,1)S(1)}, bf16[128,2048]{1,0:T(8,128)(2,1)S(1)}) custom-call(s32[1]{0:T(128)} %bitcast.own_ref, bf16[64,2176]{1,0:T(8,128)(2,1)S(1)} %collective-permute-done.2.refs_0_, bf16[64,2176]{1,0:T(8,128)(2,1)S(1)} %collective-permute-done.refs_1_, bf16[64,2176]{1,0:T(8,128)(2,1)S(1)} %collective-permute-done.4.refs_2_, ...), custom_call_target="tpu_custom_call" | custom-call | tf_op jit(solution)/shard_map/pallas_call | solution.py:158
  33.2 0.1 collective-permute-start.7
  33.3 0.5 collective-permute-start.11
  33.8 0.1 collective-permute-start.14
  33.9 0.0 collective-permute-done.10.refs_0_
  33.9 0.4 collective-permute-start.13
  34.3 0.0 collective-permute-done.12.refs_3_
  34.3 0.7 collective-permute-start.9
  35.0 0.6 collective-permute-done.11.refs_2_
  35.6 3.0 %shard_map.67 = (bf16[128,2048]{1,0:T(8,128)(2,1)S(1)}, bf16[128,2048]{1,0:T(8,128)(2,1)S(1)}) custom-call(s32[1]{0:T(128)} %bitcast.own_ref, bf16[64,2176]{1,0:T(8,128)(2,1)S(1)} %collective-permute-done.1.refs_0_, bf16[64,2176]{1,0:T(8,128)(2,1)S(1)} %copy-done, bf16[64,2176]{1,0:T(8,128)(2,1)S(1)} %collective-permute-done.11.refs_2_, ...), custom_call_target="tpu_custom_call" | custom-call | tf_op jit(solution)/shard_map/pallas_call | solution.py:158
  38.6 0.2 collective-permute-start.24
  38.7 0.0 collective-permute-done.14.refs_3_
  38.7 0.4 collective-permute-start.16
  39.1 0.0 collective-permute-done.13.refs_2_
  39.1 3.0 %shard_map.68 = (bf16[128,2048]{1,0:T(8,128)(2,1)S(1)}, bf16[128,2048]{1,0:T(8,128)(2,1)S(1)}) custom-call(s32[1]{0:T(128)} %bitcast.own_ref, bf16[64,2176]{1,0:T(8,128)(2,1)S(1)} %collective-permute-done.10.refs_0_, bf16[64,2176]{1,0:T(8,128)(2,1)S(1)} %collective-permute-done.3.refs_1_, bf16[64,2176]{1,0:T(8,128)(2,1)S(1)} %collective-permute-done.13.refs_2_, ...), custom_call_target="tpu_custom_call" | custom-call | tf_op jit(solution)/shard_map/pallas_call | solution.py:158
  42.1 0.8 %collective-permute-done.9.refs_0_ = bf16[64,2176]{1,0:T(8,128)(2,1)S(1)} collective-permute-done((bf16[64,2176]{1,0:T(8,128)(2,1)S(1)}, bf16[64,2176]{1,0:T(8,128)(2,1)S(1)}, u32[]{:S(2)}, u32[]{:S(2)}) %collective-permute-start.9) | collective-permute-done | bytes 278560 | tf_op jit(solution)/shard_map/ppermute | solution.py:180
  42.9 0.0 collective-permute-start.15
  42.9 0.0 collective-permute-done.7
  42.9 0.1 add_convert_fusion.8
  43.0 0.8 collective-permute-start.8
  43.8 0.0 collective-permute-done.16.refs_3_
  43.8 0.7 collective-permute-done.15.refs_2_
  44.5 3.0 %shard_map.69 = (bf16[128,2048]{1,0:T(8,128)(2,1)S(1)}, bf16[128,2048]{1,0:T(8,128)(2,1)S(1)}) custom-call(s32[1]{0:T(128)} %bitcast.own_ref, bf16[64,2176]{1,0:T(8,128)(2,1)S(1)} %collective-permute-done.9.refs_0_, bf16[64,2176]{1,0:T(8,128)(2,1)S(1)} %collective-permute-done.6.refs_1_, bf16[64,2176]{1,0:T(8,128)(2,1)S(1)} %collective-permute-done.15.refs_2_, ...), custom_call_target="tpu_custom_call" | custom-call | tf_op jit(solution)/shard_map/pallas_call | solution.py:158
  47.5 0.2 collective-permute-start.17
  47.7 0.0 collective-permute-done.24
  47.7 0.1 add_convert_fusion.2
  47.7 0.5 collective-permute-start.18
  48.2 3.6 %collective-permute-done.8 = bf16[64,2048]{1,0:T(8,128)(2,1)S(1)} collective-permute-done((bf16[64,2048]{1,0:T(8,128)(2,1)S(1)}, bf16[64,2048]{1,0:T(8,128)(2,1)S(1)}, u32[]{:S(2)}, u32[]{:S(2)}) %collective-permute-start.8) | collective-permute-done | bytes 262176 | tf_op jit(solution)/shard_map/ppermute | solution.py:180
  51.8 0.1 add_convert_fusion.7
  51.9 0.0 collective-permute-done.17
  51.9 0.1 add_convert_fusion.6
  52.0 0.8 collective-permute-start.20
  52.8 0.1 add_convert_fusion.5
  52.8 3.0 %collective-permute-start.19 = (bf16[64,2048]{1,0:T(8,128)(2,1)S(1)}, bf16[64,2048]{1,0:T(8,128)(2,1)S(1)}, u32[]{:S(2)}, u32[]{:S(2)}) collective-permute-start(bf16[64,2048]{1,0:T(8,128)(2,1)S(1)} %add_convert_fusion.7), channel_id=1, source_target_pairs={{0,12},{1,13},{2,14},{3,15},{4,0},{5,1},{6,2},{7,3},{8,4},{9,5},{1... | collective-permute-start | bytes 786440 | tf_op jit(solution)/shard_map/ppermute | solution.py:184
  55.8 0.8 %collective-permute-start.22 = (bf16[64,2048]{1,0:T(8,128)(2,1)S(1)}, bf16[64,2048]{1,0:T(8,128)(2,1)S(1)}, u32[]{:S(2)}, u32[]{:S(2)}) collective-permute-start(bf16[64,2048]{1,0:T(8,128)(2,1)S(1)} %add_convert_fusion.5), channel_id=1, source_target_pairs={{0,2},{1,3},{2,0},{3,1},{4,6},{5,7},{6,4},{7,5},{8,10},{9,11},{10,... | collective-permute-start | bytes 786440 | tf_op jit(solution)/shard_map/ppermute | solution.py:180
  56.7 4.6 %collective-permute-done.20 = bf16[64,2048]{1,0:T(8,128)(2,1)S(1)} collective-permute-done((bf16[64,2048]{1,0:T(8,128)(2,1)S(1)}, bf16[64,2048]{1,0:T(8,128)(2,1)S(1)}, u32[]{:S(2)}, u32[]{:S(2)}) %collective-permute-start.20) | collective-permute-done | bytes 262176 | tf_op jit(solution)/shard_map/ppermute | solution.py:180
  61.3 0.1 add_convert_fusion.4
  61.4 0.8 collective-permute-start.25
  62.1 1.8 %collective-permute-start.21 = (bf16[64,2048]{1,0:T(8,128)(2,1)S(1)}, bf16[64,2048]{1,0:T(8,128)(2,1)S(1)}, u32[]{:S(2)}, u32[]{:S(2)}) collective-permute-start(bf16[64,2048]{1,0:T(8,128)(2,1)S(1)} %add_convert_fusion.4), channel_id=1, source_target_pairs={{0,8},{1,9},{2,10},{3,11},{4,12},{5,13},{6,14},{7,15},{8,0},{9,1},... | collective-permute-start | bytes 786440 | tf_op jit(solution)/shard_map/ppermute | solution.py:184
  63.9 2.9 %collective-permute-done.22 = bf16[64,2048]{1,0:T(8,128)(2,1)S(1)} collective-permute-done((bf16[64,2048]{1,0:T(8,128)(2,1)S(1)}, bf16[64,2048]{1,0:T(8,128)(2,1)S(1)}, u32[]{:S(2)}, u32[]{:S(2)}) %collective-permute-start.22) | collective-permute-done | bytes 262176 | tf_op jit(solution)/shard_map/ppermute | solution.py:180
  66.9 0.1 add_convert_fusion.3
  67.0 0.1 collective-permute-start.23
  67.0 0.0 collective-permute-done.19
  67.1 4.2 %collective-permute-done.25 = bf16[64,2048]{1,0:T(8,128)(2,1)S(1)} collective-permute-done((bf16[64,2048]{1,0:T(8,128)(2,1)S(1)}, bf16[64,2048]{1,0:T(8,128)(2,1)S(1)}, u32[]{:S(2)}, u32[]{:S(2)}) %collective-permute-start.25) | collective-permute-done | bytes 262176 | tf_op jit(solution)/shard_map/ppermute | solution.py:180
  71.2 8.5 %collective-permute-done.21 = bf16[64,2048]{1,0:T(8,128)(2,1)S(1)} collective-permute-done((bf16[64,2048]{1,0:T(8,128)(2,1)S(1)}, bf16[64,2048]{1,0:T(8,128)(2,1)S(1)}, u32[]{:S(2)}, u32[]{:S(2)}) %collective-permute-start.21) | collective-permute-done | bytes 262176 | tf_op jit(solution)/shard_map/ppermute | solution.py:184
  79.8 0.9 %add_convert_fusion = bf16[64,2048]{1,0:T(8,128)(2,1)} fusion(bf16[64,2048]{1,0:T(8,128)(2,1)S(1)} %collective-permute-done.23, bf16[64,2048]{1,0:T(8,128)(2,1)S(1)} %collective-permute-done.21, bf16[64,2048]{1,0:T(8,128)(2,1)S(1)} %collective-permute-done.19, bf16[64,2048]{1,0:T(8,128)(2,1)S(1)} %collective-permute-done.25, ...), kind=kLoop, calls=%fused_computation | loop fusion | flops 1835008 | bytes 1835008 | tf_op jit(solution)/shard_map/convert_element_type | solution.py:229
  (4 shorter events, 0.0 us)
Async XLA Ops:
  1.7 12.8 %collective-permute-start = (bf16[64,2176]{1,0:T(8,128)(2,1)}, bf16[64,2176]{1,0:T(8,128)(2,1)S(1)}, u32[]{:S(2)}, u32[]{:S(2)}) collective-permute-start(bf16[64,2176]{1,0:T(8,128)(2,1)} %shard_map.64.refs_1_), channel_id=1, source_target_pairs={{0,4},{1,5},{2,6},{3,7},{4,8},{5,9},{6,10},{7,11},{8,12},{9,13},{1... | collective-permute-start | bytes 835592 | tf_op jit(solution)/shard_map/ppermute | solution.py:184
  4.8 9.8 %collective-permute-start.1 = (bf16[64,2176]{1,0:T(8,128)(2,1)}, bf16[64,2176]{1,0:T(8,128)(2,1)S(1)}, u32[]{:S(2)}, u32[]{:S(2)}) collective-permute-start(bf16[64,2176]{1,0:T(8,128)(2,1)} %shard_map.64.refs_1_), channel_id=1, source_target_pairs={{0,2},{1,3},{2,0},{3,1},{4,6},{5,7},{6,4},{7,5},{8,10},{9,11},{10,... | collective-permute-start | bytes 835592 | tf_op jit(solution)/shard_map/ppermute | solution.py:180
  6.3 14.2 %collective-permute-start.3 = (bf16[64,2176]{1,0:T(8,128)(2,1)}, bf16[64,2176]{1,0:T(8,128)(2,1)S(1)}, u32[]{:S(2)}, u32[]{:S(2)}) collective-permute-start(bf16[64,2176]{1,0:T(8,128)(2,1)} %shard_map.64.refs_1_), channel_id=1, source_target_pairs={{0,12},{1,13},{2,14},{3,15},{4,0},{5,1},{6,2},{7,3},{8,4},{9,5},{1... | collective-permute-start | bytes 835592 | tf_op jit(solution)/shard_map/ppermute | solution.py:184
  14.5 7.0 %collective-permute-start.2 = (bf16[64,2176]{1,0:T(8,128)(2,1)S(1)}, bf16[64,2176]{1,0:T(8,128)(2,1)S(1)}, u32[]{:S(2)}, u32[]{:S(2)}) collective-permute-start(bf16[64,2176]{1,0:T(8,128)(2,1)S(1)} %collective-permute-done.refs_1_), channel_id=1, source_target_pairs={{0,2},{1,3},{2,0},{3,1},{4,6},{5,7},{6,4},{7,5},{8,10},{9,11},{10,... | collective-permute-start | bytes 835592 | tf_op jit(solution)/shard_map/ppermute | solution.py:180
  16.3 10.1 %collective-permute-start.6 = (bf16[64,2176]{1,0:T(8,128)(2,1)S(1)}, bf16[64,2176]{1,0:T(8,128)(2,1)S(1)}, u32[]{:S(2)}, u32[]{:S(2)}) collective-permute-start(bf16[64,2176]{1,0:T(8,128)(2,1)S(1)} %collective-permute-done.refs_1_), channel_id=1, source_target_pairs={{0,4},{1,5},{2,6},{3,7},{4,8},{5,9},{6,10},{7,11},{8,12},{9,13},{1... | collective-permute-start | bytes 835592 | tf_op jit(solution)/shard_map/ppermute | solution.py:184
  16.3 13.9 %collective-permute-start.5 = (bf16[64,2176]{1,0:T(8,128)(2,1)S(1)}, bf16[64,2176]{1,0:T(8,128)(2,1)S(1)}, u32[]{:S(2)}, u32[]{:S(2)}) collective-permute-start(bf16[64,2176]{1,0:T(8,128)(2,1)S(1)} %collective-permute-done.refs_1_), channel_id=1, source_target_pairs={{0,1},{1,0},{2,3},{3,2},{4,5},{5,4},{6,7},{7,6},{8,9},{9,8},{10,11... | collective-permute-start | bytes 835592 | tf_op jit(solution)/shard_map/ppermute | solution.py:177
  21.5 8.7 %collective-permute-start.4 = (bf16[64,2176]{1,0:T(8,128)(2,1)S(1)}, bf16[64,2176]{1,0:T(8,128)(2,1)S(1)}, u32[]{:S(2)}, u32[]{:S(2)}) collective-permute-start(bf16[64,2176]{1,0:T(8,128)(2,1)S(1)} %collective-permute-done.2.refs_0_), channel_id=1, source_target_pairs={{0,1},{1,0},{2,3},{3,2},{4,5},{5,4},{6,7},{7,6},{8,9},{9,8},{10,11... | collective-permute-start | bytes 835592 | tf_op jit(solution)/shard_map/ppermute | solution.py:177
  21.6 12.3 %collective-permute-start.10 = (bf16[64,2176]{1,0:T(8,128)(2,1)S(1)}, bf16[64,2176]{1,0:T(8,128)(2,1)S(1)}, u32[]{:S(2)}, u32[]{:S(2)}) collective-permute-start(bf16[64,2176]{1,0:T(8,128)(2,1)S(1)} %collective-permute-done.3.refs_1_), channel_id=1, source_target_pairs={{0,2},{1,3},{2,0},{3,1},{4,6},{5,7},{6,4},{7,5},{8,10},{9,11},{10,... | collective-permute-start | bytes 835592 | tf_op jit(solution)/shard_map/ppermute | solution.py:180
  22.8 11.5 %collective-permute-start.12 = (bf16[64,2176]{1,0:T(8,128)(2,1)}, bf16[64,2176]{1,0:T(8,128)(2,1)S(1)}, u32[]{:S(2)}, u32[]{:S(2)}) collective-permute-start(bf16[64,2176]{1,0:T(8,128)(2,1)} %shard_map.64.refs_1_), channel_id=1, source_target_pairs={{0,1},{1,0},{2,3},{3,2},{4,5},{5,4},{6,7},{7,6},{8,9},{9,8},{10,11... | collective-permute-start | bytes 835592 | tf_op jit(solution)/shard_map/ppermute | solution.py:177
  30.2 5.3 %copy-start = (bf16[64,2176]{1,0:T(8,128)(2,1)S(1)}, bf16[64,2176]{1,0:T(8,128)(2,1)}, u32[]{:S(2)}) copy-start(bf16[64,2176]{1,0:T(8,128)(2,1)} %shard_map.64.refs_1_) | copy-start | bytes 835588
  33.2 9.7 %collective-permute-start.7 = (bf16[128,2048]{1,0:T(8,128)(2,1)S(1)}, bf16[128,2048]{1,0:T(8,128)(2,1)S(1)}, u32[]{:S(2)}, u32[]{:S(2)}) collective-permute-start(bf16[128,2048]{1,0:T(8,128)(2,1)S(1)} %get-tuple-element.40), channel_id=1, source_target_pairs={{0,1},{1,0},{2,3},{3,2},{4,5},{5,4},{6,7},{7,6},{8,9},{9,8},{10,11... | collective-permute-start | bytes 1572872 | tf_op jit(solution)/shard_map/ppermute | solution.py:177
  33.3 2.3 %collective-permute-start.11 = (bf16[64,2176]{1,0:T(8,128)(2,1)S(1)}, bf16[64,2176]{1,0:T(8,128)(2,1)S(1)}, u32[]{:S(2)}, u32[]{:S(2)}) collective-permute-start(bf16[64,2176]{1,0:T(8,128)(2,1)S(1)} %collective-permute-done.1.refs_0_), channel_id=1, source_target_pairs={{0,1},{1,0},{2,3},{3,2},{4,5},{5,4},{6,7},{7,6},{8,9},{9,8},{10,11... | collective-permute-start | bytes 835592 | tf_op jit(solution)/shard_map/ppermute | solution.py:177
  33.8 5.0 %collective-permute-start.14 = (bf16[64,2176]{1,0:T(8,128)(2,1)S(1)}, bf16[64,2176]{1,0:T(8,128)(2,1)S(1)}, u32[]{:S(2)}, u32[]{:S(2)}) collective-permute-start(bf16[64,2176]{1,0:T(8,128)(2,1)S(1)} %collective-permute-done.3.refs_1_), channel_id=1, source_target_pairs={{0,1},{1,0},{2,3},{3,2},{4,5},{5,4},{6,7},{7,6},{8,9},{9,8},{10,11... | collective-permute-start | bytes 835592 | tf_op jit(solution)/shard_map/ppermute | solution.py:177
  33.9 5.3 %collective-permute-start.13 = (bf16[64,2176]{1,0:T(8,128)(2,1)S(1)}, bf16[64,2176]{1,0:T(8,128)(2,1)S(1)}, u32[]{:S(2)}, u32[]{:S(2)}) collective-permute-start(bf16[64,2176]{1,0:T(8,128)(2,1)S(1)} %collective-permute-done.10.refs_0_), channel_id=1, source_target_pairs={{0,1},{1,0},{2,3},{3,2},{4,5},{5,4},{6,7},{7,6},{8,9},{9,8},{10,11... | collective-permute-start | bytes 835592 | tf_op jit(solution)/shard_map/ppermute | solution.py:177
  34.3 8.6 %collective-permute-start.9 = (bf16[64,2176]{1,0:T(8,128)(2,1)S(1)}, bf16[64,2176]{1,0:T(8,128)(2,1)S(1)}, u32[]{:S(2)}, u32[]{:S(2)}) collective-permute-start(bf16[64,2176]{1,0:T(8,128)(2,1)S(1)} %collective-permute-done.6.refs_1_), channel_id=1, source_target_pairs={{0,2},{1,3},{2,0},{3,1},{4,6},{5,7},{6,4},{7,5},{8,10},{9,11},{10,... | collective-permute-start | bytes 835592 | tf_op jit(solution)/shard_map/ppermute | solution.py:180
  38.6 9.1 %collective-permute-start.24 = (bf16[128,2048]{1,0:T(8,128)(2,1)S(1)}, bf16[128,2048]{1,0:T(8,128)(2,1)S(1)}, u32[]{:S(2)}, u32[]{:S(2)}) collective-permute-start(bf16[128,2048]{1,0:T(8,128)(2,1)S(1)} %get-tuple-element.45), channel_id=1, source_target_pairs={{0,1},{1,0},{2,3},{3,2},{4,5},{5,4},{6,7},{7,6},{8,9},{9,8},{10,11... | collective-permute-start | bytes 1572872 | tf_op jit(solution)/shard_map/ppermute | solution.py:177
  38.7 5.0 %collective-permute-start.16 = (bf16[64,2176]{1,0:T(8,128)(2,1)S(1)}, bf16[64,2176]{1,0:T(8,128)(2,1)S(1)}, u32[]{:S(2)}, u32[]{:S(2)}) collective-permute-start(bf16[64,2176]{1,0:T(8,128)(2,1)S(1)} %collective-permute-done.6.refs_1_), channel_id=1, source_target_pairs={{0,1},{1,0},{2,3},{3,2},{4,5},{5,4},{6,7},{7,6},{8,9},{9,8},{10,11... | collective-permute-start | bytes 835592 | tf_op jit(solution)/shard_map/ppermute | solution.py:177
  42.9 1.6 %collective-permute-start.15 = (bf16[64,2176]{1,0:T(8,128)(2,1)S(1)}, bf16[64,2176]{1,0:T(8,128)(2,1)S(1)}, u32[]{:S(2)}, u32[]{:S(2)}) collective-permute-start(bf16[64,2176]{1,0:T(8,128)(2,1)S(1)} %collective-permute-done.9.refs_0_), channel_id=1, source_target_pairs={{0,1},{1,0},{2,3},{3,2},{4,5},{5,4},{6,7},{7,6},{8,9},{9,8},{10,11... | collective-permute-start | bytes 835592 | tf_op jit(solution)/shard_map/ppermute | solution.py:177
  43.0 8.8 %collective-permute-start.8 = (bf16[64,2048]{1,0:T(8,128)(2,1)S(1)}, bf16[64,2048]{1,0:T(8,128)(2,1)S(1)}, u32[]{:S(2)}, u32[]{:S(2)}) collective-permute-start(bf16[64,2048]{1,0:T(8,128)(2,1)S(1)} %add_convert_fusion.8), channel_id=1, source_target_pairs={{0,2},{1,3},{2,0},{3,1},{4,6},{5,7},{6,4},{7,5},{8,10},{9,11},{10,... | collective-permute-start | bytes 786440 | tf_op jit(solution)/shard_map/ppermute | solution.py:180
  47.5 4.4 %collective-permute-start.17 = (bf16[128,2048]{1,0:T(8,128)(2,1)S(1)}, bf16[128,2048]{1,0:T(8,128)(2,1)S(1)}, u32[]{:S(2)}, u32[]{:S(2)}) collective-permute-start(bf16[128,2048]{1,0:T(8,128)(2,1)S(1)} %get-tuple-element.51), channel_id=1, source_target_pairs={{0,1},{1,0},{2,3},{3,2},{4,5},{5,4},{6,7},{7,6},{8,9},{9,8},{10,11... | collective-permute-start | bytes 1572872 | tf_op jit(solution)/shard_map/ppermute | solution.py:177
  47.7 5.0 %collective-permute-start.18 = (bf16[128,2048]{1,0:T(8,128)(2,1)S(1)}, bf16[128,2048]{1,0:T(8,128)(2,1)S(1)}, u32[]{:S(2)}, u32[]{:S(2)}) collective-permute-start(bf16[128,2048]{1,0:T(8,128)(2,1)S(1)} %get-tuple-element.48), channel_id=1, source_target_pairs={{0,1},{1,0},{2,3},{3,2},{4,5},{5,4},{6,7},{7,6},{8,9},{9,8},{10,11... | collective-permute-start | bytes 1572872 | tf_op jit(solution)/shard_map/ppermute | solution.py:177
  52.0 9.3 %collective-permute-start.20 = (bf16[64,2048]{1,0:T(8,128)(2,1)S(1)}, bf16[64,2048]{1,0:T(8,128)(2,1)S(1)}, u32[]{:S(2)}, u32[]{:S(2)}) collective-permute-start(bf16[64,2048]{1,0:T(8,128)(2,1)S(1)} %add_convert_fusion.6), channel_id=1, source_target_pairs={{0,2},{1,3},{2,0},{3,1},{4,6},{5,7},{6,4},{7,5},{8,10},{9,11},{10,... | collective-permute-start | bytes 786440 | tf_op jit(solution)/shard_map/ppermute | solution.py:180
  52.8 14.2 %collective-permute-start.19 = (bf16[64,2048]{1,0:T(8,128)(2,1)S(1)}, bf16[64,2048]{1,0:T(8,128)(2,1)S(1)}, u32[]{:S(2)}, u32[]{:S(2)}) collective-permute-start(bf16[64,2048]{1,0:T(8,128)(2,1)S(1)} %add_convert_fusion.7), channel_id=1, source_target_pairs={{0,12},{1,13},{2,14},{3,15},{4,0},{5,1},{6,2},{7,3},{8,4},{9,5},{1... | collective-permute-start | bytes 786440 | tf_op jit(solution)/shard_map/ppermute | solution.py:184
  55.8 11.0 %collective-permute-start.22 = (bf16[64,2048]{1,0:T(8,128)(2,1)S(1)}, bf16[64,2048]{1,0:T(8,128)(2,1)S(1)}, u32[]{:S(2)}, u32[]{:S(2)}) collective-permute-start(bf16[64,2048]{1,0:T(8,128)(2,1)S(1)} %add_convert_fusion.5), channel_id=1, source_target_pairs={{0,2},{1,3},{2,0},{3,1},{4,6},{5,7},{6,4},{7,5},{8,10},{9,11},{10,... | collective-permute-start | bytes 786440 | tf_op jit(solution)/shard_map/ppermute | solution.py:180
  61.4 9.9 %collective-permute-start.25 = (bf16[64,2048]{1,0:T(8,128)(2,1)S(1)}, bf16[64,2048]{1,0:T(8,128)(2,1)S(1)}, u32[]{:S(2)}, u32[]{:S(2)}) collective-permute-start(bf16[64,2048]{1,0:T(8,128)(2,1)S(1)} %add_convert_fusion.2), channel_id=1, source_target_pairs={{0,2},{1,3},{2,0},{3,1},{4,6},{5,7},{6,4},{7,5},{8,10},{9,11},{10,... | collective-permute-start | bytes 786440 | tf_op jit(solution)/shard_map/ppermute | solution.py:180
  62.1 17.6 %collective-permute-start.21 = (bf16[64,2048]{1,0:T(8,128)(2,1)S(1)}, bf16[64,2048]{1,0:T(8,128)(2,1)S(1)}, u32[]{:S(2)}, u32[]{:S(2)}) collective-permute-start(bf16[64,2048]{1,0:T(8,128)(2,1)S(1)} %add_convert_fusion.4), channel_id=1, source_target_pairs={{0,8},{1,9},{2,10},{3,11},{4,12},{5,13},{6,14},{7,15},{8,0},{9,1},... | collective-permute-start | bytes 786440 | tf_op jit(solution)/shard_map/ppermute | solution.py:184
  67.0 12.8 %collective-permute-start.23 = (bf16[64,2048]{1,0:T(8,128)(2,1)S(1)}, bf16[64,2048]{1,0:T(8,128)(2,1)S(1)}, u32[]{:S(2)}, u32[]{:S(2)}) collective-permute-start(bf16[64,2048]{1,0:T(8,128)(2,1)S(1)} %add_convert_fusion.3), channel_id=1, source_target_pairs={{0,4},{1,5},{2,6},{3,7},{4,8},{5,9},{6,10},{7,11},{8,12},{9,13},{1... | collective-permute-start | bytes 786440 | tf_op jit(solution)/shard_map/ppermute | solution.py:184

commit v5 on v4

--- a/solution.py
+++ b/solution.py
@@ -129,7 +129,7 @@
     blocks, (gate_ref, up_ref, down_ref) = refs[:PLANE], refs[PLANE : PLANE + 3]
     outs, total_ref = refs[PLANE + 3 : PLANE + 5], refs[PLANE + 5]
     rows, (width, hidden_width) = blocks[0].shape[0], gate_ref.shape[1:]
-    tile = 256
+    tile = hidden_width
     tokens = jnp.concatenate([block[:, :width] for block in blocks], axis=0)
     for start in range(0, hidden_width, tile):
         columns = slice(start, start + tile)

time: 80.9 us -> 80.5 us (level)
  Pallas kernels: 17.3 us -> 16 us
    pallas_call x4, Pallas kernels: 11.8 us -> 10.5 us  [expert_rows(): pl.pallas_call(expert_kernel, in_specs=[pl.BlockSpec(memory_space=pltpu.S...]
  transfers between devices with their start and end apart: 26 -> 26, of which waited for: 12 -> 12; matrix products, arithmetic and copies ran while one was open for 1% -> 1% of each run, Pallas kernels for 19% -> 18%
where the time goes in v5:
time: 80.5 us; the launch traced here: 80.4 us
  waiting for transfers between devices  41.3 us (51%)
  starting transfers between devices  21.4 us (27%)
  Pallas kernels  16 us (20%)
  other arithmetic  1.49 us (2%)
    ppermute x6, waiting for transfers between devices, turn(): return lax.ppermute(block, 'expert', pairs)  22.1 us
    ppermute x8, waiting for transfers between devices, side(): return lax.ppermute(block, 'expert', side_pairs)  17.9 us
    ppermute x6, starting transfers between devices, turn(): return lax.ppermute(block, 'expert', pairs)  10.8 us
    pallas_call x4, Pallas kernels, expert_rows(): pl.pallas_call(expert_kernel, in_specs=[pl.BlockSpec(memory_space=pltpu.S...  10.5 us
    ppermute x8, starting transfers between devices, side(): return lax.ppermute(block, 'expert', side_pairs)  8.07 us
    pallas_call x1, Pallas kernels, load(): pl.pallas_call(load_kernel, in_specs=[pl.BlockSpec(memory_space=pltpu.HBM...  3.78 us
    ppermute x12, starting transfers between devices, core(): return lax.ppermute(block, 'expert', core_pairs)  2.53 us
    pallas_call x1, Pallas kernels, pack(): pl.pallas_call(pack_kernel, in_specs=[pl.BlockSpec(memory_space=pltpu.HBM...  1.68 us
  transfers between devices with their start and end apart: 26, of which 12 were waited for; matrix products, arithmetic and copies ran while one was open for 1% of the time, Pallas kernels for 18%

profile of v5, /device:TPU:0, one launch (start us, length us, event | category | flops | bytes accessed | tf_op | source)
XLA Modules:
  0.0 80.4 jit_solution(4047278740295209261)
XLA Ops:
  0.0 1.7 %shard_map.64.refs_1_ = bf16[64,2176]{1,0:T(8,128)(2,1)} custom-call(bf16[64,2048]{1,0:T(8,128)(2,1)} %tokens_hbm.1, s32[8,64]{1,0:T(8,128)} %bitcast.3, s32[8,64]{1,0:T(8,128)} %bitcast.4), custom_call_target="tpu_custom_call" | custom-call | bytes 524288 | tf_op jit(solution)/shard_map/pallas_call | solution.py:88
  1.7 3.1 %collective-permute-start = (bf16[64,2176]{1,0:T(8,128)(2,1)}, bf16[64,2176]{1,0:T(8,128)(2,1)S(1)}, u32[]{:S(2)}, u32[]{:S(2)}) collective-permute-start(bf16[64,2176]{1,0:T(8,128)(2,1)} %shard_map.64.refs_1_), channel_id=1, source_target_pairs={{0,4},{1,5},{2,6},{3,7},{4,8},{5,9},{6,10},{7,11},{8,12},{9,13},{1... | collective-permute-start | bytes 835592 | tf_op jit(solution)/shard_map/ppermute | solution.py:184
  4.8 1.5 %collective-permute-start.1 = (bf16[64,2176]{1,0:T(8,128)(2,1)}, bf16[64,2176]{1,0:T(8,128)(2,1)S(1)}, u32[]{:S(2)}, u32[]{:S(2)}) collective-permute-start(bf16[64,2176]{1,0:T(8,128)(2,1)} %shard_map.64.refs_1_), channel_id=1, source_target_pairs={{0,2},{1,3},{2,0},{3,1},{4,6},{5,7},{6,4},{7,5},{8,10},{9,11},{10,... | collective-permute-start | bytes 835592 | tf_op jit(solution)/shard_map/ppermute | solution.py:180
  6.3 2.2 %collective-permute-start.3 = (bf16[64,2176]{1,0:T(8,128)(2,1)}, bf16[64,2176]{1,0:T(8,128)(2,1)S(1)}, u32[]{:S(2)}, u32[]{:S(2)}) collective-permute-start(bf16[64,2176]{1,0:T(8,128)(2,1)} %shard_map.64.refs_1_), channel_id=1, source_target_pairs={{0,12},{1,13},{2,14},{3,15},{4,0},{5,1},{6,2},{7,3},{8,4},{9,5},{1... | collective-permute-start | bytes 835592 | tf_op jit(solution)/shard_map/ppermute | solution.py:184
  8.5 6.0 %collective-permute-done.refs_1_ = bf16[64,2176]{1,0:T(8,128)(2,1)S(1)} collective-permute-done((bf16[64,2176]{1,0:T(8,128)(2,1)}, bf16[64,2176]{1,0:T(8,128)(2,1)S(1)}, u32[]{:S(2)}, u32[]{:S(2)}) %collective-permute-start) | collective-permute-done | bytes 278560 | tf_op jit(solution)/shard_map/ppermute | solution.py:184
  14.5 0.0 collective-permute-done.1.refs_0_
  14.5 1.7 %collective-permute-start.2 = (bf16[64,2176]{1,0:T(8,128)(2,1)S(1)}, bf16[64,2176]{1,0:T(8,128)(2,1)S(1)}, u32[]{:S(2)}, u32[]{:S(2)}) collective-permute-start(bf16[64,2176]{1,0:T(8,128)(2,1)S(1)} %collective-permute-done.refs_1_), channel_id=1, source_target_pairs={{0,2},{1,3},{2,0},{3,1},{4,6},{5,7},{6,4},{7,5},{8,10},{9,11},{10,... | collective-permute-start | bytes 835592 | tf_op jit(solution)/shard_map/ppermute | solution.py:180
  16.3 0.0 collective-permute-start.6
  16.3 0.0 collective-permute-start.5
  16.3 4.1 %collective-permute-done.3.refs_1_ = bf16[64,2176]{1,0:T(8,128)(2,1)S(1)} collective-permute-done((bf16[64,2176]{1,0:T(8,128)(2,1)}, bf16[64,2176]{1,0:T(8,128)(2,1)S(1)}, u32[]{:S(2)}, u32[]{:S(2)}) %collective-permute-start.3) | collective-permute-done | bytes 278560 | tf_op jit(solution)/shard_map/ppermute | solution.py:184
  20.4 1.1 %collective-permute-done.2.refs_0_ = bf16[64,2176]{1,0:T(8,128)(2,1)S(1)} collective-permute-done((bf16[64,2176]{1,0:T(8,128)(2,1)S(1)}, bf16[64,2176]{1,0:T(8,128)(2,1)S(1)}, u32[]{:S(2)}, u32[]{:S(2)}) %collective-permute-start.2) | collective-permute-done | bytes 278560 | tf_op jit(solution)/shard_map/ppermute | solution.py:180
  21.5 0.0 collective-permute-start.4
  21.6 1.3 %collective-permute-start.10 = (bf16[64,2176]{1,0:T(8,128)(2,1)S(1)}, bf16[64,2176]{1,0:T(8,128)(2,1)S(1)}, u32[]{:S(2)}, u32[]{:S(2)}) collective-permute-start(bf16[64,2176]{1,0:T(8,128)(2,1)S(1)} %collective-permute-done.3.refs_1_), channel_id=1, source_target_pairs={{0,2},{1,3},{2,0},{3,1},{4,6},{5,7},{6,4},{7,5},{8,10},{9,11},{10,... | collective-permute-start | bytes 835592 | tf_op jit(solution)/shard_map/ppermute | solution.py:180
  22.8 0.2 collective-permute-start.12
  23.1 3.4 %collective-permute-done.6.refs_1_ = bf16[64,2176]{1,0:T(8,128)(2,1)S(1)} collective-permute-done((bf16[64,2176]{1,0:T(8,128)(2,1)S(1)}, bf16[64,2176]{1,0:T(8,128)(2,1)S(1)}, u32[]{:S(2)}, u32[]{:S(2)}) %collective-permute-start.6) | collective-permute-done | bytes 278560 | tf_op jit(solution)/shard_map/ppermute | solution.py:184
  26.4 3.8 %shard_map.65 = (bf16[1,2048,768]{2,1,0:T(8,128)(2,1)S(1)}, bf16[1,2048,768]{2,1,0:T(8,128)(2,1)S(1)}, bf16[1,768,2048]{2,1,0:T(8,128)(2,1)S(1)}) custom-call(bf16[1,2048,768]{2,1,0:T(8,128)(2,1)} %refs_0_, bf16[1,2048,768]{2,1,0:T(8,128)(2,1)} %refs_1_, bf16[1,768,2048]{2,1,0:T(8,128)(2,1)} %refs_2_), custom_call_target="tpu_custom_call" | custom-call | tf_op jit(solution)/shard_map/pallas_call | solution.py:117
  30.2 0.0 collective-permute-done.5.refs_3_
  30.2 0.0 collective-permute-done.4.refs_2_
  30.2 2.6 %shard_map.66 = (bf16[128,2048]{1,0:T(8,128)(2,1)S(1)}, bf16[128,2048]{1,0:T(8,128)(2,1)S(1)}) custom-call(s32[1]{0:T(128)} %bitcast.own_ref, bf16[64,2176]{1,0:T(8,128)(2,1)S(1)} %collective-permute-done.2.refs_0_, bf16[64,2176]{1,0:T(8,128)(2,1)S(1)} %collective-permute-done.refs_1_, bf16[64,2176]{1,0:T(8,128)(2,1)S(1)} %collective-permute-done.4.refs_2_, ...), custom_call_target="tpu_custom_call" | custom-call | tf_op jit(solution)/shard_map/pallas_call | solution.py:158
  32.9 0.1 collective-permute-start.7
  33.0 0.5 collective-permute-start.11
  33.5 0.1 collective-permute-start.14
  33.5 0.0 collective-permute-done.10.refs_0_
  33.5 0.4 collective-permute-start.13
  34.0 0.0 collective-permute-done.12.refs_3_
  34.0 0.7 collective-permute-start.9
  34.7 0.6 collective-permute-done.11.refs_2_
  35.3 2.6 %shard_map.67 = (bf16[128,2048]{1,0:T(8,128)(2,1)S(1)}, bf16[128,2048]{1,0:T(8,128)(2,1)S(1)}) custom-call(s32[1]{0:T(128)} %bitcast.own_ref, bf16[64,2176]{1,0:T(8,128)(2,1)S(1)} %collective-permute-done.1.refs_0_, bf16[64,2176]{1,0:T(8,128)(2,1)S(1)} %copy-done, bf16[64,2176]{1,0:T(8,128)(2,1)S(1)} %collective-permute-done.11.refs_2_, ...), custom_call_target="tpu_custom_call" | custom-call | tf_op jit(solution)/shard_map/pallas_call | solution.py:158
  37.9 0.2 collective-permute-start.24
  38.1 0.0 collective-permute-done.14.refs_3_
  38.1 0.4 collective-permute-start.16
  38.5 0.0 collective-permute-done.13.refs_2_
  38.5 2.6 %shard_map.68 = (bf16[128,2048]{1,0:T(8,128)(2,1)S(1)}, bf16[128,2048]{1,0:T(8,128)(2,1)S(1)}) custom-call(s32[1]{0:T(128)} %bitcast.own_ref, bf16[64,2176]{1,0:T(8,128)(2,1)S(1)} %collective-permute-done.10.refs_0_, bf16[64,2176]{1,0:T(8,128)(2,1)S(1)} %collective-permute-done.3.refs_1_, bf16[64,2176]{1,0:T(8,128)(2,1)S(1)} %collective-permute-done.13.refs_2_, ...), custom_call_target="tpu_custom_call" | custom-call | tf_op jit(solution)/shard_map/pallas_call | solution.py:158
  41.1 1.5 %collective-permute-done.9.refs_0_ = bf16[64,2176]{1,0:T(8,128)(2,1)S(1)} collective-permute-done((bf16[64,2176]{1,0:T(8,128)(2,1)S(1)}, bf16[64,2176]{1,0:T(8,128)(2,1)S(1)}, u32[]{:S(2)}, u32[]{:S(2)}) %collective-permute-start.9) | collective-permute-done | bytes 278560 | tf_op jit(solution)/shard_map/ppermute | solution.py:180
  42.6 0.0 collective-permute-start.15
  42.6 0.0 collective-permute-done.7
  42.6 0.1 add_convert_fusion.8
  42.7 0.8 collective-permute-start.8
  43.5 0.0 collective-permute-done.16.refs_3_
  43.5 0.7 collective-permute-done.15.refs_2_
  44.2 2.6 %shard_map.69 = (bf16[128,2048]{1,0:T(8,128)(2,1)S(1)}, bf16[128,2048]{1,0:T(8,128)(2,1)S(1)}) custom-call(s32[1]{0:T(128)} %bitcast.own_ref, bf16[64,2176]{1,0:T(8,128)(2,1)S(1)} %collective-permute-done.9.refs_0_, bf16[64,2176]{1,0:T(8,128)(2,1)S(1)} %collective-permute-done.6.refs_1_, bf16[64,2176]{1,0:T(8,128)(2,1)S(1)} %collective-permute-done.15.refs_2_, ...), custom_call_target="tpu_custom_call" | custom-call | tf_op jit(solution)/shard_map/pallas_call | solution.py:158
  46.8 0.2 collective-permute-start.17
  47.0 0.0 collective-permute-done.24
  47.0 0.1 add_convert_fusion.2
  47.1 0.4 collective-permute-start.18
  47.5 4.0 %collective-permute-done.8 = bf16[64,2048]{1,0:T(8,128)(2,1)S(1)} collective-permute-done((bf16[64,2048]{1,0:T(8,128)(2,1)S(1)}, bf16[64,2048]{1,0:T(8,128)(2,1)S(1)}, u32[]{:S(2)}, u32[]{:S(2)}) %collective-permute-start.8) | collective-permute-done | bytes 262176 | tf_op jit(solution)/shard_map/ppermute | solution.py:180
  51.5 0.1 add_convert_fusion.7
  51.6 0.0 collective-permute-done.17
  51.6 0.1 add_convert_fusion.6
  51.7 0.8 collective-permute-start.20
  52.4 0.1 add_convert_fusion.5
  52.5 3.3 %collective-permute-start.19 = (bf16[64,2048]{1,0:T(8,128)(2,1)S(1)}, bf16[64,2048]{1,0:T(8,128)(2,1)S(1)}, u32[]{:S(2)}, u32[]{:S(2)}) collective-permute-start(bf16[64,2048]{1,0:T(8,128)(2,1)S(1)} %add_convert_fusion.7), channel_id=1, source_target_pairs={{0,12},{1,13},{2,14},{3,15},{4,0},{5,1},{6,2},{7,3},{8,4},{9,5},{1... | collective-permute-start | bytes 786440 | tf_op jit(solution)/shard_map/ppermute | solution.py:184
  55.8 0.5 collective-permute-start.22
  56.4 4.6 %collective-permute-done.20 = bf16[64,2048]{1,0:T(8,128)(2,1)S(1)} collective-permute-done((bf16[64,2048]{1,0:T(8,128)(2,1)S(1)}, bf16[64,2048]{1,0:T(8,128)(2,1)S(1)}, u32[]{:S(2)}, u32[]{:S(2)}) %collective-permute-start.20) | collective-permute-done | bytes 262176 | tf_op jit(solution)/shard_map/ppermute | solution.py:180
  60.9 0.1 add_convert_fusion.4
  61.0 0.8 collective-permute-start.25
  61.8 2.1 %collective-permute-start.21 = (bf16[64,2048]{1,0:T(8,128)(2,1)S(1)}, bf16[64,2048]{1,0:T(8,128)(2,1)S(1)}, u32[]{:S(2)}, u32[]{:S(2)}) collective-permute-start(bf16[64,2048]{1,0:T(8,128)(2,1)S(1)} %add_convert_fusion.4), channel_id=1, source_target_pairs={{0,8},{1,9},{2,10},{3,11},{4,12},{5,13},{6,14},{7,15},{8,0},{9,1},... | collective-permute-start | bytes 786440 | tf_op jit(solution)/shard_map/ppermute | solution.py:184
  63.9 2.6 %collective-permute-done.22 = bf16[64,2048]{1,0:T(8,128)(2,1)S(1)} collective-permute-done((bf16[64,2048]{1,0:T(8,128)(2,1)S(1)}, bf16[64,2048]{1,0:T(8,128)(2,1)S(1)}, u32[]{:S(2)}, u32[]{:S(2)}) %collective-permute-start.22) | collective-permute-done | bytes 262176 | tf_op jit(solution)/shard_map/ppermute | solution.py:180
  66.6 0.1 add_convert_fusion.3
  66.7 0.1 collective-permute-start.23
  66.7 0.0 collective-permute-done.19
  66.7 4.2 %collective-permute-done.25 = bf16[64,2048]{1,0:T(8,128)(2,1)S(1)} collective-permute-done((bf16[64,2048]{1,0:T(8,128)(2,1)S(1)}, bf16[64,2048]{1,0:T(8,128)(2,1)S(1)}, u32[]{:S(2)}, u32[]{:S(2)}) %collective-permute-start.25) | collective-permute-done | bytes 262176 | tf_op jit(solution)/shard_map/ppermute | solution.py:180
  70.9 8.5 %collective-permute-done.21 = bf16[64,2048]{1,0:T(8,128)(2,1)S(1)} collective-permute-done((bf16[64,2048]{1,0:T(8,128)(2,1)S(1)}, bf16[64,2048]{1,0:T(8,128)(2,1)S(1)}, u32[]{:S(2)}, u32[]{:S(2)}) %collective-permute-start.21) | collective-permute-done | bytes 262176 | tf_op jit(solution)/shard_map/ppermute | solution.py:184
  79.4 0.9 %add_convert_fusion = bf16[64,2048]{1,0:T(8,128)(2,1)} fusion(bf16[64,2048]{1,0:T(8,128)(2,1)S(1)} %collective-permute-done.23, bf16[64,2048]{1,0:T(8,128)(2,1)S(1)} %collective-permute-done.21, bf16[64,2048]{1,0:T(8,128)(2,1)S(1)} %collective-permute-done.19, bf16[64,2048]{1,0:T(8,128)(2,1)S(1)} %collective-permute-done.25, ...), kind=kLoop, calls=%fused_computation | loop fusion | flops 1835008 | bytes 1835008 | tf_op jit(solution)/shard_map/convert_element_type | solution.py:229
  (4 shorter events, 0.0 us)
Async XLA Ops:
  1.7 12.8 %collective-permute-start = (bf16[64,2176]{1,0:T(8,128)(2,1)}, bf16[64,2176]{1,0:T(8,128)(2,1)S(1)}, u32[]{:S(2)}, u32[]{:S(2)}) collective-permute-start(bf16[64,2176]{1,0:T(8,128)(2,1)} %shard_map.64.refs_1_), channel_id=1, source_target_pairs={{0,4},{1,5},{2,6},{3,7},{4,8},{5,9},{6,10},{7,11},{8,12},{9,13},{1... | collective-permute-start | bytes 835592 | tf_op jit(solution)/shard_map/ppermute | solution.py:184
  4.8 9.8 %collective-permute-start.1 = (bf16[64,2176]{1,0:T(8,128)(2,1)}, bf16[64,2176]{1,0:T(8,128)(2,1)S(1)}, u32[]{:S(2)}, u32[]{:S(2)}) collective-permute-start(bf16[64,2176]{1,0:T(8,128)(2,1)} %shard_map.64.refs_1_), channel_id=1, source_target_pairs={{0,2},{1,3},{2,0},{3,1},{4,6},{5,7},{6,4},{7,5},{8,10},{9,11},{10,... | collective-permute-start | bytes 835592 | tf_op jit(solution)/shard_map/ppermute | solution.py:180
  6.3 14.2 %collective-permute-start.3 = (bf16[64,2176]{1,0:T(8,128)(2,1)}, bf16[64,2176]{1,0:T(8,128)(2,1)S(1)}, u32[]{:S(2)}, u32[]{:S(2)}) collective-permute-start(bf16[64,2176]{1,0:T(8,128)(2,1)} %shard_map.64.refs_1_), channel_id=1, source_target_pairs={{0,12},{1,13},{2,14},{3,15},{4,0},{5,1},{6,2},{7,3},{8,4},{9,5},{1... | collective-permute-start | bytes 835592 | tf_op jit(solution)/shard_map/ppermute | solution.py:184
  14.5 7.0 %collective-permute-start.2 = (bf16[64,2176]{1,0:T(8,128)(2,1)S(1)}, bf16[64,2176]{1,0:T(8,128)(2,1)S(1)}, u32[]{:S(2)}, u32[]{:S(2)}) collective-permute-start(bf16[64,2176]{1,0:T(8,128)(2,1)S(1)} %collective-permute-done.refs_1_), channel_id=1, source_target_pairs={{0,2},{1,3},{2,0},{3,1},{4,6},{5,7},{6,4},{7,5},{8,10},{9,11},{10,... | collective-permute-start | bytes 835592 | tf_op jit(solution)/shard_map/ppermute | solution.py:180
  16.3 10.1 %collective-permute-start.6 = (bf16[64,2176]{1,0:T(8,128)(2,1)S(1)}, bf16[64,2176]{1,0:T(8,128)(2,1)S(1)}, u32[]{:S(2)}, u32[]{:S(2)}) collective-permute-start(bf16[64,2176]{1,0:T(8,128)(2,1)S(1)} %collective-permute-done.refs_1_), channel_id=1, source_target_pairs={{0,4},{1,5},{2,6},{3,7},{4,8},{5,9},{6,10},{7,11},{8,12},{9,13},{1... | collective-permute-start | bytes 835592 | tf_op jit(solution)/shard_map/ppermute | solution.py:184
  16.3 13.9 %collective-permute-start.5 = (bf16[64,2176]{1,0:T(8,128)(2,1)S(1)}, bf16[64,2176]{1,0:T(8,128)(2,1)S(1)}, u32[]{:S(2)}, u32[]{:S(2)}) collective-permute-start(bf16[64,2176]{1,0:T(8,128)(2,1)S(1)} %collective-permute-done.refs_1_), channel_id=1, source_target_pairs={{0,1},{1,0},{2,3},{3,2},{4,5},{5,4},{6,7},{7,6},{8,9},{9,8},{10,11... | collective-permute-start | bytes 835592 | tf_op jit(solution)/shard_map/ppermute | solution.py:177
  21.5 8.7 %collective-permute-start.4 = (bf16[64,2176]{1,0:T(8,128)(2,1)S(1)}, bf16[64,2176]{1,0:T(8,128)(2,1)S(1)}, u32[]{:S(2)}, u32[]{:S(2)}) collective-permute-start(bf16[64,2176]{1,0:T(8,128)(2,1)S(1)} %collective-permute-done.2.refs_0_), channel_id=1, source_target_pairs={{0,1},{1,0},{2,3},{3,2},{4,5},{5,4},{6,7},{7,6},{8,9},{9,8},{10,11... | collective-permute-start | bytes 835592 | tf_op jit(solution)/shard_map/ppermute | solution.py:177
  21.6 12.0 %collective-permute-start.10 = (bf16[64,2176]{1,0:T(8,128)(2,1)S(1)}, bf16[64,2176]{1,0:T(8,128)(2,1)S(1)}, u32[]{:S(2)}, u32[]{:S(2)}) collective-permute-start(bf16[64,2176]{1,0:T(8,128)(2,1)S(1)} %collective-permute-done.3.refs_1_), channel_id=1, source_target_pairs={{0,2},{1,3},{2,0},{3,1},{4,6},{5,7},{6,4},{7,5},{8,10},{9,11},{10,... | collective-permute-start | bytes 835592 | tf_op jit(solution)/shard_map/ppermute | solution.py:180
  22.8 11.1 %collective-permute-start.12 = (bf16[64,2176]{1,0:T(8,128)(2,1)}, bf16[64,2176]{1,0:T(8,128)(2,1)S(1)}, u32[]{:S(2)}, u32[]{:S(2)}) collective-permute-start(bf16[64,2176]{1,0:T(8,128)(2,1)} %shard_map.64.refs_1_), channel_id=1, source_target_pairs={{0,1},{1,0},{2,3},{3,2},{4,5},{5,4},{6,7},{7,6},{8,9},{9,8},{10,11... | collective-permute-start | bytes 835592 | tf_op jit(solution)/shard_map/ppermute | solution.py:177
  30.2 5.0 %copy-start = (bf16[64,2176]{1,0:T(8,128)(2,1)S(1)}, bf16[64,2176]{1,0:T(8,128)(2,1)}, u32[]{:S(2)}) copy-start(bf16[64,2176]{1,0:T(8,128)(2,1)} %shard_map.64.refs_1_) | copy-start | bytes 835588
  32.9 9.7 %collective-permute-start.7 = (bf16[128,2048]{1,0:T(8,128)(2,1)S(1)}, bf16[128,2048]{1,0:T(8,128)(2,1)S(1)}, u32[]{:S(2)}, u32[]{:S(2)}) collective-permute-start(bf16[128,2048]{1,0:T(8,128)(2,1)S(1)} %get-tuple-element.40), channel_id=1, source_target_pairs={{0,1},{1,0},{2,3},{3,2},{4,5},{5,4},{6,7},{7,6},{8,9},{9,8},{10,11... | collective-permute-start | bytes 1572872 | tf_op jit(solution)/shard_map/ppermute | solution.py:177
  33.0 2.3 %collective-permute-start.11 = (bf16[64,2176]{1,0:T(8,128)(2,1)S(1)}, bf16[64,2176]{1,0:T(8,128)(2,1)S(1)}, u32[]{:S(2)}, u32[]{:S(2)}) collective-permute-start(bf16[64,2176]{1,0:T(8,128)(2,1)S(1)} %collective-permute-done.1.refs_0_), channel_id=1, source_target_pairs={{0,1},{1,0},{2,3},{3,2},{4,5},{5,4},{6,7},{7,6},{8,9},{9,8},{10,11... | collective-permute-start | bytes 835592 | tf_op jit(solution)/shard_map/ppermute | solution.py:177
  33.5 4.6 %collective-permute-start.14 = (bf16[64,2176]{1,0:T(8,128)(2,1)S(1)}, bf16[64,2176]{1,0:T(8,128)(2,1)S(1)}, u32[]{:S(2)}, u32[]{:S(2)}) collective-permute-start(bf16[64,2176]{1,0:T(8,128)(2,1)S(1)} %collective-permute-done.3.refs_1_), channel_id=1, source_target_pairs={{0,1},{1,0},{2,3},{3,2},{4,5},{5,4},{6,7},{7,6},{8,9},{9,8},{10,11... | collective-permute-start | bytes 835592 | tf_op jit(solution)/shard_map/ppermute | solution.py:177
  33.5 4.9 %collective-permute-start.13 = (bf16[64,2176]{1,0:T(8,128)(2,1)S(1)}, bf16[64,2176]{1,0:T(8,128)(2,1)S(1)}, u32[]{:S(2)}, u32[]{:S(2)}) collective-permute-start(bf16[64,2176]{1,0:T(8,128)(2,1)S(1)} %collective-permute-done.10.refs_0_), channel_id=1, source_target_pairs={{0,1},{1,0},{2,3},{3,2},{4,5},{5,4},{6,7},{7,6},{8,9},{9,8},{10,11... | collective-permute-start | bytes 835592 | tf_op jit(solution)/shard_map/ppermute | solution.py:177
  34.0 8.6 %collective-permute-start.9 = (bf16[64,2176]{1,0:T(8,128)(2,1)S(1)}, bf16[64,2176]{1,0:T(8,128)(2,1)S(1)}, u32[]{:S(2)}, u32[]{:S(2)}) collective-permute-start(bf16[64,2176]{1,0:T(8,128)(2,1)S(1)} %collective-permute-done.6.refs_1_), channel_id=1, source_target_pairs={{0,2},{1,3},{2,0},{3,1},{4,6},{5,7},{6,4},{7,5},{8,10},{9,11},{10,... | collective-permute-start | bytes 835592 | tf_op jit(solution)/shard_map/ppermute | solution.py:180
  37.9 9.1 %collective-permute-start.24 = (bf16[128,2048]{1,0:T(8,128)(2,1)S(1)}, bf16[128,2048]{1,0:T(8,128)(2,1)S(1)}, u32[]{:S(2)}, u32[]{:S(2)}) collective-permute-start(bf16[128,2048]{1,0:T(8,128)(2,1)S(1)} %get-tuple-element.45), channel_id=1, source_target_pairs={{0,1},{1,0},{2,3},{3,2},{4,5},{5,4},{6,7},{7,6},{8,9},{9,8},{10,11... | collective-permute-start | bytes 1572872 | tf_op jit(solution)/shard_map/ppermute | solution.py:177
  38.1 5.4 %collective-permute-start.16 = (bf16[64,2176]{1,0:T(8,128)(2,1)S(1)}, bf16[64,2176]{1,0:T(8,128)(2,1)S(1)}, u32[]{:S(2)}, u32[]{:S(2)}) collective-permute-start(bf16[64,2176]{1,0:T(8,128)(2,1)S(1)} %collective-permute-done.6.refs_1_), channel_id=1, source_target_pairs={{0,1},{1,0},{2,3},{3,2},{4,5},{5,4},{6,7},{7,6},{8,9},{9,8},{10,11... | collective-permute-start | bytes 835592 | tf_op jit(solution)/shard_map/ppermute | solution.py:177
  42.6 1.6 %collective-permute-start.15 = (bf16[64,2176]{1,0:T(8,128)(2,1)S(1)}, bf16[64,2176]{1,0:T(8,128)(2,1)S(1)}, u32[]{:S(2)}, u32[]{:S(2)}) collective-permute-start(bf16[64,2176]{1,0:T(8,128)(2,1)S(1)} %collective-permute-done.9.refs_0_), channel_id=1, source_target_pairs={{0,1},{1,0},{2,3},{3,2},{4,5},{5,4},{6,7},{7,6},{8,9},{9,8},{10,11... | collective-permute-start | bytes 835592 | tf_op jit(solution)/shard_map/ppermute | solution.py:177
  42.7 8.8 %collective-permute-start.8 = (bf16[64,2048]{1,0:T(8,128)(2,1)S(1)}, bf16[64,2048]{1,0:T(8,128)(2,1)S(1)}, u32[]{:S(2)}, u32[]{:S(2)}) collective-permute-start(bf16[64,2048]{1,0:T(8,128)(2,1)S(1)} %add_convert_fusion.8), channel_id=1, source_target_pairs={{0,2},{1,3},{2,0},{3,1},{4,6},{5,7},{6,4},{7,5},{8,10},{9,11},{10,... | collective-permute-start | bytes 786440 | tf_op jit(solution)/shard_map/ppermute | solution.py:180
  46.8 4.8 %collective-permute-start.17 = (bf16[128,2048]{1,0:T(8,128)(2,1)S(1)}, bf16[128,2048]{1,0:T(8,128)(2,1)S(1)}, u32[]{:S(2)}, u32[]{:S(2)}) collective-permute-start(bf16[128,2048]{1,0:T(8,128)(2,1)S(1)} %get-tuple-element.51), channel_id=1, source_target_pairs={{0,1},{1,0},{2,3},{3,2},{4,5},{5,4},{6,7},{7,6},{8,9},{9,8},{10,11... | collective-permute-start | bytes 1572872 | tf_op jit(solution)/shard_map/ppermute | solution.py:177
  47.1 5.4 %collective-permute-start.18 = (bf16[128,2048]{1,0:T(8,128)(2,1)S(1)}, bf16[128,2048]{1,0:T(8,128)(2,1)S(1)}, u32[]{:S(2)}, u32[]{:S(2)}) collective-permute-start(bf16[128,2048]{1,0:T(8,128)(2,1)S(1)} %get-tuple-element.48), channel_id=1, source_target_pairs={{0,1},{1,0},{2,3},{3,2},{4,5},{5,4},{6,7},{7,6},{8,9},{9,8},{10,11... | collective-permute-start | bytes 1572872 | tf_op jit(solution)/shard_map/ppermute | solution.py:177
  51.7 9.3 %collective-permute-start.20 = (bf16[64,2048]{1,0:T(8,128)(2,1)S(1)}, bf16[64,2048]{1,0:T(8,128)(2,1)S(1)}, u32[]{:S(2)}, u32[]{:S(2)}) collective-permute-start(bf16[64,2048]{1,0:T(8,128)(2,1)S(1)} %add_convert_fusion.6), channel_id=1, source_target_pairs={{0,2},{1,3},{2,0},{3,1},{4,6},{5,7},{6,4},{7,5},{8,10},{9,11},{10,... | collective-permute-start | bytes 786440 | tf_op jit(solution)/shard_map/ppermute | solution.py:180
  52.5 14.2 %collective-permute-start.19 = (bf16[64,2048]{1,0:T(8,128)(2,1)S(1)}, bf16[64,2048]{1,0:T(8,128)(2,1)S(1)}, u32[]{:S(2)}, u32[]{:S(2)}) collective-permute-start(bf16[64,2048]{1,0:T(8,128)(2,1)S(1)} %add_convert_fusion.7), channel_id=1, source_target_pairs={{0,12},{1,13},{2,14},{3,15},{4,0},{5,1},{6,2},{7,3},{8,4},{9,5},{1... | collective-permute-start | bytes 786440 | tf_op jit(solution)/shard_map/ppermute | solution.py:184
  55.8 10.7 %collective-permute-start.22 = (bf16[64,2048]{1,0:T(8,128)(2,1)S(1)}, bf16[64,2048]{1,0:T(8,128)(2,1)S(1)}, u32[]{:S(2)}, u32[]{:S(2)}) collective-permute-start(bf16[64,2048]{1,0:T(8,128)(2,1)S(1)} %add_convert_fusion.5), channel_id=1, source_target_pairs={{0,2},{1,3},{2,0},{3,1},{4,6},{5,7},{6,4},{7,5},{8,10},{9,11},{10,... | collective-permute-start | bytes 786440 | tf_op jit(solution)/shard_map/ppermute | solution.py:180
  61.0 9.9 %collective-permute-start.25 = (bf16[64,2048]{1,0:T(8,128)(2,1)S(1)}, bf16[64,2048]{1,0:T(8,128)(2,1)S(1)}, u32[]{:S(2)}, u32[]{:S(2)}) collective-permute-start(bf16[64,2048]{1,0:T(8,128)(2,1)S(1)} %add_convert_fusion.2), channel_id=1, source_target_pairs={{0,2},{1,3},{2,0},{3,1},{4,6},{5,7},{6,4},{7,5},{8,10},{9,11},{10,... | collective-permute-start | bytes 786440 | tf_op jit(solution)/shard_map/ppermute | solution.py:180
  61.8 17.6 %collective-permute-start.21 = (bf16[64,2048]{1,0:T(8,128)(2,1)S(1)}, bf16[64,2048]{1,0:T(8,128)(2,1)S(1)}, u32[]{:S(2)}, u32[]{:S(2)}) collective-permute-start(bf16[64,2048]{1,0:T(8,128)(2,1)S(1)} %add_convert_fusion.4), channel_id=1, source_target_pairs={{0,8},{1,9},{2,10},{3,11},{4,12},{5,13},{6,14},{7,15},{8,0},{9,1},... | collective-permute-start | bytes 786440 | tf_op jit(solution)/shard_map/ppermute | solution.py:184
  66.7 12.8 %collective-permute-start.23 = (bf16[64,2048]{1,0:T(8,128)(2,1)S(1)}, bf16[64,2048]{1,0:T(8,128)(2,1)S(1)}, u32[]{:S(2)}, u32[]{:S(2)}) collective-permute-start(bf16[64,2048]{1,0:T(8,128)(2,1)S(1)} %add_convert_fusion.3), channel_id=1, source_target_pairs={{0,4},{1,5},{2,6},{3,7},{4,8},{5,9},{6,10},{7,11},{8,12},{9,13},{1... | collective-permute-start | bytes 786440 | tf_op jit(solution)/shard_map/ppermute | solution.py:184
